TPU v7x, 32 devices: a whole 2x2x4 slice. The times are simulated.
32 devices in a mesh: parts: 1, ep: 16 (over z, y, x), fan: 2 (over core).
Axes of the slice: x: 2, y: 2, z: 4, core: 2. Of those that a mesh axis runs over, the one named last changes fastest.
Arguments:
- queries: bfloat16 [1024, 2, 8192], P(('parts', 'ep', 'fan')), may hold values from -300 to 300
- new_kv: bfloat16 [1024, 2, 1024], P(('parts', 'ep', 'fan')), may hold values from -6 to 6
- prompt_kv: bfloat16 [64, 1024, 1024], P(('parts', 'ep', 'fan')), may hold values from -6 to 6
- prompt_lens: int32 [64], P(('parts', 'ep')), may hold values from 1 to 1024, 40960 in all
- sample_prompt: int32 [1024], P(('parts', 'ep', 'fan')), may hold values from 0 to 3, as said below
- hidden: bfloat16 [1024, 4096], P(('parts', 'ep', 'fan')), may hold values from -6 to 6
- norm_gain: bfloat16 [4096], replicated, may hold values from 0.099609375 to 1.8984375
- route_ids: int32 [1024, 8], P(('parts', 'ep', 'fan')), may hold values from 0 to 15, all different within a row; in each aligned block of 32 rows (0 to 31, 32 to 63, ...) at most 32 rows name the same one
- route_logits: float32 [1024, 8], P(('parts', 'ep', 'fan')), may hold values from -8 to 8
- w_gate: bfloat16 [16, 4096, 1536], P('ep', None, 'fan'), may hold values from -0.09375 to 0.09375
- w_up: bfloat16 [16, 4096, 1536], P('ep', None, 'fan'), may hold values from -0.09375 to 0.09375
- w_down: bfloat16 [16, 1536, 4096], P('ep', 'fan'), may hold values from -0.15625 to 0.15625
Outputs:
- context: bfloat16 [1024, 2, 8192], P(('parts', 'ep', 'fan'))
- expert_out: bfloat16 [1024, 4096], P(('parts', 'ep', 'fan'))
Inputs may be any that keep to these rules, and one draw needn't show every extreme that they name: `sample_prompt`: each sample names one of the 4 prompts held by the devices of its chip, numbered by device then position; each of them has exactly 16 samples on that chip. `prompt_lens`: some prompt has exactly 1024. `route_ids`: each token names 8 different experts; among the tokens of one device no expert is named more than 32 times.
All inputs are finite; a program needn't handle non-finite values. No bound on the sum of `prompt_lens` on one device may be relied on, other than what follows from the above.
Results may differ from a plain program's by a relative error of at most 0.0071.
Values may be sent and summed in bfloat16 or wider, within the bound.
No kernel may reach another device: no remote copies, remote signals or barrier semaphores. Data moves between devices by JAX's collectives and lax.ppermute only.
A program may use at most 256 MiB of HBM per device.

v0:
```python
import functools

import jax
import jax.numpy as jnp
from jax import lax
from jax.experimental import pallas as pl
from jax.experimental.pallas import tpu as pltpu
from jax.sharding import PartitionSpec as P

KVH = 4
HD = 128
STEPS = 2
SAMP = 16
TOP = 8
GROUP = SAMP * STEPS
LANES = 128
BAND = 64
WIDE = 256
DEEP = 1024
EXPERT_VMEM = 12
ATTEND_VMEM = 16
LOG2E = 1.4426950408889634
MIB = 1 << 20


def dot(a, b, contract=((1,), (0,))):
    return lax.dot_general(a, b, (contract, ((), ())), preferred_element_type=jnp.float32)


SMALL = pl.CostEstimate(flops=1 << 20, bytes_accessed=1 << 14, transcendentals=0)


def norm_kernel(hidden_ref, gain_ref, ids_ref, logits_ref, out_ref):
    rows, width = hidden_ref.shape
    hidden = hidden_ref[...].astype(jnp.float32)
    meansq = jnp.mean(hidden * hidden, axis=-1, keepdims=True)
    gain = gain_ref[...].astype(jnp.float32).reshape(1, width)
    out_ref[:, :width] = (hidden * lax.rsqrt(meansq + 1e-06) * gain).astype(jnp.bfloat16)
    logits = logits_ref[...]
    raised = jnp.exp(logits - jnp.max(logits, axis=0, keepdims=True))
    weights = raised / jnp.sum(raised, axis=0, keepdims=True)
    ids = ids_ref[...]
    number = lax.broadcasted_iota(jnp.int32, (LANES, rows), 0)
    total = jnp.zeros((LANES, rows), jnp.float32)
    for choice in range(TOP):
        picked = (number % 16) == ids[choice : choice + 1, :]
        total = total + jnp.where(picked, weights[choice : choice + 1, :], 0.0)
    high = total.astype(jnp.bfloat16).astype(jnp.float32)
    middle = (total - high).astype(jnp.bfloat16).astype(jnp.float32)
    low = total - high - middle
    piece = number // 16
    parts = jnp.where(
        piece == 0, high, jnp.where(piece == 1, middle, jnp.where(piece == 2, low, 0.0))
    ).astype(jnp.bfloat16)
    first = lax.broadcasted_iota(jnp.int32, (LANES, LANES), 0)
    second = lax.broadcasted_iota(jnp.int32, (LANES, LANES), 1)
    identity = jnp.where(first == second, 1.0, 0.0).astype(jnp.bfloat16)
    out_ref[:, width:] = dot(parts, identity, ((0,), (0,))).astype(jnp.bfloat16)


def norm_message(hidden, gain, ids, logits):
    rows, width = hidden.shape
    return pl.pallas_call(
        norm_kernel,
        out_shape=jax.ShapeDtypeStruct((rows, width + LANES), jnp.bfloat16),
        cost_estimate=SMALL,
        name="norm_message",
    )(hidden, gain, ids.T, logits.T)


def rank_rows(match, rows):
    first = lax.broadcasted_iota(jnp.int32, (rows, rows), 0)
    second = lax.broadcasted_iota(jnp.int32, (rows, rows), 1)
    below = jnp.where(second < first, 1.0, 0.0).astype(jnp.bfloat16)
    return dot(below, match)


def attend_kernel(local, heads, lens_ref, q_mine, q_other, o_mine, o_other, cache, *refs):
    out_ref, keys, values, q_ref, score_ref, weight_ref, total_ref, k_sem, v_sem = refs[-9:]
    copies = []
    for i, head in enumerate(heads):
        at = pl.ds(head * HD, HD)
        copies.append(pltpu.make_async_copy(cache.at[local, :, at], keys.at[i], k_sem.at[i]))
        at = pl.ds((KVH + head) * HD, HD)
        copies.append(pltpu.make_async_copy(cache.at[local, :, at], values.at[i], v_sem.at[i]))
    for copy in copies:
        copy.start()
    number = lax.axis_index("fan") * 2 + local
    length = lens_ref[number]
    span = keys.shape[1]
    head_width = q_mine.shape[1] // KVH
    group = head_width // HD
    marks = 2 * KVH * HD
    prompts = jnp.concatenate([o_mine[:, marks:], o_other[:, marks:]], axis=0).astype(jnp.float32)
    chosen = prompts == number.astype(jnp.float32)
    rank = rank_rows(jnp.where(chosen, 1.0, 0.0).astype(jnp.bfloat16), LANES)
    lane = lax.broadcasted_iota(jnp.int32, (LANES, LANES), 1)
    here = chosen & (rank == lane.astype(jnp.float32))
    select = jnp.where(here, 1.0, 0.0).astype(jnp.bfloat16)

    def pick(mine, other, first, amount, rows):
        at = slice(first, first + amount)
        both = jnp.concatenate([mine[:, at], other[:, at]], axis=0)
        return dot(select[:, :rows], both, ((0,), (0,))).astype(jnp.bfloat16)

    factor = HD**-0.5 * LOG2E
    usable = lax.broadcasted_iota(jnp.int32, (1, span), 1) < length
    row = lax.broadcasted_iota(jnp.int32, (LANES, LANES), 0) % GROUP
    causal = ((row // STEPS == lane // STEPS) & (lane <= row))[:BAND]
    bands = group * GROUP // WIDE
    items = [(i, band) for i in range(len(heads)) for band in range(bands)]
    own = {}

    def products(step):
        i, band = items[step]
        head, slot = heads[i], step % 2
        if band == 0:
            queries = pick(q_mine, q_other, head * head_width, head_width, GROUP)
            for j in range(group):
                q_ref[i, j * GROUP : (j + 1) * GROUP] = queries[:, j * HD : (j + 1) * HD]
            own[i] = (
                pick(o_mine, o_other, head * HD, HD, LANES),
                pick(o_mine, o_other, (KVH + head) * HD, HD, LANES),
            )
            copies[2 * i].wait()
        queries = q_ref[i, band * WIDE : (band + 1) * WIDE]
        score_ref[slot, :, :span] = dot(queries, keys[i], ((1,), (1,)))
        score_ref[slot, :, span:] = dot(queries, own[i][0], ((1,), (1,)))

    products(0)
    for step, (i, band) in enumerate(items):
        slot = step % 2
        if step + 1 < len(items):
            products(step + 1)
        for base in range(0, WIDE, BAND):
            at = slice(base, base + BAND)
            scores = jnp.where(usable, score_ref[slot, at, :span], -1e30)
            mine = jnp.where(causal, score_ref[slot, at, span:], -1e30)
            highest = jnp.maximum(
                jnp.max(scores, axis=-1, keepdims=True), jnp.max(mine, axis=-1, keepdims=True)
            )
            raised = jnp.exp2((scores - highest) * factor)
            own_raised = jnp.exp2((mine - highest) * factor)
            total = jnp.sum(raised, axis=-1, keepdims=True) + jnp.sum(
                own_raised, axis=-1, keepdims=True
            )
            weight_ref[slot, at, :span] = raised.astype(jnp.bfloat16)
            weight_ref[slot, at, span:] = own_raised.astype(jnp.bfloat16)
            total_ref[slot, at] = jnp.broadcast_to(1.0 / total, (BAND, HD))
        if band == 0:
            copies[2 * i + 1].wait()
        mixed = dot(weight_ref[slot, :, :span], values[i])
        mixed = mixed + dot(weight_ref[slot, :, span:], own[i][1])
        mixed = (mixed * total_ref[slot]).astype(jnp.bfloat16)
        for j in range(WIDE // GROUP):
            first = i * head_width + (band * (WIDE // GROUP) + j) * HD
            out_ref[:, first : first + HD] = mixed[j * GROUP : (j + 1) * GROUP]


def attend(local, heads, lens, queries, own, cache, *after):
    rows, q_width = queries[0].shape
    span = cache.shape[1]
    head = q_width // KVH
    band = head // HD * GROUP
    some = len(heads)
    whole = pl.BlockSpec(memory_space=pltpu.VMEM)
    return pl.pallas_call(
        functools.partial(attend_kernel, local, heads),
        out_shape=jax.ShapeDtypeStruct((GROUP, some * head), jnp.bfloat16),
        in_specs=[pl.BlockSpec(memory_space=pltpu.SMEM)]
        + [whole] * 4
        + [pl.BlockSpec(memory_space=pltpu.HBM)]
        + [pl.BlockSpec(memory_space=pl.ANY)] * len(after),
        out_specs=whole,
        scratch_shapes=[
            pltpu.VMEM((some, span, HD), jnp.bfloat16),
            pltpu.VMEM((some, span, HD), jnp.bfloat16),
            pltpu.VMEM((some, band, HD), jnp.bfloat16),
            pltpu.VMEM((2, WIDE, span + LANES), jnp.float32),
            pltpu.VMEM((2, WIDE, span + LANES), jnp.bfloat16),
            pltpu.VMEM((2, WIDE, HD), jnp.float32),
            pltpu.SemaphoreType.DMA((some,)),
            pltpu.SemaphoreType.DMA((some,)),
        ],
        compiler_params=pltpu.CompilerParams(vmem_limit_bytes=ATTEND_VMEM * MIB),
        cost_estimate=SMALL,
        name="attend",
    )(lens, *queries, *own, cache, *after)


def place_kernel(halves, o_mine, *refs):
    out_ref = refs[-1]
    rows = o_mine.shape[0]
    lane = lax.broadcasted_iota(jnp.int32, (rows, LANES), 1)
    part = lane // GROUP
    side, local = part // 2, part % 2
    fan = lax.axis_index("fan")
    number = jnp.where(side == 0, fan, 1 - fan) * 2 + local
    prompts = o_mine[:, 2 * KVH * HD :].astype(jnp.float32)
    chosen = prompts == number.astype(jnp.float32)
    match = jnp.where(chosen, 1.0, 0.0).astype(jnp.bfloat16)
    rank = rank_rows(match, rows)
    ahead = GROUP - dot(jnp.ones((rows, rows), jnp.bfloat16), match)
    rank = rank + jnp.where(side == 1, ahead, 0.0)
    here = chosen & (rank == (lane % GROUP).astype(jnp.float32))
    place = jnp.where(here, 1.0, 0.0).astype(jnp.bfloat16)
    width = refs[0].shape[1]
    for half in range(halves):
        stacked = jnp.concatenate([ref[...] for ref in refs[4 * half : 4 * half + 4]], axis=0)
        result = dot(place, stacked).astype(jnp.bfloat16)
        at = slice(half * width, (half + 1) * width)
        out_ref[:, :, at] = result.reshape(rows // STEPS, STEPS, width)


def place_context(own, contexts, out_shape):
    whole = pl.BlockSpec(memory_space=pltpu.VMEM)
    return pl.pallas_call(
        functools.partial(place_kernel, len(contexts) // 4),
        out_shape=out_shape,
        in_specs=[whole] * (1 + len(contexts)),
        out_specs=whole,
        compiler_params=pltpu.CompilerParams(vmem_limit_bytes=12 * MIB),
        cost_estimate=SMALL,
        name="place_context",
    )(own, *contexts)


def expert_kernel(count, at_row, tokens, *refs):
    xs, (gate, up, down) = refs[:count], refs[count : count + 3]
    keep, send, other = refs[-8:-5]
    x, opened, raised, units, x_sem = refs[-5:]
    width, hidden = gate.shape
    copies = []
    for i in range(count):
        copies.append(
            pltpu.make_async_copy(
                xs[i].at[pl.ds(at_row, tokens)], x.at[pl.ds(i * tokens, tokens)], x_sem.at[i]
            )
        )
    for copy in copies:
        copy.start()
    for copy in copies:
        copy.wait()
    for i in range(width // DEEP):
        at = slice(i * DEEP, (i + 1) * DEEP)
        product = dot(x[:, at], gate[at])
        opened[...] = product if i == 0 else opened[...] + product
        product = dot(x[:, at], up[at])
        raised[...] = product if i == 0 else raised[...] + product
    through = opened[...]
    units[...] = (through * jax.nn.sigmoid(through) * raised[...]).astype(jnp.bfloat16)
    marks = x[:, width:].astype(jnp.float32)
    lane = lax.broadcasted_iota(jnp.int32, marks.shape, 1)
    mine = (lane % 16 == lax.axis_index("ep")) & (lane < 48)
    weight = jnp.sum(jnp.where(mine, marks, 0.0), axis=1, keepdims=True)
    half = count // 2 * tokens
    for i in range(width // DEEP):
        at = slice(i * DEEP, (i + 1) * DEEP)
        result = (dot(units[...], down[:, at]) * weight).astype(jnp.bfloat16)
        keep[:, at] = result[: half // 2]
        send[:, at] = result[half // 2 : half]
        other[:, at] = result[half:]


def expert_chunk(pieces, at_row, tokens, gate, up, down, *after):
    count = len(pieces)
    message = pieces[0].shape[1]
    width, hidden = gate.shape
    rows = count * tokens
    whole = pl.BlockSpec(memory_space=pltpu.VMEM)
    return pl.pallas_call(
        functools.partial(expert_kernel, count, at_row, tokens),
        out_shape=(
            jax.ShapeDtypeStruct((rows // 4, width), jnp.bfloat16),
            jax.ShapeDtypeStruct((rows // 4, width), jnp.bfloat16),
            jax.ShapeDtypeStruct((rows // 2, width), jnp.bfloat16),
        ),
        in_specs=[pl.BlockSpec(memory_space=pl.ANY)] * count
        + [whole] * 3
        + [pl.BlockSpec(memory_space=pl.ANY)] * len(after),
        out_specs=(whole, whole, whole),
        scratch_shapes=[
            pltpu.VMEM((rows, message), jnp.bfloat16),
            pltpu.VMEM((rows, hidden), jnp.float32),
            pltpu.VMEM((rows, hidden), jnp.float32),
            pltpu.VMEM((rows, hidden), jnp.bfloat16),
            pltpu.SemaphoreType.DMA((count,)),
        ],
        compiler_params=pltpu.CompilerParams(vmem_limit_bytes=EXPERT_VMEM * MIB),
        cost_estimate=SMALL,
        name="expert_chunk",
    )(*pieces, gate, up, down, *after)


def on_device(
    queries,
    new_kv,
    prompt_kv,
    prompt_lens,
    sample_prompt,
    hidden,
    norm_gain,
    route_ids,
    route_logits,
    w_gate,
    w_up,
    w_down,
):
    chips = lax.axis_size("ep")
    count, _, q_width = queries.shape
    rows = count * STEPS

    def swap(value, by_fan):
        pairs = [
            ((e * 2 + f), ((e ^ by_fan[f]) * 2 + f)) for e in range(chips) for f in range(2)
        ]
        return lax.ppermute(value, ("ep", "fan"), pairs)

    def near(value):
        return swap(value, (1, 2))

    def cross(value):
        return swap(value, (2, 1))

    def far(value, layer):
        return swap(value, (4 * layer, 4 * layer))

    def beside(value):
        return lax.ppermute(value, "fan", [(0, 1), (1, 0)])

    gate, up, down = w_gate[0], w_up[0], w_down[0]
    tokens = hidden.shape[0]
    sync = lax.optimization_barrier
    token = norm_message(hidden, norm_gain, route_ids, route_logits)
    token, queries, new_kv = sync((token, queries, new_kv))
    marks = jnp.broadcast_to(sample_prompt.astype(jnp.bfloat16)[:, None, None], (count, STEPS, LANES))
    q_mine = queries.reshape(rows, q_width)
    own_mine = jnp.concatenate([new_kv, marks], axis=2).reshape(rows, -1)
    q_both = (q_mine, beside(q_mine))
    own_both = (own_mine, beside(own_mine))

    def attend_half(local, half, *after):
        heads = tuple(range(half * KVH // 2, (half + 1) * KVH // 2))
        return attend(local, heads, prompt_lens, q_both, own_both, prompt_kv, *after)

    def expert(pieces, at_row, *after):
        return expert_chunk(pieces, at_row, tokens, gate, up, down, *after)

    def with_fan(pieces):
        return pieces + [beside(piece) for piece in pieces]

    def sum_cores(result, back):
        send = result[1]
        half = send.shape[0]
        return (send.astype(jnp.float32) + back[half:].astype(jnp.float32)).astype(jnp.bfloat16)

    def sum_cross(result, back, turned):
        single = tokens

        def total(at):
            mine = result[0][at].astype(jnp.float32) + back[at].astype(jnp.float32)
            return mine + turned[at].astype(jnp.float32)

        return total(slice(0, single)), total(slice(single, 2 * single)).astype(jnp.bfloat16)

    def widen(value):
        return value.astype(jnp.float32)

    def narrow(value):
        return value.astype(jnp.bfloat16)

    level_2, level_1 = far(token, 2), far(token, 1)
    first_0, cross_0 = near(token), cross(token)
    pair = jnp.concatenate([level_2, level_1], axis=0)
    level_3 = far(level_2, 1)
    third_0 = cross(first_0)
    context_0a = attend_half(0, 0, pair, first_0, cross_0)
    context_0a, third_0 = sync((context_0a, third_0))
    pieces_0 = with_fan([token, first_0, cross_0, third_0])
    context_0b = attend_half(0, 1, context_0a)
    context_0b, level_3, first_p, cross_p, *pieces_0 = sync(
        (context_0b, level_3, near(pair), cross(pair), *pieces_0)
    )
    third_p = cross(first_p)
    first_3, cross_3 = near(level_3), cross(level_3)
    result_0 = expert(pieces_0, 0, context_0b, first_p)

    third_p, first_3, cross_3, result_0 = sync((third_p, first_3, cross_3, result_0))
    back_0 = beside(result_0[2])
    pieces_p = with_fan([pair, first_p, cross_p, third_p])
    third_3 = cross(first_3)
    context_1a = attend_half(1, 0, third_p, first_3)
    context_1a, back_0, third_3, *pieces_p = sync((context_1a, back_0, third_3, *pieces_p))
    there_0 = sum_cores(result_0, back_0)
    pieces_3 = with_fan([level_3, first_3, cross_3, third_3])
    result_2 = expert(pieces_p, 0, context_1a, there_0)

    turned_0, result_2, *pieces_3 = sync((cross(there_0), result_2, *pieces_3))
    back_2 = beside(result_2[2])
    held_0, passed_0 = sum_cross(result_0, back_0, turned_0)
    there_2 = sum_cores(result_2, back_2)
    result_3 = expert(pieces_3, 0, there_2, passed_0)

    ended_0, turned_2, result_3 = sync((near(passed_0), cross(there_2), result_3))
    back_3 = beside(result_3[2])
    held_2, passed_2 = sum_cross(result_2, back_2, turned_2)
    context_1b = attend_half(1, 1, passed_2)
    context_1b, back_3 = sync((context_1b, back_3))
    there_3 = sum_cores(result_3, back_3)
    result_1 = expert(pieces_p, tokens, there_3, passed_2)

    contexts = [context_0a, context_0b, context_1a, context_1b]
    sent = [beside(value) for value in contexts]
    ended_2, turned_3, result_1, sent = sync((near(passed_2), cross(there_3), result_1, sent))
    back_1 = beside(result_1[2])
    held_3, passed_3 = sum_cross(result_3, back_3, turned_3)
    ordered = [contexts[0], contexts[2], sent[0], sent[2], contexts[1], contexts[3], sent[1], sent[3]]
    far_2 = far(narrow(held_2 + widen(ended_2)), 2)
    there_1 = sum_cores(result_1, back_1)
    own_late, _ = sync((own_mine, there_1))
    context = place_context(own_late, ordered, jax.ShapeDtypeStruct(queries.shape, jnp.bfloat16))
    context, ended_3 = sync((context, near(passed_3)))
    far_3 = far(narrow(held_3 + widen(ended_3)), 3)
    held_1, passed_1 = sum_cross(result_1, back_1, cross(there_1))
    far_1 = far(narrow(held_1 + widen(near(passed_1))), 1)
    total = held_0 + widen(ended_0) + widen(far_1)
    expert_out = narrow(total + widen(far_2) + widen(far_3))
    return (context, expert_out)


def solution(mesh):
    placed = (
        P(("parts", "ep", "fan"), None, None),
        P(("parts", "ep", "fan"), None, None),
        P(("parts", "ep", "fan"), None, None),
        P(("parts", "ep")),
        P(("parts", "ep", "fan")),
        P(("parts", "ep", "fan"), None),
        P(),
        P(("parts", "ep", "fan"), None),
        P(("parts", "ep", "fan"), None),
        P("ep", None, "fan"),
        P("ep", None, "fan"),
        P("ep", "fan", None),
    )
    return jax.shard_map(
        on_device,
        mesh=mesh,
        in_specs=placed,
        out_specs=(P(("parts", "ep", "fan"), None, None), P(("parts", "ep", "fan"), None)),
        check_vma=False,
    )
```

profile of v0, /device:TPU:0, one launch (start us, length us, event | category | flops | bytes accessed | tf_op | source)
XLA Modules:
  0.0 137.7 jit_solution(12548211880044966858)
XLA Ops:
  0.6 1.9 %norm_message.1.refs_0_ = bf16[32,4224]{1,0:T(8,128)(2,1)} custom-call(bf16[32,4096]{1,0:T(8,128)(2,1)} %hidden_ref.1, bf16[4096]{0:T(1024)(128)(2,1)} %gain_ref.1, s32[8,32]{1,0:T(8,128)} %bitcast.21, f32[8,32]{1,0:T(8,128)} %bitcast.22), custom_call_target="tpu_custom_call" | custom-call | flops 1048576 | bytes 16384 | tf_op jit(solution)/shard_map/norm_message/pallas_call | solution.py:63
  2.6 4.0 %collective-permute-start.2 = (bf16[32,4224]{1,0:T(8,128)(2,1)}, bf16[32,4224]{1,0:T(8,128)(2,1)}, u32[]{:S(2)}, u32[]{:S(2)}) collective-permute-start(bf16[32,4224]{1,0:T(8,128)(2,1)} %norm_message.1.refs_0_), channel_id=1, source_target_pairs={{0,16},{1,17},{2,18},{3,19},{4,20},{5,21},{6,22},{7,23},{8,24},{9,... | collective-permute-start | bytes 811016 | tf_op jit(solution)/shard_map/ppermute | solution.py:317
  6.6 1.6 %collective-permute-start.3 = (bf16[32,4224]{1,0:T(8,128)(2,1)}, bf16[32,4224]{1,0:T(8,128)(2,1)}, u32[]{:S(2)}, u32[]{:S(2)}) collective-permute-start(bf16[32,4224]{1,0:T(8,128)(2,1)} %norm_message.1.refs_0_), channel_id=1, source_target_pairs={{0,8},{1,9},{2,10},{3,11},{4,12},{5,13},{6,14},{7,15},{8,0},{9,1},... | collective-permute-start | bytes 811016 | tf_op jit(solution)/shard_map/ppermute | solution.py:317
  8.2 1.5 %collective-permute-start.4 = (bf16[32,4224]{1,0:T(8,128)(2,1)}, bf16[32,4224]{1,0:T(8,128)(2,1)}, u32[]{:S(2)}, u32[]{:S(2)}) collective-permute-start(bf16[32,4224]{1,0:T(8,128)(2,1)} %norm_message.1.refs_0_), channel_id=1, source_target_pairs={{0,2},{1,5},{2,0},{3,7},{4,6},{5,1},{6,4},{7,3},{8,10},{9,13},{10,... | collective-permute-start | bytes 811016 | tf_op jit(solution)/shard_map/ppermute | solution.py:317
  9.7 1.5 %collective-permute-start.5 = (bf16[32,4224]{1,0:T(8,128)(2,1)}, bf16[32,4224]{1,0:T(8,128)(2,1)}, u32[]{:S(2)}, u32[]{:S(2)}) collective-permute-start(bf16[32,4224]{1,0:T(8,128)(2,1)} %norm_message.1.refs_0_), channel_id=1, source_target_pairs={{0,4},{1,3},{2,6},{3,1},{4,0},{5,7},{6,2},{7,5},{8,12},{9,11},{10,... | collective-permute-start | bytes 811016 | tf_op jit(solution)/shard_map/ppermute | solution.py:317
  11.2 0.7 convert_element_type.156
  11.9 1.0 pad_maximum_fusion
  13.1 1.6 %reshape.12.q_mine = bf16[64,8192]{1,0:T(8,128)(2,1)S(1)} reshape(bf16[32,2,8192]{2,1,0:T(2,128)(2,1)} %param.12) | data formatting | bytes 2097152 | tf_op jit(solution)/shard_map/reshape | solution.py:337
  14.7 4.6 %collective-permute-done.2 = bf16[32,4224]{1,0:T(8,128)(2,1)} collective-permute-done((bf16[32,4224]{1,0:T(8,128)(2,1)}, bf16[32,4224]{1,0:T(8,128)(2,1)}, u32[]{:S(2)}, u32[]{:S(2)}) %collective-permute-start.2) | collective-permute-done | bytes 270368 | tf_op jit(solution)/shard_map/ppermute | solution.py:317
  19.3 1.0 constant_dynamic-update-slice_fusion.1
  20.3 0.6 collective-permute-start.1
  20.9 1.6 %collective-permute-start.6 = (bf16[32,4224]{1,0:T(8,128)(2,1)}, bf16[32,4224]{1,0:T(8,128)(2,1)S(1)}, u32[]{:S(2)}, u32[]{:S(2)}) collective-permute-start(bf16[32,4224]{1,0:T(8,128)(2,1)} %collective-permute-done.4.refs_1_), channel_id=1, source_target_pairs={{0,4},{1,3},{2,6},{3,1},{4,0},{5,7},{6,2},{7,5},{8,12},{9,11},{10,... | collective-permute-start | bytes 811016 | tf_op jit(solution)/shard_map/ppermute | solution.py:317
  22.4 1.1 constant_dynamic-update-slice_fusion.refs_0_
  23.6 1.6 %collective-permute-start.8 = (bf16[64,4224]{1,0:T(8,128)(2,1)S(1)}, bf16[64,4224]{1,0:T(8,128)(2,1)S(1)}, u32[]{:S(2)}, u32[]{:S(2)}) collective-permute-start(bf16[64,4224]{1,0:T(8,128)(2,1)S(1)} %constant_dynamic-update-slice_fusion.refs_0_), channel_id=1, source_target_pairs={{0,2},{1,5},{2,0},{3,7},{4,6},{5,1},{6,4},{7,3},{8,10},{9,13},{10,... | collective-permute-start | bytes 1622024 | tf_op jit(solution)/shard_map/ppermute | solution.py:317
  25.2 0.6 collective-permute-start.9
  25.7 2.2 %copy-done.1 = bf16[2,1024,1024]{2,1,0:T(8,128)(2,1)S(1)} copy-done((bf16[2,1024,1024]{2,1,0:T(8,128)(2,1)S(1)}, bf16[2,1024,1024]{2,1,0:T(8,128)(2,1)}, u32[]{:S(2)}) %copy-start.1) | copy-done | bytes 4194328
  27.9 0.7 copy-done.3
  28.6 3.8 %attend.4.refs_0_ = bf16[32,4096]{1,0:T(8,128)(2,1)S(1)} custom-call(s32[4]{0:T(128)S(1)} %copy-done.3, bf16[64,8192]{1,0:T(8,128)(2,1)S(1)} %reshape.12.q_mine, bf16[64,8192]{1,0:T(8,128)(2,1)S(1)} %collective-permute-done.q_other, bf16[64,1152]{1,0:T(8,128)(2,1)S(1)} %reshape.11.o_mine, bf16[64,1152]{1,0:T(8,128)(2,1)S(1)} %collective-permute-done.1.o_other, ...), custom_call_target="tpu_custom_call" | custom-call | flops 1048576 | bytes 16384 | tf_op jit(solution)/shard_map/attend/pallas_call | solution.py:167
  32.7 0.6 collective-permute-start.7
  33.3 3.8 %attend.5.refs_11_.refs_4_ = bf16[32,4096]{1,0:T(8,128)(2,1)S(1)} custom-call(s32[4]{0:T(128)S(1)} %copy-done.3, bf16[64,8192]{1,0:T(8,128)(2,1)S(1)} %reshape.12.q_mine, bf16[64,8192]{1,0:T(8,128)(2,1)S(1)} %collective-permute-done.q_other, bf16[64,1152]{1,0:T(8,128)(2,1)S(1)} %reshape.11.o_mine, bf16[64,1152]{1,0:T(8,128)(2,1)S(1)} %collective-permute-done.1.o_other, ...), custom_call_target="tpu_custom_call" | custom-call | flops 1048576 | bytes 16384 | tf_op jit(solution)/shard_map/attend/pallas_call | solution.py:167
  37.1 4.5 %collective-permute-done.7.refs_0_ = bf16[32,4224]{1,0:T(8,128)(2,1)S(1)} collective-permute-done((bf16[32,4224]{1,0:T(8,128)(2,1)}, bf16[32,4224]{1,0:T(8,128)(2,1)S(1)}, u32[]{:S(2)}, u32[]{:S(2)}) %collective-permute-start.7) | collective-permute-done | bytes 270368 | tf_op jit(solution)/shard_map/ppermute | solution.py:317
  41.6 1.6 %collective-permute-start.14 = (bf16[64,4224]{1,0:T(8,128)(2,1)S(1)}, bf16[64,4224]{1,0:T(8,128)(2,1)S(1)}, u32[]{:S(2)}, u32[]{:S(2)}) collective-permute-start(bf16[64,4224]{1,0:T(8,128)(2,1)S(1)} %collective-permute-done.8.refs_12_.refs_1_), channel_id=1, source_target_pairs={{0,4},{1,3},{2,6},{3,1},{4,0},{5,7},{6,2},{7,5},{8,12},{9,11},{10,... | collective-permute-start | bytes 1622024 | tf_op jit(solution)/shard_map/ppermute | solution.py:317
  43.2 0.5 collective-permute-start.15
  43.7 1.2 collective-permute-start.16
  45.0 2.8 %copy-done = bf16[1,768,4096]{2,1,0:T(8,128)(2,1)S(1)} copy-done((bf16[1,768,4096]{2,1,0:T(8,128)(2,1)S(1)}, bf16[1,768,4096]{2,1,0:T(8,128)(2,1)}, u32[]{:S(2)}) %copy-start) | copy-done | bytes 6291480
  47.8 6.3 %expert_chunk.4 = (bf16[64,4096]{1,0:T(8,128)(2,1)S(1)}, bf16[64,4096]{1,0:T(8,128)(2,1)S(1)}, bf16[128,4096]{1,0:T(8,128)(2,1)S(1)}) custom-call(bf16[32,4224]{1,0:T(8,128)(2,1)S(1)} %copy-done.2, bf16[32,4224]{1,0:T(8,128)(2,1)} %collective-permute-done.4.refs_1_, bf16[32,4224]{1,0:T(8,128)(2,1)} %collective-permute-done.5.refs_2_, ...), custom_call_target="tpu_custom_call" | custom-call | flops 1048576 | bytes 16384 | tf_op jit(solution)/shard_map/expert_chunk/pallas_call | solution.py:271
  54.0 2.0 %collective-permute-done.16.refs_2_ = bf16[32,4224]{1,0:T(8,128)(2,1)S(1)} collective-permute-done((bf16[32,4224]{1,0:T(8,128)(2,1)S(1)}, bf16[32,4224]{1,0:T(8,128)(2,1)S(1)}, u32[]{:S(2)}, u32[]{:S(2)}) %collective-permute-start.16) | collective-permute-done | bytes 270368 | tf_op jit(solution)/shard_map/ppermute | solution.py:317
  56.1 0.5 collective-permute-start.19
  57.1 2.4 %collective-permute-done.19.refs_4_ = bf16[64,4224]{1,0:T(8,128)(2,1)S(1)} collective-permute-done((bf16[64,4224]{1,0:T(8,128)(2,1)S(1)}, bf16[64,4224]{1,0:T(8,128)(2,1)S(1)}, u32[]{:S(2)}, u32[]{:S(2)}) %collective-permute-start.19) | collective-permute-done | bytes 540704 | tf_op jit(solution)/shard_map/ppermute | solution.py:329
  59.5 1.1 collective-permute-start.18
  60.6 3.8 %attend.6.refs_11_.refs_1_ = bf16[32,4096]{1,0:T(8,128)(2,1)S(1)} custom-call(s32[4]{0:T(128)S(1)} %copy-done.3, bf16[64,8192]{1,0:T(8,128)(2,1)S(1)} %reshape.12.q_mine, bf16[64,8192]{1,0:T(8,128)(2,1)S(1)} %collective-permute-done.q_other, bf16[64,1152]{1,0:T(8,128)(2,1)S(1)} %reshape.11.o_mine, bf16[64,1152]{1,0:T(8,128)(2,1)S(1)} %collective-permute-done.1.o_other, ...), custom_call_target="tpu_custom_call" | custom-call | flops 1048576 | bytes 16384 | tf_op jit(solution)/shard_map/attend/pallas_call | solution.py:167
  64.4 1.5 %collective-permute-done.18.refs_3_ = bf16[32,4224]{1,0:T(8,128)(2,1)S(1)} collective-permute-done((bf16[32,4224]{1,0:T(8,128)(2,1)S(1)}, bf16[32,4224]{1,0:T(8,128)(2,1)S(1)}, u32[]{:S(2)}, u32[]{:S(2)}) %collective-permute-start.18) | collective-permute-done | bytes 270368 | tf_op jit(solution)/shard_map/ppermute | solution.py:317
  66.1 1.2 collective-permute-start.23
  67.3 0.5 collective-permute-start.25
  67.8 0.5 collective-permute-start.27
  68.3 5.3 %expert_chunk.5 = (bf16[64,4096]{1,0:T(8,128)(2,1)S(1)}, bf16[64,4096]{1,0:T(8,128)(2,1)S(1)}, bf16[128,4096]{1,0:T(8,128)(2,1)S(1)}) custom-call(bf16[64,4224]{1,0:T(8,128)(2,1)S(1)} %constant_dynamic-update-slice_fusion.refs_0_, bf16[64,4224]{1,0:T(8,128)(2,1)S(1)} %collective-permute-done.8.refs_12_.refs_1_, ...), custom_call_target="tpu_custom_call" | custom-call | flops 1048576 | bytes 16384 | tf_op jit(solution)/shard_map/expert_chunk/pallas_call | solution.py:271
  73.7 1.6 %collective-permute-done.23 = bf16[64,4096]{1,0:T(8,128)(2,1)S(1)} collective-permute-done((bf16[64,4096]{1,0:T(8,128)(2,1)S(1)}, bf16[64,4096]{1,0:T(8,128)(2,1)S(1)}, u32[]{:S(2)}, u32[]{:S(2)}) %collective-permute-start.23) | collective-permute-done | bytes 524320 | tf_op jit(solution)/shard_map/ppermute | solution.py:317
  75.4 2.7 %collective-permute-done.28 = bf16[128,4096]{1,0:T(8,128)(2,1)S(1)} collective-permute-done((bf16[128,4096]{1,0:T(8,128)(2,1)S(1)}, bf16[128,4096]{1,0:T(8,128)(2,1)S(1)}, u32[]{:S(2)}, u32[]{:S(2)}) %collective-permute-start.28) | collective-permute-done | bytes 1048608 | tf_op jit(solution)/shard_map/ppermute | solution.py:329
  78.1 1.2 collective-permute-start.30
  79.4 1.7 %collective-permute-start.29 = (bf16[32,4096]{1,0:T(8,128)(2,1)S(1)}, bf16[32,4096]{1,0:T(8,128)(2,1)S(1)}, u32[]{:S(2)}, u32[]{:S(2)}) collective-permute-start(bf16[32,4096]{1,0:T(8,128)(2,1)S(1)} %add_convert_fusion.11.refs_12_), channel_id=1, source_target_pairs={{0,2},{1,5},{2,0},{3,7},{4,6},{5,1},{6,4},{7,3},{8,10},{9,13},{10,... | collective-permute-start | bytes 786440 | tf_op jit(solution)/shard_map/ppermute | solution.py:317
  81.1 5.6 %expert_chunk.6 = (bf16[64,4096]{1,0:T(8,128)(2,1)S(1)}, bf16[64,4096]{1,0:T(8,128)(2,1)S(1)}, bf16[128,4096]{1,0:T(8,128)(2,1)S(1)}) custom-call(bf16[32,4224]{1,0:T(8,128)(2,1)S(1)} %collective-permute-done.7.refs_0_, bf16[32,4224]{1,0:T(8,128)(2,1)S(1)} %collective-permute-done.15.refs_1_, bf16[32,4224]{1,0:T(8,128)(2,1)S(1)} %collective-permute-done.16.refs_2_, ...), custom_call_target="tpu_custom_call" | custom-call | flops 1048576 | bytes 16384 | tf_op jit(solution)/shard_map/expert_chunk/pallas_call | solution.py:271
  86.7 2.1 %collective-permute-done.29 = bf16[32,4096]{1,0:T(8,128)(2,1)S(1)} collective-permute-done((bf16[32,4096]{1,0:T(8,128)(2,1)S(1)}, bf16[32,4096]{1,0:T(8,128)(2,1)S(1)}, u32[]{:S(2)}, u32[]{:S(2)}) %collective-permute-start.29) | collective-permute-done | bytes 262176 | tf_op jit(solution)/shard_map/ppermute | solution.py:317
  88.7 1.5 %collective-permute-done.30 = bf16[64,4096]{1,0:T(8,128)(2,1)S(1)} collective-permute-done((bf16[64,4096]{1,0:T(8,128)(2,1)S(1)}, bf16[64,4096]{1,0:T(8,128)(2,1)S(1)}, u32[]{:S(2)}, u32[]{:S(2)}) %collective-permute-start.30) | collective-permute-done | bytes 524320 | tf_op jit(solution)/shard_map/ppermute | solution.py:317
  90.2 0.5 collective-permute-start.34
  90.8 3.8 %attend.7.refs_5_ = bf16[32,4096]{1,0:T(8,128)(2,1)S(1)} custom-call(s32[4]{0:T(128)S(1)} %copy-done.3, bf16[64,8192]{1,0:T(8,128)(2,1)S(1)} %reshape.12.q_mine, bf16[64,8192]{1,0:T(8,128)(2,1)S(1)} %collective-permute-done.q_other, bf16[64,1152]{1,0:T(8,128)(2,1)S(1)} %reshape.11.o_mine, bf16[64,1152]{1,0:T(8,128)(2,1)S(1)} %collective-permute-done.1.o_other, ...), custom_call_target="tpu_custom_call" | custom-call | flops 1048576 | bytes 16384 | tf_op jit(solution)/shard_map/attend/pallas_call | solution.py:167
  94.8 1.2 collective-permute-start.33
  96.0 0.5 collective-permute-start.36
  96.5 1.1 collective-permute-start.31
  97.6 5.6 %expert_chunk.7 = (bf16[64,4096]{1,0:T(8,128)(2,1)S(1)}, bf16[64,4096]{1,0:T(8,128)(2,1)S(1)}, bf16[128,4096]{1,0:T(8,128)(2,1)S(1)}) custom-call(bf16[64,4224]{1,0:T(8,128)(2,1)S(1)} %constant_dynamic-update-slice_fusion.refs_0_, bf16[64,4224]{1,0:T(8,128)(2,1)S(1)} %collective-permute-done.8.refs_12_.refs_1_, ...), custom_call_target="tpu_custom_call" | custom-call | flops 1048576 | bytes 16384 | tf_op jit(solution)/shard_map/expert_chunk/pallas_call | solution.py:271
  103.2 2.5 %collective-permute-done.31 = bf16[32,4096]{1,0:T(8,128)(2,1)S(1)} collective-permute-done((bf16[32,4096]{1,0:T(8,128)(2,1)S(1)}, bf16[32,4096]{1,0:T(8,128)(2,1)S(1)}, u32[]{:S(2)}, u32[]{:S(2)}) %collective-permute-start.31) | collective-permute-done | bytes 262176 | tf_op jit(solution)/shard_map/ppermute | solution.py:317
  105.7 1.1 collective-permute-done.33
  106.9 1.1 collective-permute-start.39
  108.1 1.4 %collective-permute-done.38 = bf16[128,4096]{1,0:T(8,128)(2,1)S(1)} collective-permute-done((bf16[128,4096]{1,0:T(8,128)(2,1)S(1)}, bf16[128,4096]{1,0:T(8,128)(2,1)S(1)}, u32[]{:S(2)}, u32[]{:S(2)}) %collective-permute-start.38) | collective-permute-done | bytes 1048608 | tf_op jit(solution)/shard_map/ppermute | solution.py:329
  109.6 1.2 collective-permute-start.40
  110.9 2.5 %collective-permute-start.43 = (bf16[32,4096]{1,0:T(8,128)(2,1)S(1)}, bf16[32,4096]{1,0:T(8,128)(2,1)S(1)}, u32[]{:S(2)}, u32[]{:S(2)}) collective-permute-start(bf16[32,4096]{1,0:T(8,128)(2,1)S(1)} %add_convert_fusion.6), channel_id=1, source_target_pairs={{0,16},{1,17},{2,18},{3,19},{4,20},{5,21},{6,22},{7,23},{8,24},{9,... | collective-permute-start | bytes 786440 | tf_op jit(solution)/shard_map/ppermute | solution.py:317
  113.5 1.6 %place_context.1 = bf16[32,2,8192]{2,1,0:T(2,128)(2,1)} custom-call(bf16[64,1152]{1,0:T(8,128)(2,1)S(1)} %reshape.11.o_mine, bf16[32,4096]{1,0:T(8,128)(2,1)S(1)} %attend.4.refs_0_, bf16[32,4096]{1,0:T(8,128)(2,1)S(1)} %attend.6.refs_11_.refs_1_, bf16[32,4096]{1,0:T(8,128)(2,1)S(1)} %collective-permute-done.34.refs_2_, ...), custom_call_target="tpu_custom_call" | custom-call | flops 1048576 | bytes 16384 | tf_op jit(solution)/shard_map/place_context/pallas_call | solution.py:217
  115.1 3.8 %collective-permute-done.40 = bf16[64,4096]{1,0:T(8,128)(2,1)S(1)} collective-permute-done((bf16[64,4096]{1,0:T(8,128)(2,1)S(1)}, bf16[64,4096]{1,0:T(8,128)(2,1)S(1)}, u32[]{:S(2)}, u32[]{:S(2)}) %collective-permute-start.40) | collective-permute-done | bytes 524320 | tf_op jit(solution)/shard_map/ppermute | solution.py:317
  119.0 1.1 collective-permute-start.41
  120.2 3.5 %collective-permute-start.44 = (bf16[32,4096]{1,0:T(8,128)(2,1)S(1)}, bf16[32,4096]{1,0:T(8,128)(2,1)S(1)}, u32[]{:S(2)}, u32[]{:S(2)}) collective-permute-start(bf16[32,4096]{1,0:T(8,128)(2,1)S(1)} %add_convert_fusion.5), channel_id=1, source_target_pairs={{0,24},{1,25},{2,26},{3,27},{4,28},{5,29},{6,30},{7,31},{8,16},{9,... | collective-permute-start | bytes 786440 | tf_op jit(solution)/shard_map/ppermute | solution.py:317
  123.7 1.7 %collective-permute-done.41 = bf16[32,4096]{1,0:T(8,128)(2,1)S(1)} collective-permute-done((bf16[32,4096]{1,0:T(8,128)(2,1)S(1)}, bf16[32,4096]{1,0:T(8,128)(2,1)S(1)}, u32[]{:S(2)}, u32[]{:S(2)}) %collective-permute-start.41) | collective-permute-done | bytes 262176 | tf_op jit(solution)/shard_map/ppermute | solution.py:317
  125.5 0.6 collective-permute-start.42
  126.2 5.9 %collective-permute-done.43 = bf16[32,4096]{1,0:T(8,128)(2,1)S(1)} collective-permute-done((bf16[32,4096]{1,0:T(8,128)(2,1)S(1)}, bf16[32,4096]{1,0:T(8,128)(2,1)S(1)}, u32[]{:S(2)}, u32[]{:S(2)}) %collective-permute-start.43) | collective-permute-done | bytes 262176 | tf_op jit(solution)/shard_map/ppermute | solution.py:317
  132.1 4.7 %collective-permute-done.42 = bf16[32,4096]{1,0:T(8,128)(2,1)S(1)} collective-permute-done((bf16[32,4096]{1,0:T(8,128)(2,1)S(1)}, bf16[32,4096]{1,0:T(8,128)(2,1)S(1)}, u32[]{:S(2)}, u32[]{:S(2)}) %collective-permute-start.42) | collective-permute-done | bytes 262176 | tf_op jit(solution)/shard_map/ppermute | solution.py:317
  136.8 1.0 add_convert_fusion.4
  (73 shorter events, 2.4 us)
Async XLA Ops:
  2.6 16.7 %collective-permute-start.2 = (bf16[32,4224]{1,0:T(8,128)(2,1)}, bf16[32,4224]{1,0:T(8,128)(2,1)}, u32[]{:S(2)}, u32[]{:S(2)}) collective-permute-start(bf16[32,4224]{1,0:T(8,128)(2,1)} %norm_message.1.refs_0_), channel_id=1, source_target_pairs={{0,16},{1,17},{2,18},{3,19},{4,20},{5,21},{6,22},{7,23},{8,24},{9,... | collective-permute-start | bytes 811016 | tf_op jit(solution)/shard_map/ppermute | solution.py:317
  6.6 13.7 %collective-permute-start.3 = (bf16[32,4224]{1,0:T(8,128)(2,1)}, bf16[32,4224]{1,0:T(8,128)(2,1)}, u32[]{:S(2)}, u32[]{:S(2)}) collective-permute-start(bf16[32,4224]{1,0:T(8,128)(2,1)} %norm_message.1.refs_0_), channel_id=1, source_target_pairs={{0,8},{1,9},{2,10},{3,11},{4,12},{5,13},{6,14},{7,15},{8,0},{9,1},... | collective-permute-start | bytes 811016 | tf_op jit(solution)/shard_map/ppermute | solution.py:317
  8.2 12.7 %collective-permute-start.4 = (bf16[32,4224]{1,0:T(8,128)(2,1)}, bf16[32,4224]{1,0:T(8,128)(2,1)}, u32[]{:S(2)}, u32[]{:S(2)}) collective-permute-start(bf16[32,4224]{1,0:T(8,128)(2,1)} %norm_message.1.refs_0_), channel_id=1, source_target_pairs={{0,2},{1,5},{2,0},{3,7},{4,6},{5,1},{6,4},{7,3},{8,10},{9,13},{10,... | collective-permute-start | bytes 811016 | tf_op jit(solution)/shard_map/ppermute | solution.py:317
  9.7 15.5 %collective-permute-start.5 = (bf16[32,4224]{1,0:T(8,128)(2,1)}, bf16[32,4224]{1,0:T(8,128)(2,1)}, u32[]{:S(2)}, u32[]{:S(2)}) collective-permute-start(bf16[32,4224]{1,0:T(8,128)(2,1)} %norm_message.1.refs_0_), channel_id=1, source_target_pairs={{0,4},{1,3},{2,6},{3,1},{4,0},{5,7},{6,2},{7,5},{8,12},{9,11},{10,... | collective-permute-start | bytes 811016 | tf_op jit(solution)/shard_map/ppermute | solution.py:317
  11.2 21.5 %collective-permute-start.10 = (bf16[32,4224]{1,0:T(8,128)(2,1)}, bf16[32,4224]{1,0:T(8,128)(2,1)}, u32[]{:S(2)}, u32[]{:S(2)}) collective-permute-start(bf16[32,4224]{1,0:T(8,128)(2,1)} %norm_message.1.refs_0_), channel_id=1, source_target_pairs={{0,1},{1,0},{2,3},{3,2},{4,5},{5,4},{6,7},{7,6},{8,9},{9,8},{10,11... | collective-permute-start | bytes 811016 | tf_op jit(solution)/shard_map/ppermute | solution.py:329
  13.1 31.9 %slice-start.2 = ((s8[6291456]{0:T(1024)(128)(4,1)}), s8[2097152]{0:T(1024)(128)(4,1)S(1)}, s32[]{:S(2)}) async-start(s8[6291456]{0:T(1024)(128)(4,1)} %bitcast.11), calls=%async_computation.2 | async-start | bytes 4194304
  19.3 5.9 %collective-permute-start = (bf16[64,8192]{1,0:T(8,128)(2,1)S(1)}, bf16[64,8192]{1,0:T(8,128)(2,1)S(1)}, u32[]{:S(2)}, u32[]{:S(2)}) collective-permute-start(bf16[64,8192]{1,0:T(8,128)(2,1)S(1)} %reshape.12.q_mine), channel_id=1, source_target_pairs={{0,1},{1,0},{2,3},{3,2},{4,5},{5,4},{6,7},{7,6},{8,9},{9,8},{10,11... | collective-permute-start | bytes 3145736 | tf_op jit(solution)/shard_map/ppermute | solution.py:329
  20.3 3.3 %collective-permute-start.1 = (bf16[64,1152]{1,0:T(8,128)(2,1)S(1)}, bf16[64,1152]{1,0:T(8,128)(2,1)S(1)}, u32[]{:S(2)}, u32[]{:S(2)}) collective-permute-start(bf16[64,1152]{1,0:T(8,128)(2,1)S(1)} %reshape.11.o_mine), channel_id=1, source_target_pairs={{0,1},{1,0},{2,3},{3,2},{4,5},{5,4},{6,7},{7,6},{8,9},{9,8},{10,11... | collective-permute-start | bytes 442376 | tf_op jit(solution)/shard_map/ppermute | solution.py:329
  20.9 11.5 %collective-permute-start.6 = (bf16[32,4224]{1,0:T(8,128)(2,1)}, bf16[32,4224]{1,0:T(8,128)(2,1)S(1)}, u32[]{:S(2)}, u32[]{:S(2)}) collective-permute-start(bf16[32,4224]{1,0:T(8,128)(2,1)} %collective-permute-done.4.refs_1_), channel_id=1, source_target_pairs={{0,4},{1,3},{2,6},{3,1},{4,0},{5,7},{6,2},{7,5},{8,12},{9,11},{10,... | collective-permute-start | bytes 811016 | tf_op jit(solution)/shard_map/ppermute | solution.py:317
  22.4 22.5 %slice-start = ((s8[6291456]{0:T(1024)(128)(4,1)}), s8[4194304]{0:T(1024)(128)(4,1)S(1)}, s32[]{:S(2)}) async-start(s8[6291456]{0:T(1024)(128)(4,1)} %bitcast.5), calls=%async_computation | async-start | bytes 8388608
  23.6 21.4 %slice-start.1 = ((s8[6291456]{0:T(1024)(128)(4,1)}), s8[2097152]{0:T(1024)(128)(4,1)S(1)}, s32[]{:S(2)}) async-start(s8[6291456]{0:T(1024)(128)(4,1)} %bitcast.5), calls=%async_computation.1 | async-start | bytes 4194304
  23.6 21.4 %slice-start.3 = ((s8[6291456]{0:T(1024)(128)(4,1)}), s8[4194304]{0:T(1024)(128)(4,1)S(1)}, s32[]{:S(2)}) async-start(s8[6291456]{0:T(1024)(128)(4,1)} %bitcast.11), calls=%async_computation.3 | async-start | bytes 8388608
  23.6 18.0 %collective-permute-start.8 = (bf16[64,4224]{1,0:T(8,128)(2,1)S(1)}, bf16[64,4224]{1,0:T(8,128)(2,1)S(1)}, u32[]{:S(2)}, u32[]{:S(2)}) collective-permute-start(bf16[64,4224]{1,0:T(8,128)(2,1)S(1)} %constant_dynamic-update-slice_fusion.refs_0_), channel_id=1, source_target_pairs={{0,2},{1,5},{2,0},{3,7},{4,6},{5,1},{6,4},{7,3},{8,10},{9,13},{10,... | collective-permute-start | bytes 1622024 | tf_op jit(solution)/shard_map/ppermute | solution.py:317
  25.1 8.1 %collective-permute-start.11 = (bf16[32,4224]{1,0:T(8,128)(2,1)}, bf16[32,4224]{1,0:T(8,128)(2,1)S(1)}, u32[]{:S(2)}, u32[]{:S(2)}) collective-permute-start(bf16[32,4224]{1,0:T(8,128)(2,1)} %collective-permute-done.4.refs_1_), channel_id=1, source_target_pairs={{0,1},{1,0},{2,3},{3,2},{4,5},{5,4},{6,7},{7,6},{8,9},{9,8},{10,11... | collective-permute-start | bytes 811016 | tf_op jit(solution)/shard_map/ppermute | solution.py:329
  25.2 16.4 %collective-permute-start.9 = (bf16[64,4224]{1,0:T(8,128)(2,1)S(1)}, bf16[64,4224]{1,0:T(8,128)(2,1)S(1)}, u32[]{:S(2)}, u32[]{:S(2)}) collective-permute-start(bf16[64,4224]{1,0:T(8,128)(2,1)S(1)} %constant_dynamic-update-slice_fusion.refs_0_), channel_id=1, source_target_pairs={{0,4},{1,3},{2,6},{3,1},{4,0},{5,7},{6,2},{7,5},{8,12},{9,11},{10,... | collective-permute-start | bytes 1622024 | tf_op jit(solution)/shard_map/ppermute | solution.py:317
  25.7 2.2 %copy-start.1 = (bf16[2,1024,1024]{2,1,0:T(8,128)(2,1)S(1)}, bf16[2,1024,1024]{2,1,0:T(8,128)(2,1)}, u32[]{:S(2)}) copy-start(bf16[2,1024,1024]{2,1,0:T(8,128)(2,1)} %cache.7) | copy-start | bytes 12582916
  27.9 0.7 copy-start.3
  28.6 16.4 %copy-start.2 = (bf16[32,4224]{1,0:T(8,128)(2,1)S(1)}, bf16[32,4224]{1,0:T(8,128)(2,1)}, u32[]{:S(2)}) copy-start(bf16[32,4224]{1,0:T(8,128)(2,1)} %norm_message.1.refs_0_) | copy-start | bytes 811012
  32.4 4.7 %collective-permute-start.12 = (bf16[32,4224]{1,0:T(8,128)(2,1)}, bf16[32,4224]{1,0:T(8,128)(2,1)S(1)}, u32[]{:S(2)}, u32[]{:S(2)}) collective-permute-start(bf16[32,4224]{1,0:T(8,128)(2,1)} %collective-permute-done.5.refs_2_), channel_id=1, source_target_pairs={{0,1},{1,0},{2,3},{3,2},{4,5},{5,4},{6,7},{7,6},{8,9},{9,8},{10,11... | collective-permute-start | bytes 811016 | tf_op jit(solution)/shard_map/ppermute | solution.py:329
  32.7 8.9 %collective-permute-start.7 = (bf16[32,4224]{1,0:T(8,128)(2,1)}, bf16[32,4224]{1,0:T(8,128)(2,1)S(1)}, u32[]{:S(2)}, u32[]{:S(2)}) collective-permute-start(bf16[32,4224]{1,0:T(8,128)(2,1)} %collective-permute-done.2), channel_id=1, source_target_pairs={{0,8},{1,9},{2,10},{3,11},{4,12},{5,13},{6,14},{7,15},{8,0},{9,1},... | collective-permute-start | bytes 811016 | tf_op jit(solution)/shard_map/ppermute | solution.py:317
  33.2 8.4 %collective-permute-start.13 = (bf16[32,4224]{1,0:T(8,128)(2,1)S(1)}, bf16[32,4224]{1,0:T(8,128)(2,1)S(1)}, u32[]{:S(2)}, u32[]{:S(2)}) collective-permute-start(bf16[32,4224]{1,0:T(8,128)(2,1)S(1)} %collective-permute-done.6.refs_3_), channel_id=1, source_target_pairs={{0,1},{1,0},{2,3},{3,2},{4,5},{5,4},{6,7},{7,6},{8,9},{9,8},{10,11... | collective-permute-start | bytes 811016 | tf_op jit(solution)/shard_map/ppermute | solution.py:329
  41.6 14.5 %collective-permute-start.14 = (bf16[64,4224]{1,0:T(8,128)(2,1)S(1)}, bf16[64,4224]{1,0:T(8,128)(2,1)S(1)}, u32[]{:S(2)}, u32[]{:S(2)}) collective-permute-start(bf16[64,4224]{1,0:T(8,128)(2,1)S(1)} %collective-permute-done.8.refs_12_.refs_1_), channel_id=1, source_target_pairs={{0,4},{1,3},{2,6},{3,1},{4,0},{5,7},{6,2},{7,5},{8,12},{9,11},{10,... | collective-permute-start | bytes 1622024 | tf_op jit(solution)/shard_map/ppermute | solution.py:317
  43.2 10.8 %collective-permute-start.15 = (bf16[32,4224]{1,0:T(8,128)(2,1)S(1)}, bf16[32,4224]{1,0:T(8,128)(2,1)S(1)}, u32[]{:S(2)}, u32[]{:S(2)}) collective-permute-start(bf16[32,4224]{1,0:T(8,128)(2,1)S(1)} %collective-permute-done.7.refs_0_), channel_id=1, source_target_pairs={{0,2},{1,5},{2,0},{3,7},{4,6},{5,1},{6,4},{7,3},{8,10},{9,13},{10,... | collective-permute-start | bytes 811016 | tf_op jit(solution)/shard_map/ppermute | solution.py:317
  43.7 12.3 %collective-permute-start.16 = (bf16[32,4224]{1,0:T(8,128)(2,1)S(1)}, bf16[32,4224]{1,0:T(8,128)(2,1)S(1)}, u32[]{:S(2)}, u32[]{:S(2)}) collective-permute-start(bf16[32,4224]{1,0:T(8,128)(2,1)S(1)} %collective-permute-done.7.refs_0_), channel_id=1, source_target_pairs={{0,4},{1,3},{2,6},{3,1},{4,0},{5,7},{6,2},{7,5},{8,12},{9,11},{10,... | collective-permute-start | bytes 811016 | tf_op jit(solution)/shard_map/ppermute | solution.py:317
  45.0 2.8 %copy-start = (bf16[1,768,4096]{2,1,0:T(8,128)(2,1)S(1)}, bf16[1,768,4096]{2,1,0:T(8,128)(2,1)}, u32[]{:S(2)}) copy-start(bf16[1,768,4096]{2,1,0:T(8,128)(2,1)} %param.23) | copy-start | bytes 18874372
  56.1 9.9 %collective-permute-start.17 = (bf16[128,4096]{1,0:T(8,128)(2,1)S(1)}, bf16[128,4096]{1,0:T(8,128)(2,1)S(1)}, u32[]{:S(2)}, u32[]{:S(2)}) collective-permute-start(bf16[128,4096]{1,0:T(8,128)(2,1)S(1)} %get-tuple-element.101), channel_id=1, source_target_pairs={{0,1},{1,0},{2,3},{3,2},{4,5},{5,4},{6,7},{7,6},{8,9},{9,8},{10,11... | collective-permute-start | bytes 3145736 | tf_op jit(solution)/shard_map/ppermute | solution.py:329
  56.1 3.4 %collective-permute-start.19 = (bf16[64,4224]{1,0:T(8,128)(2,1)S(1)}, bf16[64,4224]{1,0:T(8,128)(2,1)S(1)}, u32[]{:S(2)}, u32[]{:S(2)}) collective-permute-start(bf16[64,4224]{1,0:T(8,128)(2,1)S(1)} %constant_dynamic-update-slice_fusion.refs_0_), channel_id=1, source_target_pairs={{0,1},{1,0},{2,3},{3,2},{4,5},{5,4},{6,7},{7,6},{8,9},{9,8},{10,11... | collective-permute-start | bytes 1622024 | tf_op jit(solution)/shard_map/ppermute | solution.py:329
  56.6 7.9 %collective-permute-start.20 = (bf16[64,4224]{1,0:T(8,128)(2,1)S(1)}, bf16[64,4224]{1,0:T(8,128)(2,1)S(1)}, u32[]{:S(2)}, u32[]{:S(2)}) collective-permute-start(bf16[64,4224]{1,0:T(8,128)(2,1)S(1)} %collective-permute-done.8.refs_12_.refs_1_), channel_id=1, source_target_pairs={{0,1},{1,0},{2,3},{3,2},{4,5},{5,4},{6,7},{7,6},{8,9},{9,8},{10,11... | collective-permute-start | bytes 1622024 | tf_op jit(solution)/shard_map/ppermute | solution.py:329
  56.6 7.9 %collective-permute-start.21 = (bf16[64,4224]{1,0:T(8,128)(2,1)S(1)}, bf16[64,4224]{1,0:T(8,128)(2,1)S(1)}, u32[]{:S(2)}, u32[]{:S(2)}) collective-permute-start(bf16[64,4224]{1,0:T(8,128)(2,1)S(1)} %collective-permute-done.9.refs_2_), channel_id=1, source_target_pairs={{0,1},{1,0},{2,3},{3,2},{4,5},{5,4},{6,7},{7,6},{8,9},{9,8},{10,11... | collective-permute-start | bytes 1622024 | tf_op jit(solution)/shard_map/ppermute | solution.py:329
  57.1 8.9 %collective-permute-start.22 = (bf16[64,4224]{1,0:T(8,128)(2,1)S(1)}, bf16[64,4224]{1,0:T(8,128)(2,1)S(1)}, u32[]{:S(2)}, u32[]{:S(2)}) collective-permute-start(bf16[64,4224]{1,0:T(8,128)(2,1)S(1)} %collective-permute-done.14.refs_0_.refs_3_), channel_id=1, source_target_pairs={{0,1},{1,0},{2,3},{3,2},{4,5},{5,4},{6,7},{7,6},{8,9},{9,8},{10,11... | collective-permute-start | bytes 1622024 | tf_op jit(solution)/shard_map/ppermute | solution.py:329
  59.5 6.5 %collective-permute-start.18 = (bf16[32,4224]{1,0:T(8,128)(2,1)S(1)}, bf16[32,4224]{1,0:T(8,128)(2,1)S(1)}, u32[]{:S(2)}, u32[]{:S(2)}) collective-permute-start(bf16[32,4224]{1,0:T(8,128)(2,1)S(1)} %collective-permute-done.15.refs_1_), channel_id=1, source_target_pairs={{0,4},{1,3},{2,6},{3,1},{4,0},{5,7},{6,2},{7,5},{8,12},{9,11},{10,... | collective-permute-start | bytes 811016 | tf_op jit(solution)/shard_map/ppermute | solution.py:317
  66.1 9.2 %collective-permute-start.23 = (bf16[64,4096]{1,0:T(8,128)(2,1)S(1)}, bf16[64,4096]{1,0:T(8,128)(2,1)S(1)}, u32[]{:S(2)}, u32[]{:S(2)}) collective-permute-start(bf16[64,4096]{1,0:T(8,128)(2,1)S(1)} %add_convert_fusion.3.refs_12_), channel_id=1, source_target_pairs={{0,4},{1,3},{2,6},{3,1},{4,0},{5,7},{6,2},{7,5},{8,12},{9,11},{10,... | collective-permute-start | bytes 1572872 | tf_op jit(solution)/shard_map/ppermute | solution.py:317
  67.3 6.4 %collective-permute-start.24 = (bf16[32,4224]{1,0:T(8,128)(2,1)S(1)}, bf16[32,4224]{1,0:T(8,128)(2,1)S(1)}, u32[]{:S(2)}, u32[]{:S(2)}) collective-permute-start(bf16[32,4224]{1,0:T(8,128)(2,1)S(1)} %collective-permute-done.7.refs_0_), channel_id=1, source_target_pairs={{0,1},{1,0},{2,3},{3,2},{4,5},{5,4},{6,7},{7,6},{8,9},{9,8},{10,11... | collective-permute-start | bytes 811016 | tf_op jit(solution)/shard_map/ppermute | solution.py:329
  67.3 6.4 %collective-permute-start.25 = (bf16[32,4224]{1,0:T(8,128)(2,1)S(1)}, bf16[32,4224]{1,0:T(8,128)(2,1)S(1)}, u32[]{:S(2)}, u32[]{:S(2)}) collective-permute-start(bf16[32,4224]{1,0:T(8,128)(2,1)S(1)} %collective-permute-done.15.refs_1_), channel_id=1, source_target_pairs={{0,1},{1,0},{2,3},{3,2},{4,5},{5,4},{6,7},{7,6},{8,9},{9,8},{10,11... | collective-permute-start | bytes 811016 | tf_op jit(solution)/shard_map/ppermute | solution.py:329
  67.8 5.9 %collective-permute-start.26 = (bf16[32,4224]{1,0:T(8,128)(2,1)S(1)}, bf16[32,4224]{1,0:T(8,128)(2,1)S(1)}, u32[]{:S(2)}, u32[]{:S(2)}) collective-permute-start(bf16[32,4224]{1,0:T(8,128)(2,1)S(1)} %collective-permute-done.16.refs_2_), channel_id=1, source_target_pairs={{0,1},{1,0},{2,3},{3,2},{4,5},{5,4},{6,7},{7,6},{8,9},{9,8},{10,11... | collective-permute-start | bytes 811016 | tf_op jit(solution)/shard_map/ppermute | solution.py:329
  67.8 5.9 %collective-permute-start.27 = (bf16[32,4224]{1,0:T(8,128)(2,1)S(1)}, bf16[32,4224]{1,0:T(8,128)(2,1)S(1)}, u32[]{:S(2)}, u32[]{:S(2)}) collective-permute-start(bf16[32,4224]{1,0:T(8,128)(2,1)S(1)} %collective-permute-done.18.refs_3_), channel_id=1, source_target_pairs={{0,1},{1,0},{2,3},{3,2},{4,5},{5,4},{6,7},{7,6},{8,9},{9,8},{10,11... | collective-permute-start | bytes 811016 | tf_op jit(solution)/shard_map/ppermute | solution.py:329
  75.3 2.7 %collective-permute-start.28 = (bf16[128,4096]{1,0:T(8,128)(2,1)S(1)}, bf16[128,4096]{1,0:T(8,128)(2,1)S(1)}, u32[]{:S(2)}, u32[]{:S(2)}) collective-permute-start(bf16[128,4096]{1,0:T(8,128)(2,1)S(1)} %get-tuple-element.119), channel_id=1, source_target_pairs={{0,1},{1,0},{2,3},{3,2},{4,5},{5,4},{6,7},{7,6},{8,9},{9,8},{10,11... | collective-permute-start | bytes 3145736 | tf_op jit(solution)/shard_map/ppermute | solution.py:329
  78.1 12.1 %collective-permute-start.30 = (bf16[64,4096]{1,0:T(8,128)(2,1)S(1)}, bf16[64,4096]{1,0:T(8,128)(2,1)S(1)}, u32[]{:S(2)}, u32[]{:S(2)}) collective-permute-start(bf16[64,4096]{1,0:T(8,128)(2,1)S(1)} %add_convert_fusion.2.refs_11_), channel_id=1, source_target_pairs={{0,4},{1,3},{2,6},{3,1},{4,0},{5,7},{6,2},{7,5},{8,12},{9,11},{10,... | collective-permute-start | bytes 1572872 | tf_op jit(solution)/shard_map/ppermute | solution.py:317
  79.4 9.3 %collective-permute-start.29 = (bf16[32,4096]{1,0:T(8,128)(2,1)S(1)}, bf16[32,4096]{1,0:T(8,128)(2,1)S(1)}, u32[]{:S(2)}, u32[]{:S(2)}) collective-permute-start(bf16[32,4096]{1,0:T(8,128)(2,1)S(1)} %add_convert_fusion.11.refs_12_), channel_id=1, source_target_pairs={{0,2},{1,5},{2,0},{3,7},{4,6},{5,1},{6,4},{7,3},{8,10},{9,13},{10,... | collective-permute-start | bytes 786440 | tf_op jit(solution)/shard_map/ppermute | solution.py:317
  90.2 4.4 %collective-permute-start.32 = (bf16[128,4096]{1,0:T(8,128)(2,1)S(1)}, bf16[128,4096]{1,0:T(8,128)(2,1)S(1)}, u32[]{:S(2)}, u32[]{:S(2)}) collective-permute-start(bf16[128,4096]{1,0:T(8,128)(2,1)S(1)} %get-tuple-element.136), channel_id=1, source_target_pairs={{0,1},{1,0},{2,3},{3,2},{4,5},{5,4},{6,7},{7,6},{8,9},{9,8},{10,11... | collective-permute-start | bytes 3145736 | tf_op jit(solution)/shard_map/ppermute | solution.py:329
  90.2 7.3 %collective-permute-start.34 = (bf16[32,4096]{1,0:T(8,128)(2,1)S(1)}, bf16[32,4096]{1,0:T(8,128)(2,1)S(1)}, u32[]{:S(2)}, u32[]{:S(2)}) collective-permute-start(bf16[32,4096]{1,0:T(8,128)(2,1)S(1)} %attend.4.refs_0_), channel_id=1, source_target_pairs={{0,1},{1,0},{2,3},{3,2},{4,5},{5,4},{6,7},{7,6},{8,9},{9,8},{10,11... | collective-permute-start | bytes 786440 | tf_op jit(solution)/shard_map/ppermute | solution.py:329
  94.8 12.1 %collective-permute-start.33 = (bf16[64,4096]{1,0:T(8,128)(2,1)S(1)}, bf16[64,4096]{1,0:T(8,128)(2,1)S(1)}, u32[]{:S(2)}, u32[]{:S(2)}) collective-permute-start(bf16[64,4096]{1,0:T(8,128)(2,1)S(1)} %add_convert_fusion.1.refs_11_), channel_id=1, source_target_pairs={{0,4},{1,3},{2,6},{3,1},{4,0},{5,7},{6,2},{7,5},{8,12},{9,11},{10,... | collective-permute-start | bytes 1572872 | tf_op jit(solution)/shard_map/ppermute | solution.py:317
  96.0 7.2 %collective-permute-start.35 = (bf16[32,4096]{1,0:T(8,128)(2,1)S(1)}, bf16[32,4096]{1,0:T(8,128)(2,1)S(1)}, u32[]{:S(2)}, u32[]{:S(2)}) collective-permute-start(bf16[32,4096]{1,0:T(8,128)(2,1)S(1)} %attend.5.refs_11_.refs_4_), channel_id=1, source_target_pairs={{0,1},{1,0},{2,3},{3,2},{4,5},{5,4},{6,7},{7,6},{8,9},{9,8},{10,11... | collective-permute-start | bytes 786440 | tf_op jit(solution)/shard_map/ppermute | solution.py:329
  96.0 7.2 %collective-permute-start.36 = (bf16[32,4096]{1,0:T(8,128)(2,1)S(1)}, bf16[32,4096]{1,0:T(8,128)(2,1)S(1)}, u32[]{:S(2)}, u32[]{:S(2)}) collective-permute-start(bf16[32,4096]{1,0:T(8,128)(2,1)S(1)} %attend.6.refs_11_.refs_1_), channel_id=1, source_target_pairs={{0,1},{1,0},{2,3},{3,2},{4,5},{5,4},{6,7},{7,6},{8,9},{9,8},{10,11... | collective-permute-start | bytes 786440 | tf_op jit(solution)/shard_map/ppermute | solution.py:329
  96.5 9.2 %collective-permute-start.31 = (bf16[32,4096]{1,0:T(8,128)(2,1)S(1)}, bf16[32,4096]{1,0:T(8,128)(2,1)S(1)}, u32[]{:S(2)}, u32[]{:S(2)}) collective-permute-start(bf16[32,4096]{1,0:T(8,128)(2,1)S(1)} %add_convert_fusion.10.refs_0_.refs_12_), channel_id=1, source_target_pairs={{0,2},{1,5},{2,0},{3,7},{4,6},{5,1},{6,4},{7,3},{8,10},{9,13},{10,... | collective-permute-start | bytes 786440 | tf_op jit(solution)/shard_map/ppermute | solution.py:317
  97.6 8.2 %collective-permute-start.37 = (bf16[32,4096]{1,0:T(8,128)(2,1)S(1)}, bf16[32,4096]{1,0:T(8,128)(2,1)S(1)}, u32[]{:S(2)}, u32[]{:S(2)}) collective-permute-start(bf16[32,4096]{1,0:T(8,128)(2,1)S(1)} %attend.7.refs_5_), channel_id=1, source_target_pairs={{0,1},{1,0},{2,3},{3,2},{4,5},{5,4},{6,7},{7,6},{8,9},{9,8},{10,11... | collective-permute-start | bytes 786440 | tf_op jit(solution)/shard_map/ppermute | solution.py:329
  106.8 2.7 %collective-permute-start.38 = (bf16[128,4096]{1,0:T(8,128)(2,1)S(1)}, bf16[128,4096]{1,0:T(8,128)(2,1)S(1)}, u32[]{:S(2)}, u32[]{:S(2)}) collective-permute-start(bf16[128,4096]{1,0:T(8,128)(2,1)S(1)} %get-tuple-element.143), channel_id=1, source_target_pairs={{0,1},{1,0},{2,3},{3,2},{4,5},{5,4},{6,7},{7,6},{8,9},{9,8},{10,11... | collective-permute-start | bytes 3145736 | tf_op jit(solution)/shard_map/ppermute | solution.py:329
  106.9 8.1 %collective-permute-start.39 = (bf16[32,4096]{1,0:T(8,128)(2,1)S(1)}, bf16[32,4096]{1,0:T(8,128)(2,1)S(1)}, u32[]{:S(2)}, u32[]{:S(2)}) collective-permute-start(bf16[32,4096]{1,0:T(8,128)(2,1)S(1)} %add_convert_fusion.9), channel_id=1, source_target_pairs={{0,2},{1,5},{2,0},{3,7},{4,6},{5,1},{6,4},{7,3},{8,10},{9,13},{10,... | collective-permute-start | bytes 786440 | tf_op jit(solution)/shard_map/ppermute | solution.py:317
  109.6 9.2 %collective-permute-start.40 = (bf16[64,4096]{1,0:T(8,128)(2,1)S(1)}, bf16[64,4096]{1,0:T(8,128)(2,1)S(1)}, u32[]{:S(2)}, u32[]{:S(2)}) collective-permute-start(bf16[64,4096]{1,0:T(8,128)(2,1)S(1)} %add_convert_fusion), channel_id=1, source_target_pairs={{0,4},{1,3},{2,6},{3,1},{4,0},{5,7},{6,2},{7,5},{8,12},{9,11},{10,... | collective-permute-start | bytes 1572872 | tf_op jit(solution)/shard_map/ppermute | solution.py:317
  110.9 21.1 %collective-permute-start.43 = (bf16[32,4096]{1,0:T(8,128)(2,1)S(1)}, bf16[32,4096]{1,0:T(8,128)(2,1)S(1)}, u32[]{:S(2)}, u32[]{:S(2)}) collective-permute-start(bf16[32,4096]{1,0:T(8,128)(2,1)S(1)} %add_convert_fusion.6), channel_id=1, source_target_pairs={{0,16},{1,17},{2,18},{3,19},{4,20},{5,21},{6,22},{7,23},{8,24},{9,... | collective-permute-start | bytes 786440 | tf_op jit(solution)/shard_map/ppermute | solution.py:317
  119.0 6.4 %collective-permute-start.41 = (bf16[32,4096]{1,0:T(8,128)(2,1)S(1)}, bf16[32,4096]{1,0:T(8,128)(2,1)S(1)}, u32[]{:S(2)}, u32[]{:S(2)}) collective-permute-start(bf16[32,4096]{1,0:T(8,128)(2,1)S(1)} %add_convert_fusion.8), channel_id=1, source_target_pairs={{0,2},{1,5},{2,0},{3,7},{4,6},{5,1},{6,4},{7,3},{8,10},{9,13},{10,... | collective-permute-start | bytes 786440 | tf_op jit(solution)/shard_map/ppermute | solution.py:317
  120.2 11.8 %collective-permute-start.44 = (bf16[32,4096]{1,0:T(8,128)(2,1)S(1)}, bf16[32,4096]{1,0:T(8,128)(2,1)S(1)}, u32[]{:S(2)}, u32[]{:S(2)}) collective-permute-start(bf16[32,4096]{1,0:T(8,128)(2,1)S(1)} %add_convert_fusion.5), channel_id=1, source_target_pairs={{0,24},{1,25},{2,26},{3,27},{4,28},{5,29},{6,30},{7,31},{8,16},{9,... | collective-permute-start | bytes 786440 | tf_op jit(solution)/shard_map/ppermute | solution.py:317
  125.5 11.2 %collective-permute-start.42 = (bf16[32,4096]{1,0:T(8,128)(2,1)S(1)}, bf16[32,4096]{1,0:T(8,128)(2,1)S(1)}, u32[]{:S(2)}, u32[]{:S(2)}) collective-permute-start(bf16[32,4096]{1,0:T(8,128)(2,1)S(1)} %add_convert_fusion.7), channel_id=1, source_target_pairs={{0,8},{1,9},{2,10},{3,11},{4,12},{5,13},{6,14},{7,15},{8,0},{9,1},... | collective-permute-start | bytes 786440 | tf_op jit(solution)/shard_map/ppermute | solution.py:317
where the time goes:
time: 138 us
  waiting for transfers between devices  44.1 us (32%)
  Pallas kernels  41.6 us (30%)
  starting transfers between devices  37.6 us (27%)
  local copies, waits for them, and re-layouts  9.52 us (7%)
  other arithmetic  3.98 us (3%)
    ppermute x23, waiting for transfers between devices, swap(): return lax.ppermute(value, ('ep', 'fan'), pairs)  37.6 us
    ppermute x23, starting transfers between devices, swap(): return lax.ppermute(value, ('ep', 'fan'), pairs)  33.6 us
    pallas_call x4, Pallas kernels, expert_chunk(): pl.pallas_call(functools.partial(expert_kernel, count, at_row, tokens), o...  22.8 us
    pallas_call x4, Pallas kernels, attend(): pl.pallas_call(functools.partial(attend_kernel, local, heads), out_shape=...  15.2 us
    unnamed x17, local copies, waits for them, and re-layouts  6.62 us
    ppermute x22, waiting for transfers between devices, beside(): return lax.ppermute(value, 'fan', [(0, 1), (1, 0)])  6.56 us
    ppermute x22, starting transfers between devices, beside(): return lax.ppermute(value, 'fan', [(0, 1), (1, 0)])  3.95 us
  transfers between devices with their start and end apart: 45, of which 16 were waited for; matrix products, arithmetic and copies ran while one was open for 5% of the time, Pallas kernels for 29%

commit v1 on v0

--- a/solution.py
+++ b/solution.py
@@ -28,6 +28,9 @@
 
 
 SMALL = pl.CostEstimate(flops=1 << 20, bytes_accessed=1 << 14, transcendentals=0)
+
+
+LARGE = pl.CostEstimate(flops=20 << 30, bytes_accessed=1 << 20, transcendentals=0)
 
 
 def norm_kernel(hidden_ref, gain_ref, ids_ref, logits_ref, out_ref):
@@ -63,9 +66,33 @@
     return pl.pallas_call(
         norm_kernel,
         out_shape=jax.ShapeDtypeStruct((rows, width + LANES), jnp.bfloat16),
-        cost_estimate=SMALL,
+        cost_estimate=LARGE,
         name="norm_message",
     )(hidden, gain, ids.T, logits.T)
+
+
+def stack_kernel(top, bottom, out, sem):
+    rows = top.shape[0]
+    upper = pltpu.make_async_copy(top, out.at[pl.ds(0, rows)], sem.at[0])
+    lower = pltpu.make_async_copy(bottom, out.at[pl.ds(rows, rows)], sem.at[1])
+    upper.start()
+    lower.start()
+    upper.wait()
+    lower.wait()
+
+
+def stack(top, bottom):
+    rows, width = top.shape
+    anywhere = pl.BlockSpec(memory_space=pl.ANY)
+    return pl.pallas_call(
+        stack_kernel,
+        out_shape=jax.ShapeDtypeStruct((2 * rows, width), top.dtype),
+        in_specs=[anywhere, anywhere],
+        out_specs=anywhere,
+        scratch_shapes=[pltpu.SemaphoreType.DMA((2,))],
+        cost_estimate=SMALL,
+        name="stack",
+    )(top, bottom)
 
 
 def rank_rows(match, rows):
@@ -371,59 +398,64 @@
 
     level_2, level_1 = far(token, 2), far(token, 1)
     first_0, cross_0 = near(token), cross(token)
-    pair = jnp.concatenate([level_2, level_1], axis=0)
+    third_0 = cross(first_0)
+    pair = stack(level_2, level_1)
     level_3 = far(level_2, 1)
-    third_0 = cross(first_0)
     context_0a = attend_half(0, 0, pair, first_0, cross_0)
-    context_0a, third_0 = sync((context_0a, third_0))
+    context_0a, third_0, level_3 = sync((context_0a, third_0, level_3))
     pieces_0 = with_fan([token, first_0, cross_0, third_0])
     context_0b = attend_half(0, 1, context_0a)
-    context_0b, level_3, first_p, cross_p, *pieces_0 = sync(
-        (context_0b, level_3, near(pair), cross(pair), *pieces_0)
+    context_0b, first_p, cross_p, *pieces_0 = sync(
+        (context_0b, near(pair), cross(pair), *pieces_0)
     )
     third_p = cross(first_p)
     first_3, cross_3 = near(level_3), cross(level_3)
+    fans_p = [beside(value) for value in (pair, first_p, cross_p)]
     result_0 = expert(pieces_0, 0, context_0b, first_p)
 
-    third_p, first_3, cross_3, result_0 = sync((third_p, first_3, cross_3, result_0))
+    third_p, result_0, *fans_p = sync((third_p, result_0, *fans_p))
     back_0 = beside(result_0[2])
-    pieces_p = with_fan([pair, first_p, cross_p, third_p])
+    pieces_p = [pair, first_p, cross_p, third_p, *fans_p, beside(third_p)]
+    result_2 = expert(pieces_p, 0, result_0[0])
+
+    first_3, cross_3, back_0, result_2 = sync((first_3, cross_3, back_0, result_2))
+    back_2 = beside(result_2[2])
     third_3 = cross(first_3)
-    context_1a = attend_half(1, 0, third_p, first_3)
-    context_1a, back_0, third_3, *pieces_p = sync((context_1a, back_0, third_3, *pieces_p))
-    there_0 = sum_cores(result_0, back_0)
-    pieces_3 = with_fan([level_3, first_3, cross_3, third_3])
-    result_2 = expert(pieces_p, 0, context_1a, there_0)
-
-    turned_0, result_2, *pieces_3 = sync((cross(there_0), result_2, *pieces_3))
-    back_2 = beside(result_2[2])
-    held_0, passed_0 = sum_cross(result_0, back_0, turned_0)
+    fans_3 = [beside(value) for value in (level_3, first_3, cross_3)]
+    context_1a = attend_half(1, 0, first_3, cross_3)
+    context_1a, third_3, back_2, *fans_3 = sync((context_1a, third_3, back_2, *fans_3))
+    pieces_3 = [level_3, first_3, cross_3, third_3, *fans_3, beside(third_3)]
     there_2 = sum_cores(result_2, back_2)
-    result_3 = expert(pieces_3, 0, there_2, passed_0)
-
-    ended_0, turned_2, result_3 = sync((near(passed_0), cross(there_2), result_3))
+    result_3 = expert(pieces_3, 0, there_2, context_1a)
+
+    turned_2, result_3 = sync((cross(there_2), result_3))
     back_3 = beside(result_3[2])
     held_2, passed_2 = sum_cross(result_2, back_2, turned_2)
-    context_1b = attend_half(1, 1, passed_2)
-    context_1b, back_3 = sync((context_1b, back_3))
     there_3 = sum_cores(result_3, back_3)
-    result_1 = expert(pieces_p, tokens, there_3, passed_2)
-
-    contexts = [context_0a, context_0b, context_1a, context_1b]
+    there_0 = sum_cores(result_0, back_0)
+    total_2 = narrow(held_2 + widen(near(passed_2)))
+    far_2 = far(total_2, 2)
+    result_1 = expert(pieces_p, tokens, there_3, there_0, total_2)
+
+    contexts = [context_0a, context_0b, context_1a]
     sent = [beside(value) for value in contexts]
-    ended_2, turned_3, result_1, sent = sync((near(passed_2), cross(there_3), result_1, sent))
+    turned_0, turned_3, result_1, *sent = sync((cross(there_0), cross(there_3), result_1, *sent))
     back_1 = beside(result_1[2])
     held_3, passed_3 = sum_cross(result_3, back_3, turned_3)
+    held_0, passed_0 = sum_cross(result_0, back_0, turned_0)
+    there_1 = sum_cores(result_1, back_1)
+    total_3 = narrow(held_3 + widen(near(passed_3)))
+    far_3 = far(total_3, 3)
+    held_1, passed_1 = sum_cross(result_1, back_1, cross(there_1))
+    context_1b = attend_half(1, 1, total_3, passed_1)
+
+    far_1 = far(narrow(held_1 + widen(near(passed_1))), 1)
+    contexts, sent = contexts + [context_1b], sent + [beside(context_1b)]
     ordered = [contexts[0], contexts[2], sent[0], sent[2], contexts[1], contexts[3], sent[1], sent[3]]
-    far_2 = far(narrow(held_2 + widen(ended_2)), 2)
-    there_1 = sum_cores(result_1, back_1)
-    own_late, _ = sync((own_mine, there_1))
+    own_late, far_2 = sync((own_mine, far_2))
     context = place_context(own_late, ordered, jax.ShapeDtypeStruct(queries.shape, jnp.bfloat16))
-    context, ended_3 = sync((context, near(passed_3)))
-    far_3 = far(narrow(held_3 + widen(ended_3)), 3)
-    held_1, passed_1 = sum_cross(result_1, back_1, cross(there_1))
-    far_1 = far(narrow(held_1 + widen(near(passed_1))), 1)
-    total = held_0 + widen(ended_0) + widen(far_1)
+    context, far_1, far_3 = sync((context, far_1, far_3))
+    total = held_0 + widen(near(passed_0)) + widen(far_1)
     expert_out = narrow(total + widen(far_2) + widen(far_3))
     return (context, expert_out)
 

time: 138 us -> 154 us (1.12)
  Pallas kernels: 41.6 us -> 62.6 us
  waiting for transfers between devices: 44.1 us -> 38.3 us
  local copies, waits for them, and re-layouts: 9.52 us -> 12.3 us
  other arithmetic: 3.98 us -> 2.37 us
    pallas_call x0 -> x1, Pallas kernels: none -> 17.5 us  [stack(): pl.pallas_call(stack_kernel, out_shape=jax.ShapeDtypeStruct((2 * rows, wi...]
    unnamed x17 -> x42, local copies, waits for them, and re-layouts: 6.62 us -> 11.8 us
    ppermute x22, waiting for transfers between devices: 6.56 us -> 3.39 us  [beside(): return lax.ppermute(value, 'fan', [(0, 1), (1, 0)])]
    pallas_call x4, Pallas kernels: 15.2 us -> 18.1 us  [attend(): pl.pallas_call(functools.partial(attend_kernel, local, heads), out_shape=...]
    ppermute x23, waiting for transfers between devices: 37.6 us -> 34.9 us  [swap(): return lax.ppermute(value, ('ep', 'fan'), pairs)]
    ppermute x23, starting transfers between devices: 33.6 us -> 32 us  [swap(): return lax.ppermute(value, ('ep', 'fan'), pairs)]
  transfers between devices with their start and end apart: 45 -> 45, of which waited for: 16 -> 11; matrix products, arithmetic and copies ran while one was open for 5% -> 1% of each run, Pallas kernels for 29% -> 40%
where the time goes in v1:
time: 154 us; the launch traced here: 153 us
  Pallas kernels  62.6 us (41%)
  waiting for transfers between devices  38.3 us (25%)
  starting transfers between devices  36.5 us (24%)
  local copies, waits for them, and re-layouts  12.3 us (8%)
  other arithmetic  2.37 us (2%)
    ppermute x23, waiting for transfers between devices, swap(): return lax.ppermute(value, ('ep', 'fan'), pairs)  34.9 us
    ppermute x23, starting transfers between devices, swap(): return lax.ppermute(value, ('ep', 'fan'), pairs)  32 us
    pallas_call x4, Pallas kernels, expert_chunk(): pl.pallas_call(functools.partial(expert_kernel, count, at_row, tokens), o...  23.4 us
    pallas_call x4, Pallas kernels, attend(): pl.pallas_call(functools.partial(attend_kernel, local, heads), out_shape=...  18.1 us
    pallas_call x1, Pallas kernels, stack(): pl.pallas_call(stack_kernel, out_shape=jax.ShapeDtypeStruct((2 * rows, wi...  17.5 us
    unnamed x42, local copies, waits for them, and re-layouts  11.8 us
    ppermute x22, starting transfers between devices, beside(): return lax.ppermute(value, 'fan', [(0, 1), (1, 0)])  4.48 us
    ppermute x22, waiting for transfers between devices, beside(): return lax.ppermute(value, 'fan', [(0, 1), (1, 0)])  3.39 us
  transfers between devices with their start and end apart: 45, of which 11 were waited for; matrix products, arithmetic and copies ran while one was open for 1% of the time, Pallas kernels for 40%

profile of v1, /device:TPU:0, one launch (start us, length us, event | category | flops | bytes accessed | tf_op | source)
XLA Modules:
  0.0 153.3 jit_solution(11791544031215034589)
XLA Ops:
  0.7 2.0 %norm_message.1.refs_0_ = bf16[32,4224]{1,0:T(8,128)(2,1)} custom-call(bf16[32,4096]{1,0:T(8,128)(2,1)} %hidden_ref.1, bf16[4096]{0:T(1024)(128)(2,1)} %gain_ref.1, s32[8,32]{1,0:T(8,128)} %bitcast.23, f32[8,32]{1,0:T(8,128)} %bitcast.24), custom_call_target="tpu_custom_call" | custom-call | flops 21474836480 | bytes 1048576 | tf_op jit(solution)/shard_map/norm_message/pallas_call | solution.py:66
  2.7 0.4 reshape.12.q_mine
  3.1 0.5 collective-permute-start
  3.6 3.7 %collective-permute-start.2 = (bf16[32,4224]{1,0:T(8,128)(2,1)}, bf16[32,4224]{1,0:T(8,128)(2,1)}, u32[]{:S(2)}, u32[]{:S(2)}) collective-permute-start(bf16[32,4224]{1,0:T(8,128)(2,1)} %norm_message.1.refs_0_), channel_id=1, source_target_pairs={{0,16},{1,17},{2,18},{3,19},{4,20},{5,21},{6,22},{7,23},{8,24},{9,... | collective-permute-start | bytes 811016 | tf_op jit(solution)/shard_map/ppermute | solution.py:344
  7.3 1.6 %collective-permute-start.3 = (bf16[32,4224]{1,0:T(8,128)(2,1)}, bf16[32,4224]{1,0:T(8,128)(2,1)S(1)}, u32[]{:S(2)}, u32[]{:S(2)}) collective-permute-start(bf16[32,4224]{1,0:T(8,128)(2,1)} %norm_message.1.refs_0_), channel_id=1, source_target_pairs={{0,8},{1,9},{2,10},{3,11},{4,12},{5,13},{6,14},{7,15},{8,0},{9,1},... | collective-permute-start | bytes 811016 | tf_op jit(solution)/shard_map/ppermute | solution.py:344
  8.9 1.5 collective-permute-start.4
  10.4 1.5 collective-permute-start.5
  12.0 0.1 pad_maximum_fusion
  12.2 8.4 %collective-permute-done.2.top = bf16[32,4224]{1,0:T(8,128)(2,1)} collective-permute-done((bf16[32,4224]{1,0:T(8,128)(2,1)}, bf16[32,4224]{1,0:T(8,128)(2,1)}, u32[]{:S(2)}, u32[]{:S(2)}) %collective-permute-start.2) | collective-permute-done | bytes 270368 | tf_op jit(solution)/shard_map/ppermute | solution.py:344
  20.6 1.6 %collective-permute-start.6 = (bf16[32,4224]{1,0:T(8,128)(2,1)}, bf16[32,4224]{1,0:T(8,128)(2,1)}, u32[]{:S(2)}, u32[]{:S(2)}) collective-permute-start(bf16[32,4224]{1,0:T(8,128)(2,1)} %collective-permute-done.4.refs_1_), channel_id=1, source_target_pairs={{0,4},{1,3},{2,6},{3,1},{4,0},{5,7},{6,2},{7,5},{8,12},{9,11},{10,... | collective-permute-start | bytes 811016 | tf_op jit(solution)/shard_map/ppermute | solution.py:344
  22.2 0.7 copy-done.12
  22.9 0.6 collective-permute-start.7
  23.5 17.5 %stack.1.refs_0_ = bf16[64,4224]{1,0:T(8,128)(2,1)} custom-call(bf16[32,4224]{1,0:T(8,128)(2,1)} %collective-permute-done.2.top, bf16[32,4224]{1,0:T(8,128)(2,1)} %copy-done.12), custom_call_target="tpu_custom_call" | custom-call | flops 1048576 | bytes 16384 | tf_op jit(solution)/shard_map/stack/pallas_call | solution.py:87
  41.1 1.6 %collective-permute-start.10 = (bf16[64,4224]{1,0:T(8,128)(2,1)}, bf16[64,4224]{1,0:T(8,128)(2,1)S(1)}, u32[]{:S(2)}, u32[]{:S(2)}) collective-permute-start(bf16[64,4224]{1,0:T(8,128)(2,1)} %stack.1.refs_0_), channel_id=1, source_target_pairs={{0,2},{1,5},{2,0},{3,7},{4,6},{5,1},{6,4},{7,3},{8,10},{9,13},{10,... | collective-permute-start | bytes 1622024 | tf_op jit(solution)/shard_map/ppermute | solution.py:344
  42.7 0.9 collective-permute-start.11
  43.6 2.2 %copy-done.2 = bf16[2,1024,1024]{2,1,0:T(8,128)(2,1)S(1)} copy-done((bf16[2,1024,1024]{2,1,0:T(8,128)(2,1)S(1)}, bf16[2,1024,1024]{2,1,0:T(8,128)(2,1)}, u32[]{:S(2)}) %copy-start.2) | copy-done | bytes 4194328
  45.8 1.0 copy-done.5
  46.8 4.6 %attend.4.refs_0_ = bf16[32,4096]{1,0:T(8,128)(2,1)S(1)} custom-call(s32[4]{0:T(128)S(1)} %copy-done.8, bf16[64,8192]{1,0:T(8,128)(2,1)S(1)} %reshape.12.q_mine, bf16[64,8192]{1,0:T(8,128)(2,1)} %collective-permute-done.q_other, bf16[64,1152]{1,0:T(8,128)(2,1)S(1)} %reshape.11.o_mine, bf16[64,1152]{1,0:T(8,128)(2,1)S(1)} %collective-permute-done.1.o_other, ...), custom_call_target="tpu_custom_call" | custom-call | flops 1048576 | bytes 16384 | tf_op jit(solution)/shard_map/attend/pallas_call | solution.py:194
  51.5 0.5 collective-permute-start.14
  52.1 2.2 %copy-done.3 = bf16[2,1024,1024]{2,1,0:T(8,128)(2,1)S(1)} copy-done((bf16[2,1024,1024]{2,1,0:T(8,128)(2,1)S(1)}, bf16[2,1024,1024]{2,1,0:T(8,128)(2,1)}, u32[]{:S(2)}) %copy-start.3) | copy-done | bytes 4194328
  54.3 4.5 %attend.5.refs_11_.refs_4_ = bf16[32,4096]{1,0:T(8,128)(2,1)S(1)} custom-call(s32[4]{0:T(128)S(1)} %copy-done.8, bf16[64,8192]{1,0:T(8,128)(2,1)S(1)} %reshape.12.q_mine, bf16[64,8192]{1,0:T(8,128)(2,1)} %collective-permute-done.q_other, bf16[64,1152]{1,0:T(8,128)(2,1)S(1)} %reshape.11.o_mine, bf16[64,1152]{1,0:T(8,128)(2,1)S(1)} %collective-permute-done.1.o_other, ...), custom_call_target="tpu_custom_call" | custom-call | flops 1048576 | bytes 16384 | tf_op jit(solution)/shard_map/attend/pallas_call | solution.py:194
  58.8 0.5 collective-permute-start.17
  59.3 1.2 collective-permute-start.16
  60.5 0.5 collective-permute-start.19
  61.0 2.8 %copy-done = bf16[1,4096,768]{2,1,0:T(8,128)(2,1)S(1)} copy-done((bf16[1,4096,768]{2,1,0:T(8,128)(2,1)S(1)}, bf16[1,4096,768]{2,1,0:T(8,128)(2,1)}, u32[]{:S(2)}) %copy-start) | copy-done | bytes 6291480
  63.8 2.8 %copy-done.1 = bf16[1,768,4096]{2,1,0:T(8,128)(2,1)S(1)} copy-done((bf16[1,768,4096]{2,1,0:T(8,128)(2,1)S(1)}, bf16[1,768,4096]{2,1,0:T(8,128)(2,1)}, u32[]{:S(2)}) %copy-start.1) | copy-done | bytes 6291480
  66.6 6.3 %expert_chunk.4 = (bf16[64,4096]{1,0:T(8,128)(2,1)S(1)}, bf16[64,4096]{1,0:T(8,128)(2,1)S(1)}, bf16[128,4096]{1,0:T(8,128)(2,1)S(1)}) custom-call(bf16[32,4224]{1,0:T(8,128)(2,1)S(1)} %copy-done.7, bf16[32,4224]{1,0:T(8,128)(2,1)} %collective-permute-done.4.refs_1_, bf16[32,4224]{1,0:T(8,128)(2,1)} %collective-permute-done.5.refs_2_, ...), custom_call_target="tpu_custom_call" | custom-call | flops 1048576 | bytes 16384 | tf_op jit(solution)/shard_map/expert_chunk/pallas_call | solution.py:298
  73.1 0.5 collective-permute-start.21
  73.6 0.5 collective-permute-start.8
  74.1 1.3 collective-permute-start.9
  75.4 1.1 collective-permute-done.21.refs_7_
  76.5 5.5 %expert_chunk.5 = (bf16[64,4096]{1,0:T(8,128)(2,1)S(1)}, bf16[64,4096]{1,0:T(8,128)(2,1)S(1)}, bf16[128,4096]{1,0:T(8,128)(2,1)S(1)}) custom-call(bf16[64,4224]{1,0:T(8,128)(2,1)S(1)} %copy-done.6, bf16[64,4224]{1,0:T(8,128)(2,1)S(1)} %collective-permute-done.10.refs_12_.refs_1_, bf16[64,4224]{1,0:T(8,128)(2,1)S(1)} %collective-permute-done.11.refs_2_, ...), custom_call_target="tpu_custom_call" | custom-call | flops 1048576 | bytes 16384 | tf_op jit(solution)/shard_map/expert_chunk/pallas_call | solution.py:298
  82.0 0.8 collective-permute-done.8.refs_0_.refs_1_
  82.9 0.5 collective-permute-start.24
  83.4 1.1 collective-permute-start.22
  84.6 0.5 collective-permute-start.26
  85.1 4.5 %attend.6.refs_12_.refs_1_ = bf16[32,4096]{1,0:T(8,128)(2,1)S(1)} custom-call(s32[4]{0:T(128)S(1)} %copy-done.8, bf16[64,8192]{1,0:T(8,128)(2,1)S(1)} %reshape.12.q_mine, bf16[64,8192]{1,0:T(8,128)(2,1)} %collective-permute-done.q_other, bf16[64,1152]{1,0:T(8,128)(2,1)S(1)} %reshape.11.o_mine, bf16[64,1152]{1,0:T(8,128)(2,1)S(1)} %collective-permute-done.1.o_other, ...), custom_call_target="tpu_custom_call" | custom-call | flops 1048576 | bytes 16384 | tf_op jit(solution)/shard_map/attend/pallas_call | solution.py:194
  89.6 0.3 collective-permute-done.22.refs_3_
  90.0 1.2 collective-permute-start.27
  91.3 0.5 collective-permute-start.34
  91.8 1.0 collective-permute-done.28.refs_7_
  92.8 6.1 %expert_chunk.6 = (bf16[64,4096]{1,0:T(8,128)(2,1)S(1)}, bf16[64,4096]{1,0:T(8,128)(2,1)S(1)}, bf16[128,4096]{1,0:T(8,128)(2,1)S(1)}) custom-call(bf16[32,4224]{1,0:T(8,128)(2,1)} %collective-permute-done.7.refs_0_, bf16[32,4224]{1,0:T(8,128)(2,1)S(1)} %collective-permute-done.8.refs_0_.refs_1_, bf16[32,4224]{1,0:T(8,128)(2,1)S(1)} %collective-permute-done.9.refs_1_.refs_2_, ...), custom_call_target="tpu_custom_call" | custom-call | flops 1048576 | bytes 16384 | tf_op jit(solution)/shard_map/expert_chunk/pallas_call | solution.py:298
  98.9 0.4 collective-permute-done.27
  99.4 1.2 collective-permute-start.31
  100.7 1.2 collective-permute-done.32
  102.0 0.7 collective-permute-start.29
  102.8 8.2 %collective-permute-done.29 = bf16[32,4096]{1,0:T(8,128)(2,1)S(1)} collective-permute-done((bf16[32,4096]{1,0:T(8,128)(2,1)S(1)}, bf16[32,4096]{1,0:T(8,128)(2,1)S(1)}, u32[]{:S(2)}, u32[]{:S(2)}) %collective-permute-start.29) | collective-permute-done | bytes 262176 | tf_op jit(solution)/shard_map/ppermute | solution.py:344
  111.0 1.1 collective-permute-start.33
  112.3 5.6 %expert_chunk.7 = (bf16[64,4096]{1,0:T(8,128)(2,1)S(1)}, bf16[64,4096]{1,0:T(8,128)(2,1)S(1)}, bf16[128,4096]{1,0:T(8,128)(2,1)S(1)}) custom-call(bf16[64,4224]{1,0:T(8,128)(2,1)S(1)} %copy-done.6, bf16[64,4224]{1,0:T(8,128)(2,1)S(1)} %collective-permute-done.10.refs_12_.refs_1_, bf16[64,4224]{1,0:T(8,128)(2,1)S(1)} %collective-permute-done.11.refs_2_, ...), custom_call_target="tpu_custom_call" | custom-call | flops 1048576 | bytes 16384 | tf_op jit(solution)/shard_map/expert_chunk/pallas_call | solution.py:298
  117.9 2.3 %collective-permute-done.33 = bf16[64,4096]{1,0:T(8,128)(2,1)S(1)} collective-permute-done((bf16[64,4096]{1,0:T(8,128)(2,1)S(1)}, bf16[64,4096]{1,0:T(8,128)(2,1)S(1)}, u32[]{:S(2)}, u32[]{:S(2)}) %collective-permute-start.33) | collective-permute-done | bytes 524320 | tf_op jit(solution)/shard_map/ppermute | solution.py:344
  120.2 3.0 %collective-permute-start.30 = (bf16[32,4096]{1,0:T(8,128)(2,1)S(1)}, bf16[32,4096]{1,0:T(8,128)(2,1)S(1)}, u32[]{:S(2)}, u32[]{:S(2)}) collective-permute-start(bf16[32,4096]{1,0:T(8,128)(2,1)S(1)} %add_convert_fusion.10.refs_13_), channel_id=1, source_target_pairs={{0,16},{1,17},{2,18},{3,19},{4,20},{5,21},{6,22},{7,23},{8,24},{9,... | collective-permute-start | bytes 786440 | tf_op jit(solution)/shard_map/ppermute | solution.py:344
  123.3 1.0 collective-permute-start.39
  124.4 1.2 collective-permute-start.37
  125.6 9.8 %collective-permute-done.39 = bf16[64,4096]{1,0:T(8,128)(2,1)S(1)} collective-permute-done((bf16[64,4096]{1,0:T(8,128)(2,1)S(1)}, bf16[64,4096]{1,0:T(8,128)(2,1)S(1)}, u32[]{:S(2)}, u32[]{:S(2)}) %collective-permute-start.39) | collective-permute-done | bytes 524320 | tf_op jit(solution)/shard_map/ppermute | solution.py:344
  135.5 1.1 collective-permute-start.41
  136.7 0.1 add_convert_fusion.8.refs_0_
  136.8 2.1 %collective-permute-start.43 = (bf16[32,4096]{1,0:T(8,128)(2,1)S(1)}, bf16[32,4096]{1,0:T(8,128)(2,1)S(1)}, u32[]{:S(2)}, u32[]{:S(2)}) collective-permute-start(bf16[32,4096]{1,0:T(8,128)(2,1)S(1)} %add_convert_fusion.8.refs_0_), channel_id=1, source_target_pairs={{0,24},{1,25},{2,26},{3,27},{4,28},{5,29},{6,30},{7,31},{8,16},{9,... | collective-permute-start | bytes 786440 | tf_op jit(solution)/shard_map/ppermute | solution.py:344
  138.9 4.5 %attend.7.refs_5_ = bf16[32,4096]{1,0:T(8,128)(2,1)S(1)} custom-call(s32[4]{0:T(128)S(1)} %copy-done.8, bf16[64,8192]{1,0:T(8,128)(2,1)S(1)} %reshape.12.q_mine, bf16[64,8192]{1,0:T(8,128)(2,1)} %collective-permute-done.q_other, bf16[64,1152]{1,0:T(8,128)(2,1)S(1)} %reshape.11.o_mine, bf16[64,1152]{1,0:T(8,128)(2,1)S(1)} %collective-permute-done.1.o_other, ...), custom_call_target="tpu_custom_call" | custom-call | flops 1048576 | bytes 16384 | tf_op jit(solution)/shard_map/attend/pallas_call | solution.py:194
  143.5 0.1 add_convert_fusion.6
  143.6 1.3 collective-permute-start.42
  145.0 1.0 collective-permute-start.44
  146.0 1.6 %place_context.1 = bf16[32,2,8192]{2,1,0:T(2,128)(2,1)} custom-call(bf16[64,1152]{1,0:T(8,128)(2,1)S(1)} %reshape.11.o_mine, bf16[32,4096]{1,0:T(8,128)(2,1)S(1)} %attend.4.refs_0_, bf16[32,4096]{1,0:T(8,128)(2,1)S(1)} %attend.6.refs_12_.refs_1_, bf16[32,4096]{1,0:T(8,128)(2,1)S(1)} %collective-permute-done.34.refs_2_, ...), custom_call_target="tpu_custom_call" | custom-call | flops 1048576 | bytes 16384 | tf_op jit(solution)/shard_map/place_context/pallas_call | solution.py:244
  147.6 4.8 %collective-permute-done.42 = bf16[32,4096]{1,0:T(8,128)(2,1)S(1)} collective-permute-done((bf16[32,4096]{1,0:T(8,128)(2,1)S(1)}, bf16[32,4096]{1,0:T(8,128)(2,1)S(1)}, u32[]{:S(2)}, u32[]{:S(2)}) %collective-permute-start.42) | collective-permute-done | bytes 262176 | tf_op jit(solution)/shard_map/ppermute | solution.py:344
  152.4 0.9 add_convert_fusion.4
  (99 shorter events, 1.8 us)
Async XLA Ops:
  0.6 2.0 %copy-start.9 = (bf16[32,2,8192]{2,1,0:T(2,128)(2,1)S(1)}, bf16[32,2,8192]{2,1,0:T(2,128)(2,1)}, u32[]{:S(2)}) copy-start(bf16[32,2,8192]{2,1,0:T(2,128)(2,1)} %param.12) | copy-start | bytes 3145732
  0.6 11.2 %copy-start.14 = (s32[32]{0:T(128)S(1)}, s32[32]{0:T(128)}, u32[]{:S(2)}) copy-start(s32[32]{0:T(128)} %param.16) | copy-start | bytes 388
  0.7 11.3 %copy-start.13 = (bf16[32,2,1024]{2,1,0:T(2,128)(2,1)S(1)}, bf16[32,2,1024]{2,1,0:T(2,128)(2,1)}, u32[]{:S(2)}) copy-start(bf16[32,2,1024]{2,1,0:T(2,128)(2,1)} %param.13) | copy-start | bytes 393220
  0.7 42.9 %copy-start.8 = (s32[4]{0:T(128)S(1)}, s32[4]{0:T(128)}, u32[]{:S(2)}) copy-start(s32[4]{0:T(128)} %lens_ref.7) | copy-start | bytes 52
  3.1 39.6 %collective-permute-start = (bf16[64,8192]{1,0:T(8,128)(2,1)S(1)}, bf16[64,8192]{1,0:T(8,128)(2,1)}, u32[]{:S(2)}, u32[]{:S(2)}) collective-permute-start(bf16[64,8192]{1,0:T(8,128)(2,1)S(1)} %reshape.12.q_mine), channel_id=1, source_target_pairs={{0,1},{1,0},{2,3},{3,2},{4,5},{5,4},{6,7},{7,6},{8,9},{9,8},{10,11... | collective-permute-start | bytes 3145736 | tf_op jit(solution)/shard_map/ppermute | solution.py:356
  3.6 17.0 %collective-permute-start.2 = (bf16[32,4224]{1,0:T(8,128)(2,1)}, bf16[32,4224]{1,0:T(8,128)(2,1)}, u32[]{:S(2)}, u32[]{:S(2)}) collective-permute-start(bf16[32,4224]{1,0:T(8,128)(2,1)} %norm_message.1.refs_0_), channel_id=1, source_target_pairs={{0,16},{1,17},{2,18},{3,19},{4,20},{5,21},{6,22},{7,23},{8,24},{9,... | collective-permute-start | bytes 811016 | tf_op jit(solution)/shard_map/ppermute | solution.py:344
  7.3 14.9 %collective-permute-start.3 = (bf16[32,4224]{1,0:T(8,128)(2,1)}, bf16[32,4224]{1,0:T(8,128)(2,1)S(1)}, u32[]{:S(2)}, u32[]{:S(2)}) collective-permute-start(bf16[32,4224]{1,0:T(8,128)(2,1)} %norm_message.1.refs_0_), channel_id=1, source_target_pairs={{0,8},{1,9},{2,10},{3,11},{4,12},{5,13},{6,14},{7,15},{8,0},{9,1},... | collective-permute-start | bytes 811016 | tf_op jit(solution)/shard_map/ppermute | solution.py:344
  8.9 11.7 %collective-permute-start.4 = (bf16[32,4224]{1,0:T(8,128)(2,1)}, bf16[32,4224]{1,0:T(8,128)(2,1)}, u32[]{:S(2)}, u32[]{:S(2)}) collective-permute-start(bf16[32,4224]{1,0:T(8,128)(2,1)} %norm_message.1.refs_0_), channel_id=1, source_target_pairs={{0,2},{1,5},{2,0},{3,7},{4,6},{5,1},{6,4},{7,3},{8,10},{9,13},{10,... | collective-permute-start | bytes 811016 | tf_op jit(solution)/shard_map/ppermute | solution.py:344
  10.4 30.8 %collective-permute-start.5 = (bf16[32,4224]{1,0:T(8,128)(2,1)}, bf16[32,4224]{1,0:T(8,128)(2,1)}, u32[]{:S(2)}, u32[]{:S(2)}) collective-permute-start(bf16[32,4224]{1,0:T(8,128)(2,1)} %norm_message.1.refs_0_), channel_id=1, source_target_pairs={{0,4},{1,3},{2,6},{3,1},{4,0},{5,7},{6,2},{7,5},{8,12},{9,11},{10,... | collective-permute-start | bytes 811016 | tf_op jit(solution)/shard_map/ppermute | solution.py:344
  20.6 20.4 %collective-permute-start.1 = (bf16[64,1152]{1,0:T(8,128)(2,1)S(1)}, bf16[64,1152]{1,0:T(8,128)(2,1)S(1)}, u32[]{:S(2)}, u32[]{:S(2)}) collective-permute-start(bf16[64,1152]{1,0:T(8,128)(2,1)S(1)} %reshape.11.o_mine), channel_id=1, source_target_pairs={{0,1},{1,0},{2,3},{3,2},{4,5},{5,4},{6,7},{7,6},{8,9},{9,8},{10,11... | collective-permute-start | bytes 442376 | tf_op jit(solution)/shard_map/ppermute | solution.py:356
  20.6 30.8 %collective-permute-start.6 = (bf16[32,4224]{1,0:T(8,128)(2,1)}, bf16[32,4224]{1,0:T(8,128)(2,1)}, u32[]{:S(2)}, u32[]{:S(2)}) collective-permute-start(bf16[32,4224]{1,0:T(8,128)(2,1)} %collective-permute-done.4.refs_1_), channel_id=1, source_target_pairs={{0,4},{1,3},{2,6},{3,1},{4,0},{5,7},{6,2},{7,5},{8,12},{9,11},{10,... | collective-permute-start | bytes 811016 | tf_op jit(solution)/shard_map/ppermute | solution.py:344
  22.9 28.6 %collective-permute-start.7 = (bf16[32,4224]{1,0:T(8,128)(2,1)}, bf16[32,4224]{1,0:T(8,128)(2,1)}, u32[]{:S(2)}, u32[]{:S(2)}) collective-permute-start(bf16[32,4224]{1,0:T(8,128)(2,1)} %collective-permute-done.2.top), channel_id=1, source_target_pairs={{0,8},{1,9},{2,10},{3,11},{4,12},{5,13},{6,14},{7,15},{8,0},{9,1},... | collective-permute-start | bytes 811016 | tf_op jit(solution)/shard_map/ppermute | solution.py:344
  23.5 37.5 %slice-start = ((s8[6291456]{0:T(1024)(128)(4,1)}), s8[2097152]{0:T(1024)(128)(4,1)S(1)}, s32[]{:S(2)}) async-start(s8[6291456]{0:T(1024)(128)(4,1)} %bitcast.5), calls=%async_computation | async-start | bytes 4194304
  41.0 20.0 %slice-start.1 = ((s8[6291456]{0:T(1024)(128)(4,1)}), s8[4194304]{0:T(1024)(128)(4,1)S(1)}, s32[]{:S(2)}) async-start(s8[6291456]{0:T(1024)(128)(4,1)} %bitcast.5), calls=%async_computation.1 | async-start | bytes 8388608
  41.0 10.9 %collective-permute-start.12 = (bf16[32,4224]{1,0:T(8,128)(2,1)}, bf16[32,4224]{1,0:T(8,128)(2,1)S(1)}, u32[]{:S(2)}, u32[]{:S(2)}) collective-permute-start(bf16[32,4224]{1,0:T(8,128)(2,1)} %norm_message.1.refs_0_), channel_id=1, source_target_pairs={{0,1},{1,0},{2,3},{3,2},{4,5},{5,4},{6,7},{7,6},{8,9},{9,8},{10,11... | collective-permute-start | bytes 811016 | tf_op jit(solution)/shard_map/ppermute | solution.py:356
  41.1 18.2 %collective-permute-start.10 = (bf16[64,4224]{1,0:T(8,128)(2,1)}, bf16[64,4224]{1,0:T(8,128)(2,1)S(1)}, u32[]{:S(2)}, u32[]{:S(2)}) collective-permute-start(bf16[64,4224]{1,0:T(8,128)(2,1)} %stack.1.refs_0_), channel_id=1, source_target_pairs={{0,2},{1,5},{2,0},{3,7},{4,6},{5,1},{6,4},{7,3},{8,10},{9,13},{10,... | collective-permute-start | bytes 1622024 | tf_op jit(solution)/shard_map/ppermute | solution.py:344
  42.7 16.6 %collective-permute-start.11 = (bf16[64,4224]{1,0:T(8,128)(2,1)}, bf16[64,4224]{1,0:T(8,128)(2,1)S(1)}, u32[]{:S(2)}, u32[]{:S(2)}) collective-permute-start(bf16[64,4224]{1,0:T(8,128)(2,1)} %stack.1.refs_0_), channel_id=1, source_target_pairs={{0,4},{1,3},{2,6},{3,1},{4,0},{5,7},{6,2},{7,5},{8,12},{9,11},{10,... | collective-permute-start | bytes 1622024 | tf_op jit(solution)/shard_map/ppermute | solution.py:344
  43.6 2.2 %copy-start.2 = (bf16[2,1024,1024]{2,1,0:T(8,128)(2,1)S(1)}, bf16[2,1024,1024]{2,1,0:T(8,128)(2,1)}, u32[]{:S(2)}) copy-start(bf16[2,1024,1024]{2,1,0:T(8,128)(2,1)} %cache.7) | copy-start | bytes 12582916
  46.8 12.0 %copy-start.6 = (bf16[64,4224]{1,0:T(8,128)(2,1)S(1)}, bf16[64,4224]{1,0:T(8,128)(2,1)}, u32[]{:S(2)}) copy-start(bf16[64,4224]{1,0:T(8,128)(2,1)} %stack.1.refs_0_) | copy-start | bytes 1622020
  46.8 14.2 %copy-start.7 = (bf16[32,4224]{1,0:T(8,128)(2,1)S(1)}, bf16[32,4224]{1,0:T(8,128)(2,1)}, u32[]{:S(2)}) copy-start(bf16[32,4224]{1,0:T(8,128)(2,1)} %norm_message.1.refs_0_) | copy-start | bytes 811012
  51.4 7.4 %collective-permute-start.13 = (bf16[32,4224]{1,0:T(8,128)(2,1)}, bf16[32,4224]{1,0:T(8,128)(2,1)S(1)}, u32[]{:S(2)}, u32[]{:S(2)}) collective-permute-start(bf16[32,4224]{1,0:T(8,128)(2,1)} %collective-permute-done.4.refs_1_), channel_id=1, source_target_pairs={{0,1},{1,0},{2,3},{3,2},{4,5},{5,4},{6,7},{7,6},{8,9},{9,8},{10,11... | collective-permute-start | bytes 811016 | tf_op jit(solution)/shard_map/ppermute | solution.py:356
  51.5 7.8 %collective-permute-start.14 = (bf16[32,4224]{1,0:T(8,128)(2,1)}, bf16[32,4224]{1,0:T(8,128)(2,1)S(1)}, u32[]{:S(2)}, u32[]{:S(2)}) collective-permute-start(bf16[32,4224]{1,0:T(8,128)(2,1)} %collective-permute-done.5.refs_2_), channel_id=1, source_target_pairs={{0,1},{1,0},{2,3},{3,2},{4,5},{5,4},{6,7},{7,6},{8,9},{9,8},{10,11... | collective-permute-start | bytes 811016 | tf_op jit(solution)/shard_map/ppermute | solution.py:356
  52.0 7.3 %collective-permute-start.15 = (bf16[32,4224]{1,0:T(8,128)(2,1)}, bf16[32,4224]{1,0:T(8,128)(2,1)S(1)}, u32[]{:S(2)}, u32[]{:S(2)}) collective-permute-start(bf16[32,4224]{1,0:T(8,128)(2,1)} %collective-permute-done.6.refs_3_), channel_id=1, source_target_pairs={{0,1},{1,0},{2,3},{3,2},{4,5},{5,4},{6,7},{7,6},{8,9},{9,8},{10,11... | collective-permute-start | bytes 811016 | tf_op jit(solution)/shard_map/ppermute | solution.py:356
  52.1 2.2 %copy-start.3 = (bf16[2,1024,1024]{2,1,0:T(8,128)(2,1)S(1)}, bf16[2,1024,1024]{2,1,0:T(8,128)(2,1)}, u32[]{:S(2)}) copy-start(bf16[2,1024,1024]{2,1,0:T(8,128)(2,1)} %cache.7) | copy-start | bytes 12582916
  58.8 14.1 %collective-permute-start.17 = (bf16[64,4224]{1,0:T(8,128)(2,1)S(1)}, bf16[64,4224]{1,0:T(8,128)(2,1)S(1)}, u32[]{:S(2)}, u32[]{:S(2)}) collective-permute-start(bf16[64,4224]{1,0:T(8,128)(2,1)S(1)} %copy-done.6), channel_id=1, source_target_pairs={{0,1},{1,0},{2,3},{3,2},{4,5},{5,4},{6,7},{7,6},{8,9},{9,8},{10,11... | collective-permute-start | bytes 1622024 | tf_op jit(solution)/shard_map/ppermute | solution.py:356
  59.3 13.6 %collective-permute-start.16 = (bf16[64,4224]{1,0:T(8,128)(2,1)S(1)}, bf16[64,4224]{1,0:T(8,128)(2,1)S(1)}, u32[]{:S(2)}, u32[]{:S(2)}) collective-permute-start(bf16[64,4224]{1,0:T(8,128)(2,1)S(1)} %collective-permute-done.10.refs_12_.refs_1_), channel_id=1, source_target_pairs={{0,4},{1,3},{2,6},{3,1},{4,0},{5,7},{6,2},{7,5},{8,12},{9,11},{10,... | collective-permute-start | bytes 1622024 | tf_op jit(solution)/shard_map/ppermute | solution.py:344
  60.5 12.4 %collective-permute-start.18 = (bf16[64,4224]{1,0:T(8,128)(2,1)S(1)}, bf16[64,4224]{1,0:T(8,128)(2,1)S(1)}, u32[]{:S(2)}, u32[]{:S(2)}) collective-permute-start(bf16[64,4224]{1,0:T(8,128)(2,1)S(1)} %collective-permute-done.10.refs_12_.refs_1_), channel_id=1, source_target_pairs={{0,1},{1,0},{2,3},{3,2},{4,5},{5,4},{6,7},{7,6},{8,9},{9,8},{10,11... | collective-permute-start | bytes 1622024 | tf_op jit(solution)/shard_map/ppermute | solution.py:356
  60.5 12.4 %collective-permute-start.19 = (bf16[64,4224]{1,0:T(8,128)(2,1)S(1)}, bf16[64,4224]{1,0:T(8,128)(2,1)S(1)}, u32[]{:S(2)}, u32[]{:S(2)}) collective-permute-start(bf16[64,4224]{1,0:T(8,128)(2,1)S(1)} %collective-permute-done.11.refs_2_), channel_id=1, source_target_pairs={{0,1},{1,0},{2,3},{3,2},{4,5},{5,4},{6,7},{7,6},{8,9},{9,8},{10,11... | collective-permute-start | bytes 1622024 | tf_op jit(solution)/shard_map/ppermute | solution.py:356
  61.0 2.8 %copy-start = (bf16[1,4096,768]{2,1,0:T(8,128)(2,1)S(1)}, bf16[1,4096,768]{2,1,0:T(8,128)(2,1)}, u32[]{:S(2)}) copy-start(bf16[1,4096,768]{2,1,0:T(8,128)(2,1)} %param.22) | copy-start | bytes 18874372
  63.8 2.8 %copy-start.1 = (bf16[1,768,4096]{2,1,0:T(8,128)(2,1)S(1)}, bf16[1,768,4096]{2,1,0:T(8,128)(2,1)}, u32[]{:S(2)}) copy-start(bf16[1,768,4096]{2,1,0:T(8,128)(2,1)} %param.23) | copy-start | bytes 18874372
  72.9 19.9 %slice-start.2 = ((s8[6291456]{0:T(1024)(128)(4,1)}), s8[4194304]{0:T(1024)(128)(4,1)S(1)}, s32[]{:S(2)}) async-start(s8[6291456]{0:T(1024)(128)(4,1)} %bitcast.13), calls=%async_computation.2 | async-start | bytes 8388608
  72.9 19.9 %slice-start.4 = ((s8[6291456]{0:T(1024)(128)(4,1)}), s8[4194304]{0:T(1024)(128)(4,1)S(1)}, s32[]{:S(2)}) async-start(s8[6291456]{0:T(1024)(128)(4,1)} %bitcast.19), calls=%async_computation.4 | async-start | bytes 8388608
  72.9 12.1 %copy-start.4 = (bf16[2,1024,1024]{2,1,0:T(8,128)(2,1)S(1)}, bf16[2,1024,1024]{2,1,0:T(8,128)(2,1)}, u32[]{:S(2)}) copy-start(bf16[2,1024,1024]{2,1,0:T(8,128)(2,1)} %cache.7) | copy-start | bytes 12582916
  73.0 19.8 %slice-start.3 = ((s8[6291456]{0:T(1024)(128)(4,1)}), s8[2097152]{0:T(1024)(128)(4,1)S(1)}, s32[]{:S(2)}) async-start(s8[6291456]{0:T(1024)(128)(4,1)} %bitcast.13), calls=%async_computation.3 | async-start | bytes 4194304
  73.0 19.8 %slice-start.5 = ((s8[6291456]{0:T(1024)(128)(4,1)}), s8[2097152]{0:T(1024)(128)(4,1)S(1)}, s32[]{:S(2)}) async-start(s8[6291456]{0:T(1024)(128)(4,1)} %bitcast.19), calls=%async_computation.5 | async-start | bytes 4194304
  73.0 9.9 %collective-permute-start.20 = (bf16[128,4096]{1,0:T(8,128)(2,1)S(1)}, bf16[128,4096]{1,0:T(8,128)(2,1)S(1)}, u32[]{:S(2)}, u32[]{:S(2)}) collective-permute-start(bf16[128,4096]{1,0:T(8,128)(2,1)S(1)} %get-tuple-element.87), channel_id=1, source_target_pairs={{0,1},{1,0},{2,3},{3,2},{4,5},{5,4},{6,7},{7,6},{8,9},{9,8},{10,11... | collective-permute-start | bytes 3145736 | tf_op jit(solution)/shard_map/ppermute | solution.py:356
  73.1 3.4 %collective-permute-start.21 = (bf16[64,4224]{1,0:T(8,128)(2,1)S(1)}, bf16[64,4224]{1,0:T(8,128)(2,1)S(1)}, u32[]{:S(2)}, u32[]{:S(2)}) collective-permute-start(bf16[64,4224]{1,0:T(8,128)(2,1)S(1)} %collective-permute-done.16.refs_3_), channel_id=1, source_target_pairs={{0,1},{1,0},{2,3},{3,2},{4,5},{5,4},{6,7},{7,6},{8,9},{9,8},{10,11... | collective-permute-start | bytes 1622024 | tf_op jit(solution)/shard_map/ppermute | solution.py:356
  73.6 9.3 %collective-permute-start.8 = (bf16[32,4224]{1,0:T(8,128)(2,1)}, bf16[32,4224]{1,0:T(8,128)(2,1)S(1)}, u32[]{:S(2)}, u32[]{:S(2)}) collective-permute-start(bf16[32,4224]{1,0:T(8,128)(2,1)} %collective-permute-done.7.refs_0_), channel_id=1, source_target_pairs={{0,2},{1,5},{2,0},{3,7},{4,6},{5,1},{6,4},{7,3},{8,10},{9,13},{10,... | collective-permute-start | bytes 811016 | tf_op jit(solution)/shard_map/ppermute | solution.py:344
  74.1 8.7 %collective-permute-start.9 = (bf16[32,4224]{1,0:T(8,128)(2,1)}, bf16[32,4224]{1,0:T(8,128)(2,1)S(1)}, u32[]{:S(2)}, u32[]{:S(2)}) collective-permute-start(bf16[32,4224]{1,0:T(8,128)(2,1)} %collective-permute-done.7.refs_0_), channel_id=1, source_target_pairs={{0,4},{1,3},{2,6},{3,1},{4,0},{5,7},{6,2},{7,5},{8,12},{9,11},{10,... | collective-permute-start | bytes 811016 | tf_op jit(solution)/shard_map/ppermute | solution.py:344
  82.8 1.7 %copy-start.10 = (bf16[128,4096]{1,0:T(8,128)(2,1)}, bf16[128,4096]{1,0:T(8,128)(2,1)S(1)}, u32[]{:S(2)}) copy-start(bf16[128,4096]{1,0:T(8,128)(2,1)S(1)} %collective-permute-done.20) | copy-start | bytes 3145732
  82.8 7.0 %collective-permute-start.23 = (bf16[128,4096]{1,0:T(8,128)(2,1)S(1)}, bf16[128,4096]{1,0:T(8,128)(2,1)S(1)}, u32[]{:S(2)}, u32[]{:S(2)}) collective-permute-start(bf16[128,4096]{1,0:T(8,128)(2,1)S(1)} %get-tuple-element.99), channel_id=1, source_target_pairs={{0,1},{1,0},{2,3},{3,2},{4,5},{5,4},{6,7},{7,6},{8,9},{9,8},{10,11... | collective-permute-start | bytes 3145736 | tf_op jit(solution)/shard_map/ppermute | solution.py:356
  82.9 6.7 %collective-permute-start.24 = (bf16[32,4224]{1,0:T(8,128)(2,1)}, bf16[32,4224]{1,0:T(8,128)(2,1)S(1)}, u32[]{:S(2)}, u32[]{:S(2)}) collective-permute-start(bf16[32,4224]{1,0:T(8,128)(2,1)} %collective-permute-done.7.refs_0_), channel_id=1, source_target_pairs={{0,1},{1,0},{2,3},{3,2},{4,5},{5,4},{6,7},{7,6},{8,9},{9,8},{10,11... | collective-permute-start | bytes 811016 | tf_op jit(solution)/shard_map/ppermute | solution.py:356
  83.4 6.5 %collective-permute-start.22 = (bf16[32,4224]{1,0:T(8,128)(2,1)S(1)}, bf16[32,4224]{1,0:T(8,128)(2,1)S(1)}, u32[]{:S(2)}, u32[]{:S(2)}) collective-permute-start(bf16[32,4224]{1,0:T(8,128)(2,1)S(1)} %collective-permute-done.8.refs_0_.refs_1_), channel_id=1, source_target_pairs={{0,4},{1,3},{2,6},{3,1},{4,0},{5,7},{6,2},{7,5},{8,12},{9,11},{10,... | collective-permute-start | bytes 811016 | tf_op jit(solution)/shard_map/ppermute | solution.py:344
  84.6 5.3 %collective-permute-start.25 = (bf16[32,4224]{1,0:T(8,128)(2,1)S(1)}, bf16[32,4224]{1,0:T(8,128)(2,1)S(1)}, u32[]{:S(2)}, u32[]{:S(2)}) collective-permute-start(bf16[32,4224]{1,0:T(8,128)(2,1)S(1)} %collective-permute-done.8.refs_0_.refs_1_), channel_id=1, source_target_pairs={{0,1},{1,0},{2,3},{3,2},{4,5},{5,4},{6,7},{7,6},{8,9},{9,8},{10,11... | collective-permute-start | bytes 811016 | tf_op jit(solution)/shard_map/ppermute | solution.py:356
  84.6 5.3 %collective-permute-start.26 = (bf16[32,4224]{1,0:T(8,128)(2,1)S(1)}, bf16[32,4224]{1,0:T(8,128)(2,1)S(1)}, u32[]{:S(2)}, u32[]{:S(2)}) collective-permute-start(bf16[32,4224]{1,0:T(8,128)(2,1)S(1)} %collective-permute-done.9.refs_1_.refs_2_), channel_id=1, source_target_pairs={{0,1},{1,0},{2,3},{3,2},{4,5},{5,4},{6,7},{7,6},{8,9},{9,8},{10,11... | collective-permute-start | bytes 811016 | tf_op jit(solution)/shard_map/ppermute | solution.py:356
  90.0 9.3 %copy-start.11 = (bf16[128,4096]{1,0:T(8,128)(2,1)S(1)}, bf16[128,4096]{1,0:T(8,128)(2,1)}, u32[]{:S(2)}) copy-start(bf16[128,4096]{1,0:T(8,128)(2,1)} %copy-done.10) | copy-start | bytes 3145732
  90.0 9.2 %collective-permute-start.27 = (bf16[64,4096]{1,0:T(8,128)(2,1)S(1)}, bf16[64,4096]{1,0:T(8,128)(2,1)S(1)}, u32[]{:S(2)}, u32[]{:S(2)}) collective-permute-start(bf16[64,4096]{1,0:T(8,128)(2,1)S(1)} %add_convert_fusion.3.refs_11_), channel_id=1, source_target_pairs={{0,4},{1,3},{2,6},{3,1},{4,0},{5,7},{6,2},{7,5},{8,12},{9,11},{10,... | collective-permute-start | bytes 1572872 | tf_op jit(solution)/shard_map/ppermute | solution.py:344
  91.2 1.5 %collective-permute-start.28 = (bf16[32,4224]{1,0:T(8,128)(2,1)S(1)}, bf16[32,4224]{1,0:T(8,128)(2,1)S(1)}, u32[]{:S(2)}, u32[]{:S(2)}) collective-permute-start(bf16[32,4224]{1,0:T(8,128)(2,1)S(1)} %collective-permute-done.22.refs_3_), channel_id=1, source_target_pairs={{0,1},{1,0},{2,3},{3,2},{4,5},{5,4},{6,7},{7,6},{8,9},{9,8},{10,11... | collective-permute-start | bytes 811016 | tf_op jit(solution)/shard_map/ppermute | solution.py:356
  91.3 26.6 %collective-permute-start.34 = (bf16[32,4096]{1,0:T(8,128)(2,1)S(1)}, bf16[32,4096]{1,0:T(8,128)(2,1)S(1)}, u32[]{:S(2)}, u32[]{:S(2)}) collective-permute-start(bf16[32,4096]{1,0:T(8,128)(2,1)S(1)} %attend.4.refs_0_), channel_id=1, source_target_pairs={{0,1},{1,0},{2,3},{3,2},{4,5},{5,4},{6,7},{7,6},{8,9},{9,8},{10,11... | collective-permute-start | bytes 786440 | tf_op jit(solution)/shard_map/ppermute | solution.py:356
  91.8 26.1 %collective-permute-start.35 = (bf16[32,4096]{1,0:T(8,128)(2,1)S(1)}, bf16[32,4096]{1,0:T(8,128)(2,1)S(1)}, u32[]{:S(2)}, u32[]{:S(2)}) collective-permute-start(bf16[32,4096]{1,0:T(8,128)(2,1)S(1)} %attend.5.refs_11_.refs_4_), channel_id=1, source_target_pairs={{0,1},{1,0},{2,3},{3,2},{4,5},{5,4},{6,7},{7,6},{8,9},{9,8},{10,11... | collective-permute-start | bytes 786440 | tf_op jit(solution)/shard_map/ppermute | solution.py:356
  99.3 2.7 %collective-permute-start.32 = (bf16[128,4096]{1,0:T(8,128)(2,1)S(1)}, bf16[128,4096]{1,0:T(8,128)(2,1)S(1)}, u32[]{:S(2)}, u32[]{:S(2)}) collective-permute-start(bf16[128,4096]{1,0:T(8,128)(2,1)S(1)} %get-tuple-element.115), channel_id=1, source_target_pairs={{0,1},{1,0},{2,3},{3,2},{4,5},{5,4},{6,7},{7,6},{8,9},{9,8},{10,11... | collective-permute-start | bytes 3145736 | tf_op jit(solution)/shard_map/ppermute | solution.py:356
  99.4 18.5 %collective-permute-start.31 = (bf16[64,4096]{1,0:T(8,128)(2,1)S(1)}, bf16[64,4096]{1,0:T(8,128)(2,1)S(1)}, u32[]{:S(2)}, u32[]{:S(2)}) collective-permute-start(bf16[64,4096]{1,0:T(8,128)(2,1)S(1)} %add_convert_fusion.2.refs_12_), channel_id=1, source_target_pairs={{0,4},{1,3},{2,6},{3,1},{4,0},{5,7},{6,2},{7,5},{8,12},{9,11},{10,... | collective-permute-start | bytes 1572872 | tf_op jit(solution)/shard_map/ppermute | solution.py:344
  100.6 17.3 %collective-permute-start.36 = (bf16[32,4096]{1,0:T(8,128)(2,1)S(1)}, bf16[32,4096]{1,0:T(8,128)(2,1)S(1)}, u32[]{:S(2)}, u32[]{:S(2)}) collective-permute-start(bf16[32,4096]{1,0:T(8,128)(2,1)S(1)} %attend.6.refs_12_.refs_1_), channel_id=1, source_target_pairs={{0,1},{1,0},{2,3},{3,2},{4,5},{5,4},{6,7},{7,6},{8,9},{9,8},{10,11... | collective-permute-start | bytes 786440 | tf_op jit(solution)/shard_map/ppermute | solution.py:356
  102.0 9.1 %collective-permute-start.29 = (bf16[32,4096]{1,0:T(8,128)(2,1)S(1)}, bf16[32,4096]{1,0:T(8,128)(2,1)S(1)}, u32[]{:S(2)}, u32[]{:S(2)}) collective-permute-start(bf16[32,4096]{1,0:T(8,128)(2,1)S(1)} %add_convert_fusion.11), channel_id=1, source_target_pairs={{0,2},{1,5},{2,0},{3,7},{4,6},{5,1},{6,4},{7,3},{8,10},{9,13},{10,... | collective-permute-start | bytes 786440 | tf_op jit(solution)/shard_map/ppermute | solution.py:344
  111.0 9.2 %collective-permute-start.33 = (bf16[64,4096]{1,0:T(8,128)(2,1)S(1)}, bf16[64,4096]{1,0:T(8,128)(2,1)S(1)}, u32[]{:S(2)}, u32[]{:S(2)}) collective-permute-start(bf16[64,4096]{1,0:T(8,128)(2,1)S(1)} %add_convert_fusion.1.refs_11_), channel_id=1, source_target_pairs={{0,4},{1,3},{2,6},{3,1},{4,0},{5,7},{6,2},{7,5},{8,12},{9,11},{10,... | collective-permute-start | bytes 1572872 | tf_op jit(solution)/shard_map/ppermute | solution.py:344
  120.2 3.0 %collective-permute-start.38 = (bf16[128,4096]{1,0:T(8,128)(2,1)S(1)}, bf16[128,4096]{1,0:T(8,128)(2,1)S(1)}, u32[]{:S(2)}, u32[]{:S(2)}) collective-permute-start(bf16[128,4096]{1,0:T(8,128)(2,1)S(1)} %get-tuple-element.124), channel_id=1, source_target_pairs={{0,1},{1,0},{2,3},{3,2},{4,5},{5,4},{6,7},{7,6},{8,9},{9,8},{10,11... | collective-permute-start | bytes 3145736 | tf_op jit(solution)/shard_map/ppermute | solution.py:356
  120.2 25.8 %collective-permute-start.30 = (bf16[32,4096]{1,0:T(8,128)(2,1)S(1)}, bf16[32,4096]{1,0:T(8,128)(2,1)S(1)}, u32[]{:S(2)}, u32[]{:S(2)}) collective-permute-start(bf16[32,4096]{1,0:T(8,128)(2,1)S(1)} %add_convert_fusion.10.refs_13_), channel_id=1, source_target_pairs={{0,16},{1,17},{2,18},{3,19},{4,20},{5,21},{6,22},{7,23},{8,24},{9,... | collective-permute-start | bytes 786440 | tf_op jit(solution)/shard_map/ppermute | solution.py:344
  123.3 12.1 %collective-permute-start.39 = (bf16[64,4096]{1,0:T(8,128)(2,1)S(1)}, bf16[64,4096]{1,0:T(8,128)(2,1)S(1)}, u32[]{:S(2)}, u32[]{:S(2)}) collective-permute-start(bf16[64,4096]{1,0:T(8,128)(2,1)S(1)} %add_convert_fusion), channel_id=1, source_target_pairs={{0,4},{1,3},{2,6},{3,1},{4,0},{5,7},{6,2},{7,5},{8,12},{9,11},{10,... | collective-permute-start | bytes 1572872 | tf_op jit(solution)/shard_map/ppermute | solution.py:344
  124.4 12.2 %collective-permute-start.37 = (bf16[32,4096]{1,0:T(8,128)(2,1)S(1)}, bf16[32,4096]{1,0:T(8,128)(2,1)S(1)}, u32[]{:S(2)}, u32[]{:S(2)}) collective-permute-start(bf16[32,4096]{1,0:T(8,128)(2,1)S(1)} %add_convert_fusion.9), channel_id=1, source_target_pairs={{0,2},{1,5},{2,0},{3,7},{4,6},{5,1},{6,4},{7,3},{8,10},{9,13},{10,... | collective-permute-start | bytes 786440 | tf_op jit(solution)/shard_map/ppermute | solution.py:344
  135.5 7.9 %collective-permute-start.41 = (bf16[32,4096]{1,0:T(8,128)(2,1)S(1)}, bf16[32,4096]{1,0:T(8,128)(2,1)S(1)}, u32[]{:S(2)}, u32[]{:S(2)}) collective-permute-start(bf16[32,4096]{1,0:T(8,128)(2,1)S(1)} %add_convert_fusion.7.refs_1_), channel_id=1, source_target_pairs={{0,2},{1,5},{2,0},{3,7},{4,6},{5,1},{6,4},{7,3},{8,10},{9,13},{10,... | collective-permute-start | bytes 786440 | tf_op jit(solution)/shard_map/ppermute | solution.py:344
  136.8 10.8 %collective-permute-start.43 = (bf16[32,4096]{1,0:T(8,128)(2,1)S(1)}, bf16[32,4096]{1,0:T(8,128)(2,1)S(1)}, u32[]{:S(2)}, u32[]{:S(2)}) collective-permute-start(bf16[32,4096]{1,0:T(8,128)(2,1)S(1)} %add_convert_fusion.8.refs_0_), channel_id=1, source_target_pairs={{0,24},{1,25},{2,26},{3,27},{4,28},{5,29},{6,30},{7,31},{8,16},{9,... | collective-permute-start | bytes 786440 | tf_op jit(solution)/shard_map/ppermute | solution.py:344
  143.4 2.6 %collective-permute-start.40 = (bf16[32,4096]{1,0:T(8,128)(2,1)S(1)}, bf16[32,4096]{1,0:T(8,128)(2,1)S(1)}, u32[]{:S(2)}, u32[]{:S(2)}) collective-permute-start(bf16[32,4096]{1,0:T(8,128)(2,1)S(1)} %attend.7.refs_5_), channel_id=1, source_target_pairs={{0,1},{1,0},{2,3},{3,2},{4,5},{5,4},{6,7},{7,6},{8,9},{9,8},{10,11... | collective-permute-start | bytes 786440 | tf_op jit(solution)/shard_map/ppermute | solution.py:356
  143.6 8.8 %collective-permute-start.42 = (bf16[32,4096]{1,0:T(8,128)(2,1)S(1)}, bf16[32,4096]{1,0:T(8,128)(2,1)S(1)}, u32[]{:S(2)}, u32[]{:S(2)}) collective-permute-start(bf16[32,4096]{1,0:T(8,128)(2,1)S(1)} %add_convert_fusion.6), channel_id=1, source_target_pairs={{0,8},{1,9},{2,10},{3,11},{4,12},{5,13},{6,14},{7,15},{8,0},{9,1},... | collective-permute-start | bytes 786440 | tf_op jit(solution)/shard_map/ppermute | solution.py:344
  145.0 7.4 %collective-permute-start.44 = (bf16[32,4096]{1,0:T(8,128)(2,1)S(1)}, bf16[32,4096]{1,0:T(8,128)(2,1)S(1)}, u32[]{:S(2)}, u32[]{:S(2)}) collective-permute-start(bf16[32,4096]{1,0:T(8,128)(2,1)S(1)} %add_convert_fusion.5), channel_id=1, source_target_pairs={{0,2},{1,5},{2,0},{3,7},{4,6},{5,1},{6,4},{7,3},{8,10},{9,13},{10,... | collective-permute-start | bytes 786440 | tf_op jit(solution)/shard_map/ppermute | solution.py:344
  (2 other events, 1.7 us)

commit v2 on v1

--- a/solution.py
+++ b/solution.py
@@ -28,9 +28,6 @@
 
 
 SMALL = pl.CostEstimate(flops=1 << 20, bytes_accessed=1 << 14, transcendentals=0)
-
-
-LARGE = pl.CostEstimate(flops=20 << 30, bytes_accessed=1 << 20, transcendentals=0)
 
 
 def norm_kernel(hidden_ref, gain_ref, ids_ref, logits_ref, out_ref):
@@ -66,33 +63,47 @@
     return pl.pallas_call(
         norm_kernel,
         out_shape=jax.ShapeDtypeStruct((rows, width + LANES), jnp.bfloat16),
-        cost_estimate=LARGE,
+        cost_estimate=SMALL,
         name="norm_message",
     )(hidden, gain, ids.T, logits.T)
 
 
-def stack_kernel(top, bottom, out, sem):
+def stack_kernel(top, bottom, out):
     rows = top.shape[0]
-    upper = pltpu.make_async_copy(top, out.at[pl.ds(0, rows)], sem.at[0])
-    lower = pltpu.make_async_copy(bottom, out.at[pl.ds(rows, rows)], sem.at[1])
-    upper.start()
-    lower.start()
-    upper.wait()
-    lower.wait()
+    out[:rows] = top[...]
+    out[rows:] = bottom[...]
 
 
 def stack(top, bottom):
     rows, width = top.shape
-    anywhere = pl.BlockSpec(memory_space=pl.ANY)
+    whole = pl.BlockSpec(memory_space=pltpu.VMEM)
     return pl.pallas_call(
         stack_kernel,
         out_shape=jax.ShapeDtypeStruct((2 * rows, width), top.dtype),
-        in_specs=[anywhere, anywhere],
-        out_specs=anywhere,
-        scratch_shapes=[pltpu.SemaphoreType.DMA((2,))],
+        in_specs=[whole, whole],
+        out_specs=whole,
+        compiler_params=pltpu.CompilerParams(vmem_limit_bytes=8 * MIB),
         cost_estimate=SMALL,
         name="stack",
     )(top, bottom)
+
+
+def touch_kernel(lens, *refs):
+    out = refs[-1]
+    for i in range(lens.shape[0]):
+        out[i] = lens[i]
+
+
+def touch(lens, *arrays):
+    scalars = pl.BlockSpec(memory_space=pltpu.SMEM)
+    return pl.pallas_call(
+        touch_kernel,
+        out_shape=jax.ShapeDtypeStruct(lens.shape, lens.dtype),
+        in_specs=[scalars] + [pl.BlockSpec(memory_space=pl.ANY)] * len(arrays),
+        out_specs=scalars,
+        cost_estimate=SMALL,
+        name="touch",
+    )(lens, *arrays)
 
 
 def rank_rows(match, rows):
@@ -360,6 +371,8 @@
     sync = lax.optimization_barrier
     token = norm_message(hidden, norm_gain, route_ids, route_logits)
     token, queries, new_kv = sync((token, queries, new_kv))
+    prompt_lens = touch(prompt_lens, token, prompt_kv, down)
+    new_kv, prompt_lens = sync((new_kv, prompt_lens))
     marks = jnp.broadcast_to(sample_prompt.astype(jnp.bfloat16)[:, None, None], (count, STEPS, LANES))
     q_mine = queries.reshape(rows, q_width)
     own_mine = jnp.concatenate([new_kv, marks], axis=2).reshape(rows, -1)
@@ -399,6 +412,7 @@
     level_2, level_1 = far(token, 2), far(token, 1)
     first_0, cross_0 = near(token), cross(token)
     third_0 = cross(first_0)
+    level_2, level_1, prompt_lens = sync((level_2, level_1, prompt_lens))
     pair = stack(level_2, level_1)
     level_3 = far(level_2, 1)
     context_0a = attend_half(0, 0, pair, first_0, cross_0)
@@ -422,27 +436,26 @@
     back_2 = beside(result_2[2])
     third_3 = cross(first_3)
     fans_3 = [beside(value) for value in (level_3, first_3, cross_3)]
-    context_1a = attend_half(1, 0, first_3, cross_3)
+    there_0 = sum_cores(result_0, back_0)
+    context_1a = attend_half(1, 0, first_3, cross_3, there_0)
     context_1a, third_3, back_2, *fans_3 = sync((context_1a, third_3, back_2, *fans_3))
     pieces_3 = [level_3, first_3, cross_3, third_3, *fans_3, beside(third_3)]
     there_2 = sum_cores(result_2, back_2)
     result_3 = expert(pieces_3, 0, there_2, context_1a)
 
-    turned_2, result_3 = sync((cross(there_2), result_3))
+    turned_0, turned_2, result_3 = sync((cross(there_0), cross(there_2), result_3))
     back_3 = beside(result_3[2])
     held_2, passed_2 = sum_cross(result_2, back_2, turned_2)
     there_3 = sum_cores(result_3, back_3)
-    there_0 = sum_cores(result_0, back_0)
-    total_2 = narrow(held_2 + widen(near(passed_2)))
-    far_2 = far(total_2, 2)
-    result_1 = expert(pieces_p, tokens, there_3, there_0, total_2)
+    held_0, passed_0 = sum_cross(result_0, back_0, turned_0)
+    result_1 = expert(pieces_p, tokens, there_3, passed_2, passed_0)
 
     contexts = [context_0a, context_0b, context_1a]
     sent = [beside(value) for value in contexts]
-    turned_0, turned_3, result_1, *sent = sync((cross(there_0), cross(there_3), result_1, *sent))
+    turned_3, ended_2, result_1, *sent = sync((cross(there_3), near(passed_2), result_1, *sent))
+    far_2 = far(narrow(held_2 + widen(ended_2)), 2)
     back_1 = beside(result_1[2])
     held_3, passed_3 = sum_cross(result_3, back_3, turned_3)
-    held_0, passed_0 = sum_cross(result_0, back_0, turned_0)
     there_1 = sum_cores(result_1, back_1)
     total_3 = narrow(held_3 + widen(near(passed_3)))
     far_3 = far(total_3, 3)

time: 154 us -> 127 us (0.82)
  Pallas kernels: 62.6 us -> 43 us
  local copies, waits for them, and re-layouts: 12.3 us -> 7.32 us
  waiting for transfers between devices: 38.3 us -> 34.1 us
  starting transfers between devices: 36.5 us -> 39.3 us
    pallas_call x1, Pallas kernels: 17.5 us -> 1.14 us  [stack(): pl.pallas_call(stack_kernel, out_shape=jax.ShapeDtypeStruct((2 * rows, wi...]
    unnamed x42 -> x24, local copies, waits for them, and re-layouts: 11.8 us -> 5.67 us
    ppermute x23, waiting for transfers between devices: 34.9 us -> 30.9 us  [swap(): return lax.ppermute(value, ('ep', 'fan'), pairs)]
    pallas_call x4, Pallas kernels: 18.1 us -> 15.2 us  [attend(): pl.pallas_call(functools.partial(attend_kernel, local, heads), out_shape=...]
    ppermute x23, starting transfers between devices: 32 us -> 33.6 us  [swap(): return lax.ppermute(value, ('ep', 'fan'), pairs)]
  transfers between devices with their start and end apart: 45 -> 45, of which waited for: 11 -> 13; matrix products, arithmetic and copies ran while one was open for 1% -> 1% of each run, Pallas kernels for 40% -> 32%
where the time goes in v2:
time: 127 us
  Pallas kernels  43 us (34%)
  starting transfers between devices  39.3 us (31%)
  waiting for transfers between devices  34.1 us (27%)
  local copies, waits for them, and re-layouts  7.32 us (6%)
  other arithmetic  2.36 us (2%)
    ppermute x23, starting transfers between devices, swap(): return lax.ppermute(value, ('ep', 'fan'), pairs)  33.6 us
    ppermute x23, waiting for transfers between devices, swap(): return lax.ppermute(value, ('ep', 'fan'), pairs)  30.9 us
    pallas_call x4, Pallas kernels, expert_chunk(): pl.pallas_call(functools.partial(expert_kernel, count, at_row, tokens), o...  21.9 us
    pallas_call x4, Pallas kernels, attend(): pl.pallas_call(functools.partial(attend_kernel, local, heads), out_shape=...  15.2 us
    unnamed x24, local copies, waits for them, and re-layouts  5.67 us
    ppermute x22, starting transfers between devices, beside(): return lax.ppermute(value, 'fan', [(0, 1), (1, 0)])  5.64 us
    ppermute x22, waiting for transfers between devices, beside(): return lax.ppermute(value, 'fan', [(0, 1), (1, 0)])  3.13 us
  transfers between devices with their start and end apart: 45, of which 13 were waited for; matrix products, arithmetic and copies ran while one was open for 1% of the time, Pallas kernels for 32%

profile of v2, /device:TPU:0, one launch (start us, length us, event | category | flops | bytes accessed | tf_op | source)
XLA Modules:
  0.0 127.1 jit_solution(12592417741493823308)
XLA Ops:
  0.6 1.9 %norm_message.1.refs_0_ = bf16[32,4224]{1,0:T(8,128)(2,1)} custom-call(bf16[32,4096]{1,0:T(8,128)(2,1)} %hidden_ref.1, bf16[4096]{0:T(1024)(128)(2,1)} %gain_ref.1, s32[8,32]{1,0:T(8,128)} %bitcast.20, f32[8,32]{1,0:T(8,128)} %bitcast.21), custom_call_target="tpu_custom_call" | custom-call | flops 1048576 | bytes 16384 | tf_op jit(solution)/shard_map/norm_message/pallas_call | solution.py:63
  2.6 1.5 %reshape.12.q_mine = bf16[64,8192]{1,0:T(8,128)(2,1)S(1)} reshape(bf16[32,2,8192]{2,1,0:T(2,128)(2,1)} %param.12) | data formatting | bytes 2097152 | tf_op jit(solution)/shard_map/reshape | solution.py:377
  4.1 0.5 collective-permute-start.2
  4.6 3.7 %collective-permute-start = (bf16[32,4224]{1,0:T(8,128)(2,1)}, bf16[32,4224]{1,0:T(8,128)(2,1)S(1)}, u32[]{:S(2)}, u32[]{:S(2)}) collective-permute-start(bf16[32,4224]{1,0:T(8,128)(2,1)} %norm_message.1.refs_0_), channel_id=1, source_target_pairs={{0,16},{1,17},{2,18},{3,19},{4,20},{5,21},{6,22},{7,23},{8,24},{9,... | collective-permute-start | bytes 811016 | tf_op jit(solution)/shard_map/ppermute | solution.py:355
  8.3 1.6 %collective-permute-start.1 = (bf16[32,4224]{1,0:T(8,128)(2,1)}, bf16[32,4224]{1,0:T(8,128)(2,1)}, u32[]{:S(2)}, u32[]{:S(2)}) collective-permute-start(bf16[32,4224]{1,0:T(8,128)(2,1)} %norm_message.1.refs_0_), channel_id=1, source_target_pairs={{0,8},{1,9},{2,10},{3,11},{4,12},{5,13},{6,14},{7,15},{8,0},{9,1},... | collective-permute-start | bytes 811016 | tf_op jit(solution)/shard_map/ppermute | solution.py:355
  9.8 1.5 %collective-permute-start.4 = (bf16[32,4224]{1,0:T(8,128)(2,1)}, bf16[32,4224]{1,0:T(8,128)(2,1)S(1)}, u32[]{:S(2)}, u32[]{:S(2)}) collective-permute-start(bf16[32,4224]{1,0:T(8,128)(2,1)} %norm_message.1.refs_0_), channel_id=1, source_target_pairs={{0,2},{1,5},{2,0},{3,7},{4,6},{5,1},{6,4},{7,3},{8,10},{9,13},{10,... | collective-permute-start | bytes 811016 | tf_op jit(solution)/shard_map/ppermute | solution.py:355
  11.3 1.5 %collective-permute-start.5 = (bf16[32,4224]{1,0:T(8,128)(2,1)}, bf16[32,4224]{1,0:T(8,128)(2,1)S(1)}, u32[]{:S(2)}, u32[]{:S(2)}) collective-permute-start(bf16[32,4224]{1,0:T(8,128)(2,1)} %norm_message.1.refs_0_), channel_id=1, source_target_pairs={{0,4},{1,3},{2,6},{3,1},{4,0},{5,7},{6,2},{7,5},{8,12},{9,11},{10,... | collective-permute-start | bytes 811016 | tf_op jit(solution)/shard_map/ppermute | solution.py:355
  12.8 1.2 touch.1.lens_ref
  14.2 0.1 pad_maximum_fusion
  14.4 7.0 %collective-permute-done.top = bf16[32,4224]{1,0:T(8,128)(2,1)S(1)} collective-permute-done((bf16[32,4224]{1,0:T(8,128)(2,1)}, bf16[32,4224]{1,0:T(8,128)(2,1)S(1)}, u32[]{:S(2)}, u32[]{:S(2)}) %collective-permute-start) | collective-permute-done | bytes 270368 | tf_op jit(solution)/shard_map/ppermute | solution.py:355
  21.4 0.3 collective-permute-done.1.bottom
  21.7 1.5 %collective-permute-start.7 = (bf16[32,4224]{1,0:T(8,128)(2,1)S(1)}, bf16[32,4224]{1,0:T(8,128)(2,1)S(1)}, u32[]{:S(2)}, u32[]{:S(2)}) collective-permute-start(bf16[32,4224]{1,0:T(8,128)(2,1)S(1)} %collective-permute-done.top), channel_id=1, source_target_pairs={{0,8},{1,9},{2,10},{3,11},{4,12},{5,13},{6,14},{7,15},{8,0},{9,1},... | collective-permute-start | bytes 811016 | tf_op jit(solution)/shard_map/ppermute | solution.py:355
  23.2 1.1 stack.1.refs_0_
  24.4 1.6 %collective-permute-start.6 = (bf16[32,4224]{1,0:T(8,128)(2,1)S(1)}, bf16[32,4224]{1,0:T(8,128)(2,1)S(1)}, u32[]{:S(2)}, u32[]{:S(2)}) collective-permute-start(bf16[32,4224]{1,0:T(8,128)(2,1)S(1)} %collective-permute-done.4.refs_1_), channel_id=1, source_target_pairs={{0,4},{1,3},{2,6},{3,1},{4,0},{5,7},{6,2},{7,5},{8,12},{9,11},{10,... | collective-permute-start | bytes 811016 | tf_op jit(solution)/shard_map/ppermute | solution.py:355
  26.0 1.6 %collective-permute-start.10 = (bf16[64,4224]{1,0:T(8,128)(2,1)S(1)}, bf16[64,4224]{1,0:T(8,128)(2,1)S(1)}, u32[]{:S(2)}, u32[]{:S(2)}) collective-permute-start(bf16[64,4224]{1,0:T(8,128)(2,1)S(1)} %stack.1.refs_0_), channel_id=1, source_target_pairs={{0,2},{1,5},{2,0},{3,7},{4,6},{5,1},{6,4},{7,3},{8,10},{9,13},{10,... | collective-permute-start | bytes 1622024 | tf_op jit(solution)/shard_map/ppermute | solution.py:355
  27.6 0.5 collective-permute-start.11
  28.1 2.2 %copy-done = bf16[2,1024,1024]{2,1,0:T(8,128)(2,1)S(1)} copy-done((bf16[2,1024,1024]{2,1,0:T(8,128)(2,1)S(1)}, bf16[2,1024,1024]{2,1,0:T(8,128)(2,1)}, u32[]{:S(2)}) %copy-start) | copy-done | bytes 4194328
  30.3 0.7 copy-done.6
  30.9 3.8 %attend.4.refs_0_ = bf16[32,4096]{1,0:T(8,128)(2,1)S(1)} custom-call(s32[4]{0:T(128)S(1)} %copy-done.6, bf16[64,8192]{1,0:T(8,128)(2,1)S(1)} %reshape.12.q_mine, bf16[64,8192]{1,0:T(8,128)(2,1)S(1)} %collective-permute-done.2.q_other, bf16[64,1152]{1,0:T(8,128)(2,1)S(1)} %reshape.11.o_mine, bf16[64,1152]{1,0:T(8,128)(2,1)S(1)} %collective-permute-done.3.o_other, ...), custom_call_target="tpu_custom_call" | custom-call | flops 1048576 | bytes 16384 | tf_op jit(solution)/shard_map/attend/pallas_call | solution.py:205
  34.9 0.5 collective-permute-start.14
  35.4 3.8 %attend.5.refs_11_.refs_4_ = bf16[32,4096]{1,0:T(8,128)(2,1)S(1)} custom-call(s32[4]{0:T(128)S(1)} %copy-done.7, bf16[64,8192]{1,0:T(8,128)(2,1)S(1)} %reshape.12.q_mine, bf16[64,8192]{1,0:T(8,128)(2,1)S(1)} %collective-permute-done.2.q_other, bf16[64,1152]{1,0:T(8,128)(2,1)S(1)} %reshape.11.o_mine, bf16[64,1152]{1,0:T(8,128)(2,1)S(1)} %collective-permute-done.3.o_other, ...), custom_call_target="tpu_custom_call" | custom-call | flops 1048576 | bytes 16384 | tf_op jit(solution)/shard_map/attend/pallas_call | solution.py:205
  39.3 0.5 collective-permute-start.17
  39.7 1.2 collective-permute-done.10.refs_12_.refs_1_
  40.9 1.6 %collective-permute-done.11.refs_2_ = bf16[64,4224]{1,0:T(8,128)(2,1)S(1)} collective-permute-done((bf16[64,4224]{1,0:T(8,128)(2,1)S(1)}, bf16[64,4224]{1,0:T(8,128)(2,1)S(1)}, u32[]{:S(2)}, u32[]{:S(2)}) %collective-permute-start.11) | collective-permute-done | bytes 540704 | tf_op jit(solution)/shard_map/ppermute | solution.py:355
  42.5 1.5 %collective-permute-start.16 = (bf16[64,4224]{1,0:T(8,128)(2,1)S(1)}, bf16[64,4224]{1,0:T(8,128)(2,1)S(1)}, u32[]{:S(2)}, u32[]{:S(2)}) collective-permute-start(bf16[64,4224]{1,0:T(8,128)(2,1)S(1)} %collective-permute-done.10.refs_12_.refs_1_), channel_id=1, source_target_pairs={{0,4},{1,3},{2,6},{3,1},{4,0},{5,7},{6,2},{7,5},{8,12},{9,11},{10,... | collective-permute-start | bytes 1622024 | tf_op jit(solution)/shard_map/ppermute | solution.py:355
  44.1 0.5 collective-permute-start.19
  44.6 2.8 %copy-done.3 = bf16[1,4096,768]{2,1,0:T(8,128)(2,1)S(1)} copy-done((bf16[1,4096,768]{2,1,0:T(8,128)(2,1)S(1)}, bf16[1,4096,768]{2,1,0:T(8,128)(2,1)}, u32[]{:S(2)}) %copy-start.3) | copy-done | bytes 6291480
  47.4 5.5 %expert_chunk.4 = (bf16[64,4096]{1,0:T(8,128)(2,1)S(1)}, bf16[64,4096]{1,0:T(8,128)(2,1)S(1)}, bf16[128,4096]{1,0:T(8,128)(2,1)S(1)}) custom-call(bf16[32,4224]{1,0:T(8,128)(2,1)S(1)} %copy-done.5, bf16[32,4224]{1,0:T(8,128)(2,1)S(1)} %collective-permute-done.4.refs_1_, bf16[32,4224]{1,0:T(8,128)(2,1)S(1)} %collective-permute-done.5.refs_2_, ...), custom_call_target="tpu_custom_call" | custom-call | flops 1048576 | bytes 16384 | tf_op jit(solution)/shard_map/expert_chunk/pallas_call | solution.py:309
  53.0 0.5 collective-permute-start.21
  53.5 1.5 %collective-permute-start.8 = (bf16[32,4224]{1,0:T(8,128)(2,1)S(1)}, bf16[32,4224]{1,0:T(8,128)(2,1)S(1)}, u32[]{:S(2)}, u32[]{:S(2)}) collective-permute-start(bf16[32,4224]{1,0:T(8,128)(2,1)S(1)} %collective-permute-done.7.refs_0_), channel_id=1, source_target_pairs={{0,2},{1,5},{2,0},{3,7},{4,6},{5,1},{6,4},{7,3},{8,10},{9,13},{10,... | collective-permute-start | bytes 811016 | tf_op jit(solution)/shard_map/ppermute | solution.py:355
  55.0 0.5 collective-permute-start.9
  55.5 0.9 collective-permute-done.21.refs_7_
  56.4 5.5 %expert_chunk.5 = (bf16[64,4096]{1,0:T(8,128)(2,1)S(1)}, bf16[64,4096]{1,0:T(8,128)(2,1)S(1)}, bf16[128,4096]{1,0:T(8,128)(2,1)S(1)}) custom-call(bf16[64,4224]{1,0:T(8,128)(2,1)S(1)} %stack.1.refs_0_, bf16[64,4224]{1,0:T(8,128)(2,1)S(1)} %collective-permute-done.10.refs_12_.refs_1_, bf16[64,4224]{1,0:T(8,128)(2,1)S(1)} %collective-permute-done.11.refs_2_, ...), custom_call_target="tpu_custom_call" | custom-call | flops 1048576 | bytes 16384 | tf_op jit(solution)/shard_map/expert_chunk/pallas_call | solution.py:309
  61.9 0.3 collective-permute-done.8.refs_0_.refs_1_
  62.2 0.5 collective-permute-start.24
  62.7 0.8 collective-permute-start.22
  63.5 0.4 collective-permute-start.25
  64.2 3.8 %attend.6.refs_12_.refs_1_ = bf16[32,4096]{1,0:T(8,128)(2,1)S(1)} custom-call(s32[4]{0:T(128)S(1)} %copy-done.7, bf16[64,8192]{1,0:T(8,128)(2,1)S(1)} %reshape.12.q_mine, bf16[64,8192]{1,0:T(8,128)(2,1)S(1)} %collective-permute-done.2.q_other, bf16[64,1152]{1,0:T(8,128)(2,1)S(1)} %reshape.11.o_mine, bf16[64,1152]{1,0:T(8,128)(2,1)S(1)} %collective-permute-done.3.o_other, ...), custom_call_target="tpu_custom_call" | custom-call | flops 1048576 | bytes 16384 | tf_op jit(solution)/shard_map/attend/pallas_call | solution.py:205
  68.0 1.2 collective-permute-start.27
  69.4 0.9 collective-permute-start.28
  70.3 1.5 %collective-permute-done.29.refs_7_ = bf16[32,4224]{1,0:T(8,128)(2,1)S(1)} collective-permute-done((bf16[32,4224]{1,0:T(8,128)(2,1)S(1)}, bf16[32,4224]{1,0:T(8,128)(2,1)S(1)}, u32[]{:S(2)}, u32[]{:S(2)}) %collective-permute-start.29) | collective-permute-done | bytes 270368 | tf_op jit(solution)/shard_map/ppermute | solution.py:367
  71.9 5.3 %expert_chunk.6 = (bf16[64,4096]{1,0:T(8,128)(2,1)S(1)}, bf16[64,4096]{1,0:T(8,128)(2,1)S(1)}, bf16[128,4096]{1,0:T(8,128)(2,1)S(1)}) custom-call(bf16[32,4224]{1,0:T(8,128)(2,1)S(1)} %collective-permute-done.7.refs_0_, bf16[32,4224]{1,0:T(8,128)(2,1)S(1)} %collective-permute-done.8.refs_0_.refs_1_, ...), custom_call_target="tpu_custom_call" | custom-call | flops 1048576 | bytes 16384 | tf_op jit(solution)/shard_map/expert_chunk/pallas_call | solution.py:309
  77.3 5.6 %collective-permute-done.28 = bf16[64,4096]{1,0:T(8,128)(2,1)S(1)} collective-permute-done((bf16[64,4096]{1,0:T(8,128)(2,1)S(1)}, bf16[64,4096]{1,0:T(8,128)(2,1)S(1)}, u32[]{:S(2)}, u32[]{:S(2)}) %collective-permute-start.28) | collective-permute-done | bytes 524320 | tf_op jit(solution)/shard_map/ppermute | solution.py:355
  82.9 0.5 collective-permute-start.33
  83.4 0.5 collective-permute-start.35
  84.0 1.6 %collective-permute-start.32 = (bf16[32,4096]{1,0:T(8,128)(2,1)S(1)}, bf16[32,4096]{1,0:T(8,128)(2,1)S(1)}, u32[]{:S(2)}, u32[]{:S(2)}) collective-permute-start(bf16[32,4096]{1,0:T(8,128)(2,1)S(1)} %add_convert_fusion.11.refs_12_), channel_id=1, source_target_pairs={{0,2},{1,5},{2,0},{3,7},{4,6},{5,1},{6,4},{7,3},{8,10},{9,13},{10,... | collective-permute-start | bytes 786440 | tf_op jit(solution)/shard_map/ppermute | solution.py:355
  85.7 1.2 collective-permute-start.31
  87.0 5.6 %expert_chunk.7 = (bf16[64,4096]{1,0:T(8,128)(2,1)S(1)}, bf16[64,4096]{1,0:T(8,128)(2,1)S(1)}, bf16[128,4096]{1,0:T(8,128)(2,1)S(1)}) custom-call(bf16[64,4224]{1,0:T(8,128)(2,1)S(1)} %stack.1.refs_0_, bf16[64,4224]{1,0:T(8,128)(2,1)S(1)} %collective-permute-done.10.refs_12_.refs_1_, bf16[64,4224]{1,0:T(8,128)(2,1)S(1)} %collective-permute-done.11.refs_2_, ...), custom_call_target="tpu_custom_call" | custom-call | flops 1048576 | bytes 16384 | tf_op jit(solution)/shard_map/expert_chunk/pallas_call | solution.py:309
  92.7 2.4 %collective-permute-done.31 = bf16[64,4096]{1,0:T(8,128)(2,1)S(1)} collective-permute-done((bf16[64,4096]{1,0:T(8,128)(2,1)S(1)}, bf16[64,4096]{1,0:T(8,128)(2,1)S(1)}, u32[]{:S(2)}, u32[]{:S(2)}) %collective-permute-start.31) | collective-permute-done | bytes 524320 | tf_op jit(solution)/shard_map/ppermute | solution.py:355
  95.1 0.8 collective-permute-start.38
  96.0 1.6 %collective-permute-start.37 = (bf16[32,4096]{1,0:T(8,128)(2,1)S(1)}, bf16[32,4096]{1,0:T(8,128)(2,1)S(1)}, u32[]{:S(2)}, u32[]{:S(2)}) collective-permute-start(bf16[32,4096]{1,0:T(8,128)(2,1)S(1)} %add_convert_fusion.8), channel_id=1, source_target_pairs={{0,2},{1,5},{2,0},{3,7},{4,6},{5,1},{6,4},{7,3},{8,10},{9,13},{10,... | collective-permute-start | bytes 786440 | tf_op jit(solution)/shard_map/ppermute | solution.py:355
  97.5 0.6 collective-permute-done.38
  98.3 1.2 collective-permute-start.39
  99.7 2.4 %collective-permute-start.36 = (bf16[32,4096]{1,0:T(8,128)(2,1)S(1)}, bf16[32,4096]{1,0:T(8,128)(2,1)S(1)}, u32[]{:S(2)}, u32[]{:S(2)}) collective-permute-start(bf16[32,4096]{1,0:T(8,128)(2,1)S(1)} %add_convert_fusion.9), channel_id=1, source_target_pairs={{0,16},{1,17},{2,18},{3,19},{4,20},{5,21},{6,22},{7,23},{8,24},{9,... | collective-permute-start | bytes 786440 | tf_op jit(solution)/shard_map/ppermute | solution.py:355
  102.0 5.5 %collective-permute-done.39 = bf16[64,4096]{1,0:T(8,128)(2,1)S(1)} collective-permute-done((bf16[64,4096]{1,0:T(8,128)(2,1)S(1)}, bf16[64,4096]{1,0:T(8,128)(2,1)S(1)}, u32[]{:S(2)}, u32[]{:S(2)}) %collective-permute-start.39) | collective-permute-done | bytes 524320 | tf_op jit(solution)/shard_map/ppermute | solution.py:355
  107.6 1.6 %collective-permute-start.41 = (bf16[32,4096]{1,0:T(8,128)(2,1)S(1)}, bf16[32,4096]{1,0:T(8,128)(2,1)S(1)}, u32[]{:S(2)}, u32[]{:S(2)}) collective-permute-start(bf16[32,4096]{1,0:T(8,128)(2,1)S(1)} %add_convert_fusion.6.refs_1_), channel_id=1, source_target_pairs={{0,2},{1,5},{2,0},{3,7},{4,6},{5,1},{6,4},{7,3},{8,10},{9,13},{10,... | collective-permute-start | bytes 786440 | tf_op jit(solution)/shard_map/ppermute | solution.py:355
  109.3 1.8 %collective-permute-start.43 = (bf16[32,4096]{1,0:T(8,128)(2,1)S(1)}, bf16[32,4096]{1,0:T(8,128)(2,1)S(1)}, u32[]{:S(2)}, u32[]{:S(2)}) collective-permute-start(bf16[32,4096]{1,0:T(8,128)(2,1)S(1)} %add_convert_fusion.7.refs_0_), channel_id=1, source_target_pairs={{0,24},{1,25},{2,26},{3,27},{4,28},{5,29},{6,30},{7,31},{8,16},{9,... | collective-permute-start | bytes 786440 | tf_op jit(solution)/shard_map/ppermute | solution.py:355
  111.1 3.8 %attend.7.refs_5_ = bf16[32,4096]{1,0:T(8,128)(2,1)S(1)} custom-call(s32[4]{0:T(128)S(1)} %copy-done.7, bf16[64,8192]{1,0:T(8,128)(2,1)S(1)} %reshape.12.q_mine, bf16[64,8192]{1,0:T(8,128)(2,1)S(1)} %collective-permute-done.2.q_other, bf16[64,1152]{1,0:T(8,128)(2,1)S(1)} %reshape.11.o_mine, bf16[64,1152]{1,0:T(8,128)(2,1)S(1)} %collective-permute-done.3.o_other, ...), custom_call_target="tpu_custom_call" | custom-call | flops 1048576 | bytes 16384 | tf_op jit(solution)/shard_map/attend/pallas_call | solution.py:205
  115.2 1.2 collective-permute-start.42
  116.4 1.2 collective-permute-start.44
  117.6 3.1 %collective-permute-done.36 = bf16[32,4096]{1,0:T(8,128)(2,1)S(1)} collective-permute-done((bf16[32,4096]{1,0:T(8,128)(2,1)S(1)}, bf16[32,4096]{1,0:T(8,128)(2,1)S(1)}, u32[]{:S(2)}, u32[]{:S(2)}) %collective-permute-start.36) | collective-permute-done | bytes 262176 | tf_op jit(solution)/shard_map/ppermute | solution.py:355
  120.7 1.6 %place_context.1 = bf16[32,2,8192]{2,1,0:T(2,128)(2,1)} custom-call(bf16[64,1152]{1,0:T(8,128)(2,1)S(1)} %reshape.11.o_mine, bf16[32,4096]{1,0:T(8,128)(2,1)S(1)} %attend.4.refs_0_, bf16[32,4096]{1,0:T(8,128)(2,1)S(1)} %attend.6.refs_12_.refs_1_, bf16[32,4096]{1,0:T(8,128)(2,1)S(1)} %collective-permute-done.33.refs_2_, ...), custom_call_target="tpu_custom_call" | custom-call | flops 1048576 | bytes 16384 | tf_op jit(solution)/shard_map/place_context/pallas_call | solution.py:255
  122.3 3.8 %collective-permute-done.42 = bf16[32,4096]{1,0:T(8,128)(2,1)S(1)} collective-permute-done((bf16[32,4096]{1,0:T(8,128)(2,1)S(1)}, bf16[32,4096]{1,0:T(8,128)(2,1)S(1)}, u32[]{:S(2)}, u32[]{:S(2)}) %collective-permute-start.42) | collective-permute-done | bytes 262176 | tf_op jit(solution)/shard_map/ppermute | solution.py:355
  126.1 0.9 add_convert_fusion.4
  (80 shorter events, 2.0 us)
Async XLA Ops:
  2.6 11.5 %copy-start.9 = (s32[32]{0:T(128)S(1)}, s32[32]{0:T(128)}, u32[]{:S(2)}) copy-start(s32[32]{0:T(128)} %param.16) | copy-start | bytes 388
  2.6 11.6 %copy-start.8 = (bf16[32,2,1024]{2,1,0:T(2,128)(2,1)S(1)}, bf16[32,2,1024]{2,1,0:T(2,128)(2,1)}, u32[]{:S(2)}) copy-start(bf16[32,2,1024]{2,1,0:T(2,128)(2,1)} %param.13) | copy-start | bytes 393220
  4.1 21.9 %copy-start.5 = (bf16[32,4224]{1,0:T(8,128)(2,1)S(1)}, bf16[32,4224]{1,0:T(8,128)(2,1)}, u32[]{:S(2)}) copy-start(bf16[32,4224]{1,0:T(8,128)(2,1)} %norm_message.1.refs_0_) | copy-start | bytes 811012
  4.1 23.5 %collective-permute-start.2 = (bf16[64,8192]{1,0:T(8,128)(2,1)S(1)}, bf16[64,8192]{1,0:T(8,128)(2,1)S(1)}, u32[]{:S(2)}, u32[]{:S(2)}) collective-permute-start(bf16[64,8192]{1,0:T(8,128)(2,1)S(1)} %reshape.12.q_mine), channel_id=1, source_target_pairs={{0,1},{1,0},{2,3},{3,2},{4,5},{5,4},{6,7},{7,6},{8,9},{9,8},{10,11... | collective-permute-start | bytes 3145736 | tf_op jit(solution)/shard_map/ppermute | solution.py:367
  4.6 16.8 %collective-permute-start = (bf16[32,4224]{1,0:T(8,128)(2,1)}, bf16[32,4224]{1,0:T(8,128)(2,1)S(1)}, u32[]{:S(2)}, u32[]{:S(2)}) collective-permute-start(bf16[32,4224]{1,0:T(8,128)(2,1)} %norm_message.1.refs_0_), channel_id=1, source_target_pairs={{0,16},{1,17},{2,18},{3,19},{4,20},{5,21},{6,22},{7,23},{8,24},{9,... | collective-permute-start | bytes 811016 | tf_op jit(solution)/shard_map/ppermute | solution.py:355
  8.3 13.5 %collective-permute-start.1 = (bf16[32,4224]{1,0:T(8,128)(2,1)}, bf16[32,4224]{1,0:T(8,128)(2,1)}, u32[]{:S(2)}, u32[]{:S(2)}) collective-permute-start(bf16[32,4224]{1,0:T(8,128)(2,1)} %norm_message.1.refs_0_), channel_id=1, source_target_pairs={{0,8},{1,9},{2,10},{3,11},{4,12},{5,13},{6,14},{7,15},{8,0},{9,1},... | collective-permute-start | bytes 811016 | tf_op jit(solution)/shard_map/ppermute | solution.py:355
  9.8 14.6 %collective-permute-start.4 = (bf16[32,4224]{1,0:T(8,128)(2,1)}, bf16[32,4224]{1,0:T(8,128)(2,1)S(1)}, u32[]{:S(2)}, u32[]{:S(2)}) collective-permute-start(bf16[32,4224]{1,0:T(8,128)(2,1)} %norm_message.1.refs_0_), channel_id=1, source_target_pairs={{0,2},{1,5},{2,0},{3,7},{4,6},{5,1},{6,4},{7,3},{8,10},{9,13},{10,... | collective-permute-start | bytes 811016 | tf_op jit(solution)/shard_map/ppermute | solution.py:355
  11.3 14.7 %collective-permute-start.5 = (bf16[32,4224]{1,0:T(8,128)(2,1)}, bf16[32,4224]{1,0:T(8,128)(2,1)S(1)}, u32[]{:S(2)}, u32[]{:S(2)}) collective-permute-start(bf16[32,4224]{1,0:T(8,128)(2,1)} %norm_message.1.refs_0_), channel_id=1, source_target_pairs={{0,4},{1,3},{2,6},{3,1},{4,0},{5,7},{6,2},{7,5},{8,12},{9,11},{10,... | collective-permute-start | bytes 811016 | tf_op jit(solution)/shard_map/ppermute | solution.py:355
  14.1 21.4 %copy-start.7 = (s32[4]{0:T(128)S(1)}, s32[4]{0:T(128)}, u32[]{:S(2)}) copy-start(s32[4]{0:T(128)} %touch.1.lens_ref) | copy-start | bytes 52
  21.4 4.6 %collective-permute-start.3 = (bf16[64,1152]{1,0:T(8,128)(2,1)S(1)}, bf16[64,1152]{1,0:T(8,128)(2,1)S(1)}, u32[]{:S(2)}, u32[]{:S(2)}) collective-permute-start(bf16[64,1152]{1,0:T(8,128)(2,1)S(1)} %reshape.11.o_mine), channel_id=1, source_target_pairs={{0,1},{1,0},{2,3},{3,2},{4,5},{5,4},{6,7},{7,6},{8,9},{9,8},{10,11... | collective-permute-start | bytes 442376 | tf_op jit(solution)/shard_map/ppermute | solution.py:367
  21.7 13.0 %collective-permute-start.7 = (bf16[32,4224]{1,0:T(8,128)(2,1)S(1)}, bf16[32,4224]{1,0:T(8,128)(2,1)S(1)}, u32[]{:S(2)}, u32[]{:S(2)}) collective-permute-start(bf16[32,4224]{1,0:T(8,128)(2,1)S(1)} %collective-permute-done.top), channel_id=1, source_target_pairs={{0,8},{1,9},{2,10},{3,11},{4,12},{5,13},{6,14},{7,15},{8,0},{9,1},... | collective-permute-start | bytes 811016 | tf_op jit(solution)/shard_map/ppermute | solution.py:355
  23.2 21.3 %slice-start = ((s8[6291456]{0:T(1024)(128)(4,1)}), s8[4194304]{0:T(1024)(128)(4,1)S(1)}, s32[]{:S(2)}) async-start(s8[6291456]{0:T(1024)(128)(4,1)} %bitcast.6), calls=%async_computation | async-start | bytes 8388608
  24.4 20.2 %slice-start.1 = ((s8[6291456]{0:T(1024)(128)(4,1)}), s8[2097152]{0:T(1024)(128)(4,1)S(1)}, s32[]{:S(2)}) async-start(s8[6291456]{0:T(1024)(128)(4,1)} %bitcast.6), calls=%async_computation.1 | async-start | bytes 4194304
  24.4 10.4 %collective-permute-start.6 = (bf16[32,4224]{1,0:T(8,128)(2,1)S(1)}, bf16[32,4224]{1,0:T(8,128)(2,1)S(1)}, u32[]{:S(2)}, u32[]{:S(2)}) collective-permute-start(bf16[32,4224]{1,0:T(8,128)(2,1)S(1)} %collective-permute-done.4.refs_1_), channel_id=1, source_target_pairs={{0,4},{1,3},{2,6},{3,1},{4,0},{5,7},{6,2},{7,5},{8,12},{9,11},{10,... | collective-permute-start | bytes 811016 | tf_op jit(solution)/shard_map/ppermute | solution.py:355
  26.0 9.3 %collective-permute-start.12 = (bf16[32,4224]{1,0:T(8,128)(2,1)S(1)}, bf16[32,4224]{1,0:T(8,128)(2,1)S(1)}, u32[]{:S(2)}, u32[]{:S(2)}) collective-permute-start(bf16[32,4224]{1,0:T(8,128)(2,1)S(1)} %copy-done.5), channel_id=1, source_target_pairs={{0,1},{1,0},{2,3},{3,2},{4,5},{5,4},{6,7},{7,6},{8,9},{9,8},{10,11... | collective-permute-start | bytes 811016 | tf_op jit(solution)/shard_map/ppermute | solution.py:367
  26.0 14.9 %collective-permute-start.10 = (bf16[64,4224]{1,0:T(8,128)(2,1)S(1)}, bf16[64,4224]{1,0:T(8,128)(2,1)S(1)}, u32[]{:S(2)}, u32[]{:S(2)}) collective-permute-start(bf16[64,4224]{1,0:T(8,128)(2,1)S(1)} %stack.1.refs_0_), channel_id=1, source_target_pairs={{0,2},{1,5},{2,0},{3,7},{4,6},{5,1},{6,4},{7,3},{8,10},{9,13},{10,... | collective-permute-start | bytes 1622024 | tf_op jit(solution)/shard_map/ppermute | solution.py:355
  27.6 14.9 %collective-permute-start.11 = (bf16[64,4224]{1,0:T(8,128)(2,1)S(1)}, bf16[64,4224]{1,0:T(8,128)(2,1)S(1)}, u32[]{:S(2)}, u32[]{:S(2)}) collective-permute-start(bf16[64,4224]{1,0:T(8,128)(2,1)S(1)} %stack.1.refs_0_), channel_id=1, source_target_pairs={{0,4},{1,3},{2,6},{3,1},{4,0},{5,7},{6,2},{7,5},{8,12},{9,11},{10,... | collective-permute-start | bytes 1622024 | tf_op jit(solution)/shard_map/ppermute | solution.py:355
  28.1 2.2 %copy-start = (bf16[2,1024,1024]{2,1,0:T(8,128)(2,1)S(1)}, bf16[2,1024,1024]{2,1,0:T(8,128)(2,1)}, u32[]{:S(2)}) copy-start(bf16[2,1024,1024]{2,1,0:T(8,128)(2,1)} %cache.7) | copy-start | bytes 12582916
  30.3 0.7 copy-start.6
  30.9 13.6 %copy-start.2 = (bf16[1,4096,768]{2,1,0:T(8,128)(2,1)S(1)}, bf16[1,4096,768]{2,1,0:T(8,128)(2,1)}, u32[]{:S(2)}) copy-start(bf16[1,4096,768]{2,1,0:T(8,128)(2,1)} %param.21) | copy-start | bytes 18874372
  34.8 4.5 %collective-permute-start.13 = (bf16[32,4224]{1,0:T(8,128)(2,1)S(1)}, bf16[32,4224]{1,0:T(8,128)(2,1)S(1)}, u32[]{:S(2)}, u32[]{:S(2)}) collective-permute-start(bf16[32,4224]{1,0:T(8,128)(2,1)S(1)} %collective-permute-done.4.refs_1_), channel_id=1, source_target_pairs={{0,1},{1,0},{2,3},{3,2},{4,5},{5,4},{6,7},{7,6},{8,9},{9,8},{10,11... | collective-permute-start | bytes 811016 | tf_op jit(solution)/shard_map/ppermute | solution.py:367
  34.9 4.9 %collective-permute-start.14 = (bf16[32,4224]{1,0:T(8,128)(2,1)S(1)}, bf16[32,4224]{1,0:T(8,128)(2,1)S(1)}, u32[]{:S(2)}, u32[]{:S(2)}) collective-permute-start(bf16[32,4224]{1,0:T(8,128)(2,1)S(1)} %collective-permute-done.5.refs_2_), channel_id=1, source_target_pairs={{0,1},{1,0},{2,3},{3,2},{4,5},{5,4},{6,7},{7,6},{8,9},{9,8},{10,11... | collective-permute-start | bytes 811016 | tf_op jit(solution)/shard_map/ppermute | solution.py:367
  35.3 7.2 %collective-permute-start.15 = (bf16[32,4224]{1,0:T(8,128)(2,1)S(1)}, bf16[32,4224]{1,0:T(8,128)(2,1)S(1)}, u32[]{:S(2)}, u32[]{:S(2)}) collective-permute-start(bf16[32,4224]{1,0:T(8,128)(2,1)S(1)} %collective-permute-done.6.refs_3_), channel_id=1, source_target_pairs={{0,1},{1,0},{2,3},{3,2},{4,5},{5,4},{6,7},{7,6},{8,9},{9,8},{10,11... | collective-permute-start | bytes 811016 | tf_op jit(solution)/shard_map/ppermute | solution.py:367
  39.3 13.6 %collective-permute-start.17 = (bf16[64,4224]{1,0:T(8,128)(2,1)S(1)}, bf16[64,4224]{1,0:T(8,128)(2,1)S(1)}, u32[]{:S(2)}, u32[]{:S(2)}) collective-permute-start(bf16[64,4224]{1,0:T(8,128)(2,1)S(1)} %stack.1.refs_0_), channel_id=1, source_target_pairs={{0,1},{1,0},{2,3},{3,2},{4,5},{5,4},{6,7},{7,6},{8,9},{9,8},{10,11... | collective-permute-start | bytes 1622024 | tf_op jit(solution)/shard_map/ppermute | solution.py:367
  42.5 10.3 %collective-permute-start.16 = (bf16[64,4224]{1,0:T(8,128)(2,1)S(1)}, bf16[64,4224]{1,0:T(8,128)(2,1)S(1)}, u32[]{:S(2)}, u32[]{:S(2)}) collective-permute-start(bf16[64,4224]{1,0:T(8,128)(2,1)S(1)} %collective-permute-done.10.refs_12_.refs_1_), channel_id=1, source_target_pairs={{0,4},{1,3},{2,6},{3,1},{4,0},{5,7},{6,2},{7,5},{8,12},{9,11},{10,... | collective-permute-start | bytes 1622024 | tf_op jit(solution)/shard_map/ppermute | solution.py:355
  44.1 8.8 %collective-permute-start.18 = (bf16[64,4224]{1,0:T(8,128)(2,1)S(1)}, bf16[64,4224]{1,0:T(8,128)(2,1)S(1)}, u32[]{:S(2)}, u32[]{:S(2)}) collective-permute-start(bf16[64,4224]{1,0:T(8,128)(2,1)S(1)} %collective-permute-done.10.refs_12_.refs_1_), channel_id=1, source_target_pairs={{0,1},{1,0},{2,3},{3,2},{4,5},{5,4},{6,7},{7,6},{8,9},{9,8},{10,11... | collective-permute-start | bytes 1622024 | tf_op jit(solution)/shard_map/ppermute | solution.py:367
  44.1 8.8 %collective-permute-start.19 = (bf16[64,4224]{1,0:T(8,128)(2,1)S(1)}, bf16[64,4224]{1,0:T(8,128)(2,1)S(1)}, u32[]{:S(2)}, u32[]{:S(2)}) collective-permute-start(bf16[64,4224]{1,0:T(8,128)(2,1)S(1)} %collective-permute-done.11.refs_2_), channel_id=1, source_target_pairs={{0,1},{1,0},{2,3},{3,2},{4,5},{5,4},{6,7},{7,6},{8,9},{9,8},{10,11... | collective-permute-start | bytes 1622024 | tf_op jit(solution)/shard_map/ppermute | solution.py:367
  44.6 2.8 %copy-start.3 = (bf16[1,4096,768]{2,1,0:T(8,128)(2,1)S(1)}, bf16[1,4096,768]{2,1,0:T(8,128)(2,1)}, u32[]{:S(2)}) copy-start(bf16[1,4096,768]{2,1,0:T(8,128)(2,1)} %param.22) | copy-start | bytes 18874372
  47.4 9.0 %copy-start.4 = (bf16[1,4096,768]{2,1,0:T(8,128)(2,1)S(1)}, bf16[1,4096,768]{2,1,0:T(8,128)(2,1)}, u32[]{:S(2)}) copy-start(bf16[1,4096,768]{2,1,0:T(8,128)(2,1)} %param.22) | copy-start | bytes 18874372
  52.9 11.3 %copy-start.1 = (bf16[2,1024,1024]{2,1,0:T(8,128)(2,1)S(1)}, bf16[2,1024,1024]{2,1,0:T(8,128)(2,1)}, u32[]{:S(2)}) copy-start(bf16[2,1024,1024]{2,1,0:T(8,128)(2,1)} %cache.7) | copy-start | bytes 12582916
  52.9 9.3 %collective-permute-start.20 = (bf16[128,4096]{1,0:T(8,128)(2,1)S(1)}, bf16[128,4096]{1,0:T(8,128)(2,1)S(1)}, u32[]{:S(2)}, u32[]{:S(2)}) collective-permute-start(bf16[128,4096]{1,0:T(8,128)(2,1)S(1)} %get-tuple-element.98), channel_id=1, source_target_pairs={{0,1},{1,0},{2,3},{3,2},{4,5},{5,4},{6,7},{7,6},{8,9},{9,8},{10,11... | collective-permute-start | bytes 3145736 | tf_op jit(solution)/shard_map/ppermute | solution.py:367
  53.0 3.4 %collective-permute-start.21 = (bf16[64,4224]{1,0:T(8,128)(2,1)S(1)}, bf16[64,4224]{1,0:T(8,128)(2,1)S(1)}, u32[]{:S(2)}, u32[]{:S(2)}) collective-permute-start(bf16[64,4224]{1,0:T(8,128)(2,1)S(1)} %collective-permute-done.16.refs_3_), channel_id=1, source_target_pairs={{0,1},{1,0},{2,3},{3,2},{4,5},{5,4},{6,7},{7,6},{8,9},{9,8},{10,11... | collective-permute-start | bytes 1622024 | tf_op jit(solution)/shard_map/ppermute | solution.py:367
  53.5 8.7 %collective-permute-start.8 = (bf16[32,4224]{1,0:T(8,128)(2,1)S(1)}, bf16[32,4224]{1,0:T(8,128)(2,1)S(1)}, u32[]{:S(2)}, u32[]{:S(2)}) collective-permute-start(bf16[32,4224]{1,0:T(8,128)(2,1)S(1)} %collective-permute-done.7.refs_0_), channel_id=1, source_target_pairs={{0,2},{1,5},{2,0},{3,7},{4,6},{5,1},{6,4},{7,3},{8,10},{9,13},{10,... | collective-permute-start | bytes 811016 | tf_op jit(solution)/shard_map/ppermute | solution.py:355
  55.0 7.2 %collective-permute-start.9 = (bf16[32,4224]{1,0:T(8,128)(2,1)S(1)}, bf16[32,4224]{1,0:T(8,128)(2,1)S(1)}, u32[]{:S(2)}, u32[]{:S(2)}) collective-permute-start(bf16[32,4224]{1,0:T(8,128)(2,1)S(1)} %collective-permute-done.7.refs_0_), channel_id=1, source_target_pairs={{0,4},{1,3},{2,6},{3,1},{4,0},{5,7},{6,2},{7,5},{8,12},{9,11},{10,... | collective-permute-start | bytes 811016 | tf_op jit(solution)/shard_map/ppermute | solution.py:355
  62.2 7.1 %collective-permute-start.23 = (bf16[128,4096]{1,0:T(8,128)(2,1)S(1)}, bf16[128,4096]{1,0:T(8,128)(2,1)S(1)}, u32[]{:S(2)}, u32[]{:S(2)}) collective-permute-start(bf16[128,4096]{1,0:T(8,128)(2,1)S(1)} %get-tuple-element.112), channel_id=1, source_target_pairs={{0,1},{1,0},{2,3},{3,2},{4,5},{5,4},{6,7},{7,6},{8,9},{9,8},{10,11... | collective-permute-start | bytes 3145736 | tf_op jit(solution)/shard_map/ppermute | solution.py:367
  62.2 5.8 %collective-permute-start.24 = (bf16[32,4224]{1,0:T(8,128)(2,1)S(1)}, bf16[32,4224]{1,0:T(8,128)(2,1)S(1)}, u32[]{:S(2)}, u32[]{:S(2)}) collective-permute-start(bf16[32,4224]{1,0:T(8,128)(2,1)S(1)} %collective-permute-done.7.refs_0_), channel_id=1, source_target_pairs={{0,1},{1,0},{2,3},{3,2},{4,5},{5,4},{6,7},{7,6},{8,9},{9,8},{10,11... | collective-permute-start | bytes 811016 | tf_op jit(solution)/shard_map/ppermute | solution.py:367
  62.7 6.6 %collective-permute-start.22 = (bf16[32,4224]{1,0:T(8,128)(2,1)S(1)}, bf16[32,4224]{1,0:T(8,128)(2,1)S(1)}, u32[]{:S(2)}, u32[]{:S(2)}) collective-permute-start(bf16[32,4224]{1,0:T(8,128)(2,1)S(1)} %collective-permute-done.8.refs_0_.refs_1_), channel_id=1, source_target_pairs={{0,4},{1,3},{2,6},{3,1},{4,0},{5,7},{6,2},{7,5},{8,12},{9,11},{10,... | collective-permute-start | bytes 811016 | tf_op jit(solution)/shard_map/ppermute | solution.py:355
  63.5 5.7 %collective-permute-start.25 = (bf16[32,4224]{1,0:T(8,128)(2,1)S(1)}, bf16[32,4224]{1,0:T(8,128)(2,1)S(1)}, u32[]{:S(2)}, u32[]{:S(2)}) collective-permute-start(bf16[32,4224]{1,0:T(8,128)(2,1)S(1)} %collective-permute-done.8.refs_0_.refs_1_), channel_id=1, source_target_pairs={{0,1},{1,0},{2,3},{3,2},{4,5},{5,4},{6,7},{7,6},{8,9},{9,8},{10,11... | collective-permute-start | bytes 811016 | tf_op jit(solution)/shard_map/ppermute | solution.py:367
  64.0 5.3 %collective-permute-start.26 = (bf16[32,4224]{1,0:T(8,128)(2,1)S(1)}, bf16[32,4224]{1,0:T(8,128)(2,1)S(1)}, u32[]{:S(2)}, u32[]{:S(2)}) collective-permute-start(bf16[32,4224]{1,0:T(8,128)(2,1)S(1)} %collective-permute-done.9.refs_1_.refs_2_), channel_id=1, source_target_pairs={{0,1},{1,0},{2,3},{3,2},{4,5},{5,4},{6,7},{7,6},{8,9},{9,8},{10,11... | collective-permute-start | bytes 811016 | tf_op jit(solution)/shard_map/ppermute | solution.py:367
  68.0 9.2 %collective-permute-start.27 = (bf16[64,4096]{1,0:T(8,128)(2,1)S(1)}, bf16[64,4096]{1,0:T(8,128)(2,1)S(1)}, u32[]{:S(2)}, u32[]{:S(2)}) collective-permute-start(bf16[64,4096]{1,0:T(8,128)(2,1)S(1)} %add_convert_fusion.3.refs_2_), channel_id=1, source_target_pairs={{0,4},{1,3},{2,6},{3,1},{4,0},{5,7},{6,2},{7,5},{8,12},{9,11},{10,... | collective-permute-start | bytes 1572872 | tf_op jit(solution)/shard_map/ppermute | solution.py:355
  69.4 13.5 %collective-permute-start.28 = (bf16[64,4096]{1,0:T(8,128)(2,1)S(1)}, bf16[64,4096]{1,0:T(8,128)(2,1)S(1)}, u32[]{:S(2)}, u32[]{:S(2)}) collective-permute-start(bf16[64,4096]{1,0:T(8,128)(2,1)S(1)} %add_convert_fusion.2.refs_11_), channel_id=1, source_target_pairs={{0,4},{1,3},{2,6},{3,1},{4,0},{5,7},{6,2},{7,5},{8,12},{9,11},{10,... | collective-permute-start | bytes 1572872 | tf_op jit(solution)/shard_map/ppermute | solution.py:355
  70.3 1.5 %collective-permute-start.29 = (bf16[32,4224]{1,0:T(8,128)(2,1)S(1)}, bf16[32,4224]{1,0:T(8,128)(2,1)S(1)}, u32[]{:S(2)}, u32[]{:S(2)}) collective-permute-start(bf16[32,4224]{1,0:T(8,128)(2,1)S(1)} %collective-permute-done.22.refs_3_), channel_id=1, source_target_pairs={{0,1},{1,0},{2,3},{3,2},{4,5},{5,4},{6,7},{7,6},{8,9},{9,8},{10,11... | collective-permute-start | bytes 811016 | tf_op jit(solution)/shard_map/ppermute | solution.py:367
  82.9 2.7 %collective-permute-start.30 = (bf16[128,4096]{1,0:T(8,128)(2,1)S(1)}, bf16[128,4096]{1,0:T(8,128)(2,1)S(1)}, u32[]{:S(2)}, u32[]{:S(2)}) collective-permute-start(bf16[128,4096]{1,0:T(8,128)(2,1)S(1)} %get-tuple-element.125), channel_id=1, source_target_pairs={{0,1},{1,0},{2,3},{3,2},{4,5},{5,4},{6,7},{7,6},{8,9},{9,8},{10,11... | collective-permute-start | bytes 3145736 | tf_op jit(solution)/shard_map/ppermute | solution.py:367
  82.9 9.7 %collective-permute-start.33 = (bf16[32,4096]{1,0:T(8,128)(2,1)S(1)}, bf16[32,4096]{1,0:T(8,128)(2,1)S(1)}, u32[]{:S(2)}, u32[]{:S(2)}) collective-permute-start(bf16[32,4096]{1,0:T(8,128)(2,1)S(1)} %attend.4.refs_0_), channel_id=1, source_target_pairs={{0,1},{1,0},{2,3},{3,2},{4,5},{5,4},{6,7},{7,6},{8,9},{9,8},{10,11... | collective-permute-start | bytes 786440 | tf_op jit(solution)/shard_map/ppermute | solution.py:367
  83.4 9.2 %collective-permute-start.34 = (bf16[32,4096]{1,0:T(8,128)(2,1)S(1)}, bf16[32,4096]{1,0:T(8,128)(2,1)S(1)}, u32[]{:S(2)}, u32[]{:S(2)}) collective-permute-start(bf16[32,4096]{1,0:T(8,128)(2,1)S(1)} %attend.5.refs_11_.refs_4_), channel_id=1, source_target_pairs={{0,1},{1,0},{2,3},{3,2},{4,5},{5,4},{6,7},{7,6},{8,9},{9,8},{10,11... | collective-permute-start | bytes 786440 | tf_op jit(solution)/shard_map/ppermute | solution.py:367
  83.4 9.3 %collective-permute-start.35 = (bf16[32,4096]{1,0:T(8,128)(2,1)S(1)}, bf16[32,4096]{1,0:T(8,128)(2,1)S(1)}, u32[]{:S(2)}, u32[]{:S(2)}) collective-permute-start(bf16[32,4096]{1,0:T(8,128)(2,1)S(1)} %attend.6.refs_12_.refs_1_), channel_id=1, source_target_pairs={{0,1},{1,0},{2,3},{3,2},{4,5},{5,4},{6,7},{7,6},{8,9},{9,8},{10,11... | collective-permute-start | bytes 786440 | tf_op jit(solution)/shard_map/ppermute | solution.py:367
  84.0 8.7 %collective-permute-start.32 = (bf16[32,4096]{1,0:T(8,128)(2,1)S(1)}, bf16[32,4096]{1,0:T(8,128)(2,1)S(1)}, u32[]{:S(2)}, u32[]{:S(2)}) collective-permute-start(bf16[32,4096]{1,0:T(8,128)(2,1)S(1)} %add_convert_fusion.11.refs_12_), channel_id=1, source_target_pairs={{0,2},{1,5},{2,0},{3,7},{4,6},{5,1},{6,4},{7,3},{8,10},{9,13},{10,... | collective-permute-start | bytes 786440 | tf_op jit(solution)/shard_map/ppermute | solution.py:355
  85.7 9.4 %collective-permute-start.31 = (bf16[64,4096]{1,0:T(8,128)(2,1)S(1)}, bf16[64,4096]{1,0:T(8,128)(2,1)S(1)}, u32[]{:S(2)}, u32[]{:S(2)}) collective-permute-start(bf16[64,4096]{1,0:T(8,128)(2,1)S(1)} %add_convert_fusion.1.refs_11_), channel_id=1, source_target_pairs={{0,4},{1,3},{2,6},{3,1},{4,0},{5,7},{6,2},{7,5},{8,12},{9,11},{10,... | collective-permute-start | bytes 1572872 | tf_op jit(solution)/shard_map/ppermute | solution.py:355
  95.1 3.1 %collective-permute-start.38 = (bf16[128,4096]{1,0:T(8,128)(2,1)S(1)}, bf16[128,4096]{1,0:T(8,128)(2,1)S(1)}, u32[]{:S(2)}, u32[]{:S(2)}) collective-permute-start(bf16[128,4096]{1,0:T(8,128)(2,1)S(1)} %get-tuple-element.137), channel_id=1, source_target_pairs={{0,1},{1,0},{2,3},{3,2},{4,5},{5,4},{6,7},{7,6},{8,9},{9,8},{10,11... | collective-permute-start | bytes 3145736 | tf_op jit(solution)/shard_map/ppermute | solution.py:367
  96.0 13.2 %collective-permute-start.37 = (bf16[32,4096]{1,0:T(8,128)(2,1)S(1)}, bf16[32,4096]{1,0:T(8,128)(2,1)S(1)}, u32[]{:S(2)}, u32[]{:S(2)}) collective-permute-start(bf16[32,4096]{1,0:T(8,128)(2,1)S(1)} %add_convert_fusion.8), channel_id=1, source_target_pairs={{0,2},{1,5},{2,0},{3,7},{4,6},{5,1},{6,4},{7,3},{8,10},{9,13},{10,... | collective-permute-start | bytes 786440 | tf_op jit(solution)/shard_map/ppermute | solution.py:355
  98.3 9.2 %collective-permute-start.39 = (bf16[64,4096]{1,0:T(8,128)(2,1)S(1)}, bf16[64,4096]{1,0:T(8,128)(2,1)S(1)}, u32[]{:S(2)}, u32[]{:S(2)}) collective-permute-start(bf16[64,4096]{1,0:T(8,128)(2,1)S(1)} %add_convert_fusion), channel_id=1, source_target_pairs={{0,4},{1,3},{2,6},{3,1},{4,0},{5,7},{6,2},{7,5},{8,12},{9,11},{10,... | collective-permute-start | bytes 1572872 | tf_op jit(solution)/shard_map/ppermute | solution.py:355
  99.7 21.0 %collective-permute-start.36 = (bf16[32,4096]{1,0:T(8,128)(2,1)S(1)}, bf16[32,4096]{1,0:T(8,128)(2,1)S(1)}, u32[]{:S(2)}, u32[]{:S(2)}) collective-permute-start(bf16[32,4096]{1,0:T(8,128)(2,1)S(1)} %add_convert_fusion.9), channel_id=1, source_target_pairs={{0,16},{1,17},{2,18},{3,19},{4,20},{5,21},{6,22},{7,23},{8,24},{9,... | collective-permute-start | bytes 786440 | tf_op jit(solution)/shard_map/ppermute | solution.py:355
  107.6 7.4 %collective-permute-start.41 = (bf16[32,4096]{1,0:T(8,128)(2,1)S(1)}, bf16[32,4096]{1,0:T(8,128)(2,1)S(1)}, u32[]{:S(2)}, u32[]{:S(2)}) collective-permute-start(bf16[32,4096]{1,0:T(8,128)(2,1)S(1)} %add_convert_fusion.6.refs_1_), channel_id=1, source_target_pairs={{0,2},{1,5},{2,0},{3,7},{4,6},{5,1},{6,4},{7,3},{8,10},{9,13},{10,... | collective-permute-start | bytes 786440 | tf_op jit(solution)/shard_map/ppermute | solution.py:355
  109.3 13.0 %collective-permute-start.43 = (bf16[32,4096]{1,0:T(8,128)(2,1)S(1)}, bf16[32,4096]{1,0:T(8,128)(2,1)S(1)}, u32[]{:S(2)}, u32[]{:S(2)}) collective-permute-start(bf16[32,4096]{1,0:T(8,128)(2,1)S(1)} %add_convert_fusion.7.refs_0_), channel_id=1, source_target_pairs={{0,24},{1,25},{2,26},{3,27},{4,28},{5,29},{6,30},{7,31},{8,16},{9,... | collective-permute-start | bytes 786440 | tf_op jit(solution)/shard_map/ppermute | solution.py:355
  114.9 5.7 %collective-permute-start.40 = (bf16[32,4096]{1,0:T(8,128)(2,1)S(1)}, bf16[32,4096]{1,0:T(8,128)(2,1)S(1)}, u32[]{:S(2)}, u32[]{:S(2)}) collective-permute-start(bf16[32,4096]{1,0:T(8,128)(2,1)S(1)} %attend.7.refs_5_), channel_id=1, source_target_pairs={{0,1},{1,0},{2,3},{3,2},{4,5},{5,4},{6,7},{7,6},{8,9},{9,8},{10,11... | collective-permute-start | bytes 786440 | tf_op jit(solution)/shard_map/ppermute | solution.py:367
  115.2 11.0 %collective-permute-start.42 = (bf16[32,4096]{1,0:T(8,128)(2,1)S(1)}, bf16[32,4096]{1,0:T(8,128)(2,1)S(1)}, u32[]{:S(2)}, u32[]{:S(2)}) collective-permute-start(bf16[32,4096]{1,0:T(8,128)(2,1)S(1)} %add_convert_fusion.5), channel_id=1, source_target_pairs={{0,8},{1,9},{2,10},{3,11},{4,12},{5,13},{6,14},{7,15},{8,0},{9,1},... | collective-permute-start | bytes 786440 | tf_op jit(solution)/shard_map/ppermute | solution.py:355
  116.4 9.8 %collective-permute-start.44 = (bf16[32,4096]{1,0:T(8,128)(2,1)S(1)}, bf16[32,4096]{1,0:T(8,128)(2,1)S(1)}, u32[]{:S(2)}, u32[]{:S(2)}) collective-permute-start(bf16[32,4096]{1,0:T(8,128)(2,1)S(1)} %add_convert_fusion.10.refs_13_), channel_id=1, source_target_pairs={{0,2},{1,5},{2,0},{3,7},{4,6},{5,1},{6,4},{7,3},{8,10},{9,13},{10,... | collective-permute-start | bytes 786440 | tf_op jit(solution)/shard_map/ppermute | solution.py:355

commit v3 on v2

--- a/solution.py
+++ b/solution.py
@@ -68,6 +68,42 @@
     )(hidden, gain, ids.T, logits.T)
 
 
+def pack_kernel(queries, new_kv, prompt, q_out, own_out):
+    rows = q_out.shape[0]
+    count = rows // STEPS
+    kv_width = new_kv.shape[2]
+    q_out[...] = queries[...].reshape(rows, q_out.shape[1])
+    own_out[:, :kv_width] = new_kv[...].reshape(rows, kv_width)
+    row = lax.broadcasted_iota(jnp.int32, (rows, count), 0) // STEPS
+    column = lax.broadcasted_iota(jnp.int32, (rows, count), 1)
+    prompts = prompt[...].reshape(1, count).astype(jnp.float32)
+    spread = jnp.where(row == column, prompts, 0.0).astype(jnp.bfloat16)
+    ones = jnp.ones((count, LANES), jnp.bfloat16)
+    own_out[:, kv_width:] = dot(spread, ones).astype(jnp.bfloat16)
+
+
+def pack(queries, new_kv, prompt, *after):
+    count, steps, q_width = queries.shape
+    rows = count * steps
+    whole = pl.BlockSpec(memory_space=pltpu.VMEM)
+
+    def kernel(q, kv, p, *refs):
+        pack_kernel(q, kv, p, *refs[-2:])
+
+    return pl.pallas_call(
+        kernel,
+        out_shape=(
+            jax.ShapeDtypeStruct((rows, q_width), queries.dtype),
+            jax.ShapeDtypeStruct((rows, new_kv.shape[2] + LANES), queries.dtype),
+        ),
+        in_specs=[whole] * 3 + [pl.BlockSpec(memory_space=pl.ANY)] * len(after),
+        out_specs=(whole, whole),
+        compiler_params=pltpu.CompilerParams(vmem_limit_bytes=10 * MIB),
+        cost_estimate=SMALL,
+        name="pack",
+    )(queries, new_kv, prompt, *after)
+
+
 def stack_kernel(top, bottom, out):
     rows = top.shape[0]
     out[:rows] = top[...]
@@ -86,24 +122,6 @@
         cost_estimate=SMALL,
         name="stack",
     )(top, bottom)
-
-
-def touch_kernel(lens, *refs):
-    out = refs[-1]
-    for i in range(lens.shape[0]):
-        out[i] = lens[i]
-
-
-def touch(lens, *arrays):
-    scalars = pl.BlockSpec(memory_space=pltpu.SMEM)
-    return pl.pallas_call(
-        touch_kernel,
-        out_shape=jax.ShapeDtypeStruct(lens.shape, lens.dtype),
-        in_specs=[scalars] + [pl.BlockSpec(memory_space=pl.ANY)] * len(arrays),
-        out_specs=scalars,
-        cost_estimate=SMALL,
-        name="touch",
-    )(lens, *arrays)
 
 
 def rank_rows(match, rows):
@@ -370,12 +388,10 @@
     tokens = hidden.shape[0]
     sync = lax.optimization_barrier
     token = norm_message(hidden, norm_gain, route_ids, route_logits)
-    token, queries, new_kv = sync((token, queries, new_kv))
-    prompt_lens = touch(prompt_lens, token, prompt_kv, down)
-    new_kv, prompt_lens = sync((new_kv, prompt_lens))
-    marks = jnp.broadcast_to(sample_prompt.astype(jnp.bfloat16)[:, None, None], (count, STEPS, LANES))
-    q_mine = queries.reshape(rows, q_width)
-    own_mine = jnp.concatenate([new_kv, marks], axis=2).reshape(rows, -1)
+    level_2, level_1 = far(token, 2), far(token, 1)
+    first_0, cross_0 = near(token), cross(token)
+    third_0 = cross(first_0)
+    q_mine, own_mine = pack(queries, new_kv, sample_prompt, token)
     q_both = (q_mine, beside(q_mine))
     own_both = (own_mine, beside(own_mine))
 
@@ -409,65 +425,68 @@
     def narrow(value):
         return value.astype(jnp.bfloat16)
 
-    level_2, level_1 = far(token, 2), far(token, 1)
-    first_0, cross_0 = near(token), cross(token)
-    third_0 = cross(first_0)
-    level_2, level_1, prompt_lens = sync((level_2, level_1, prompt_lens))
+    context_0a = attend_half(0, 0)
+    own_0 = token
+    context_0a, level_2, level_1, own_0, first_0, third_0 = sync(
+        (context_0a, level_2, level_1, own_0, first_0, third_0)
+    )
     pair = stack(level_2, level_1)
     level_3 = far(level_2, 1)
-    context_0a = attend_half(0, 0, pair, first_0, cross_0)
-    context_0a, third_0, level_3 = sync((context_0a, third_0, level_3))
-    pieces_0 = with_fan([token, first_0, cross_0, third_0])
-    context_0b = attend_half(0, 1, context_0a)
-    context_0b, first_p, cross_p, *pieces_0 = sync(
-        (context_0b, near(pair), cross(pair), *pieces_0)
-    )
+    pieces_0 = with_fan([own_0, first_0, cross_0, third_0])
+    context_0b = attend_half(0, 1, context_0a, pair)
+    context_0b, level_3, *pieces_0 = sync((context_0b, level_3, *pieces_0))
+    result_0 = expert(pieces_0, 0, context_0b)
+
+    first_p, cross_p, result_0 = sync((near(pair), cross(pair), result_0))
+    back_0 = beside(result_0[2])
     third_p = cross(first_p)
     first_3, cross_3 = near(level_3), cross(level_3)
     fans_p = [beside(value) for value in (pair, first_p, cross_p)]
-    result_0 = expert(pieces_0, 0, context_0b, first_p)
-
-    third_p, result_0, *fans_p = sync((third_p, result_0, *fans_p))
-    back_0 = beside(result_0[2])
+    context_1a = attend_half(1, 0, first_p)
+    context_1a, third_p, *fans_p = sync((context_1a, third_p, *fans_p))
     pieces_p = [pair, first_p, cross_p, third_p, *fans_p, beside(third_p)]
-    result_2 = expert(pieces_p, 0, result_0[0])
-
-    first_3, cross_3, back_0, result_2 = sync((first_3, cross_3, back_0, result_2))
+    result_2 = expert(pieces_p, 0, context_1a)
+
+    sent = [beside(value) for value in (context_0a, context_0b)]
+    first_3, cross_3, back_0, result_2, *sent = sync(
+        (first_3, cross_3, back_0, result_2, *sent)
+    )
     back_2 = beside(result_2[2])
     third_3 = cross(first_3)
     fans_3 = [beside(value) for value in (level_3, first_3, cross_3)]
-    there_0 = sum_cores(result_0, back_0)
-    context_1a = attend_half(1, 0, first_3, cross_3, there_0)
-    context_1a, third_3, back_2, *fans_3 = sync((context_1a, third_3, back_2, *fans_3))
+    context_1b = attend_half(1, 1, first_3, cross_3)
+    context_1b, third_3, back_2, *fans_3 = sync((context_1b, third_3, back_2, *fans_3))
     pieces_3 = [level_3, first_3, cross_3, third_3, *fans_3, beside(third_3)]
     there_2 = sum_cores(result_2, back_2)
-    result_3 = expert(pieces_3, 0, there_2, context_1a)
-
-    turned_0, turned_2, result_3 = sync((cross(there_0), cross(there_2), result_3))
+    back_0, there_2 = sync((back_0, there_2))
+    there_0 = sum_cores(result_0, back_0)
+    result_3 = expert(pieces_3, 0, there_2, there_0)
+
+    turned_2, result_3, sent_1a = sync((cross(there_2), result_3, beside(context_1a)))
     back_3 = beside(result_3[2])
     held_2, passed_2 = sum_cross(result_2, back_2, turned_2)
     there_3 = sum_cores(result_3, back_3)
-    held_0, passed_0 = sum_cross(result_0, back_0, turned_0)
-    result_1 = expert(pieces_p, tokens, there_3, passed_2, passed_0)
-
-    contexts = [context_0a, context_0b, context_1a]
-    sent = [beside(value) for value in contexts]
-    turned_3, ended_2, result_1, *sent = sync((cross(there_3), near(passed_2), result_1, *sent))
+    result_1 = expert(pieces_p, tokens, there_3, passed_2)
+
+    contexts = [context_0a, context_0b, context_1a, context_1b]
+    turned_0, turned_3, ended_2, result_1, sent_1b = sync(
+        (cross(there_0), cross(there_3), near(passed_2), result_1, beside(context_1b))
+    )
+    sent = [*sent, sent_1a, sent_1b]
     far_2 = far(narrow(held_2 + widen(ended_2)), 2)
     back_1 = beside(result_1[2])
     held_3, passed_3 = sum_cross(result_3, back_3, turned_3)
+    held_0, passed_0 = sum_cross(result_0, back_0, turned_0)
     there_1 = sum_cores(result_1, back_1)
     total_3 = narrow(held_3 + widen(near(passed_3)))
     far_3 = far(total_3, 3)
-    held_1, passed_1 = sum_cross(result_1, back_1, cross(there_1))
-    context_1b = attend_half(1, 1, total_3, passed_1)
-
+    ordered = [contexts[0], contexts[2], sent[0], sent[2], contexts[1], contexts[3], sent[1], sent[3]]
+    own_late, _ = sync((own_mine, total_3))
+    context = place_context(own_late, ordered, jax.ShapeDtypeStruct(queries.shape, jnp.bfloat16))
+    turned_1, context, far_2 = sync((cross(there_1), context, far_2))
+    held_1, passed_1 = sum_cross(result_1, back_1, turned_1)
+    passed_1, passed_0 = sync((passed_1, passed_0))
     far_1 = far(narrow(held_1 + widen(near(passed_1))), 1)
-    contexts, sent = contexts + [context_1b], sent + [beside(context_1b)]
-    ordered = [contexts[0], contexts[2], sent[0], sent[2], contexts[1], contexts[3], sent[1], sent[3]]
-    own_late, far_2 = sync((own_mine, far_2))
-    context = place_context(own_late, ordered, jax.ShapeDtypeStruct(queries.shape, jnp.bfloat16))
-    context, far_1, far_3 = sync((context, far_1, far_3))
     total = held_0 + widen(near(passed_0)) + widen(far_1)
     expert_out = narrow(total + widen(far_2) + widen(far_3))
     return (context, expert_out)

time: 127 us -> 132 us (1.039)
  waiting for transfers between devices: 34.1 us -> 43.1 us
  starting transfers between devices: 39.3 us -> 34.7 us
    ppermute x23, waiting for transfers between devices: 30.9 us -> 38.9 us  [swap(): return lax.ppermute(value, ('ep', 'fan'), pairs)]
    unnamed x24, local copies, waits for them, and re-layouts: 5.67 us -> 8.43 us
    ppermute x22, starting transfers between devices: 5.64 us -> 3.33 us  [beside(): return lax.ppermute(value, 'fan', [(0, 1), (1, 0)])]
    ppermute x23, starting transfers between devices: 33.6 us -> 31.4 us  [swap(): return lax.ppermute(value, ('ep', 'fan'), pairs)]
    reshape x2 -> x0, local copies, waits for them, and re-layouts: 1.56 us -> none  [the longest x1 1.5 us: on_device(): q_mine = queries.reshape(rows, q_width)]
  transfers between devices with their start and end apart: 45 -> 45, of which waited for: 13 -> 20; matrix products, arithmetic and copies ran while one was open for 1% -> 1% of each run, Pallas kernels for 32% -> 30%
where the time goes in v3:
time: 132 us; the launch traced here: 131 us
  waiting for transfers between devices  43.1 us (33%)
  Pallas kernels  42 us (32%)
  starting transfers between devices  34.7 us (26%)
  local copies, waits for them, and re-layouts  8.43 us (6%)
  other arithmetic  2.23 us (2%)
    ppermute x23, waiting for transfers between devices, swap(): return lax.ppermute(value, ('ep', 'fan'), pairs)  38.9 us
    ppermute x23, starting transfers between devices, swap(): return lax.ppermute(value, ('ep', 'fan'), pairs)  31.4 us
    pallas_call x4, Pallas kernels, expert_chunk(): pl.pallas_call(functools.partial(expert_kernel, count, at_row, tokens), o...  22.8 us
    pallas_call x4, Pallas kernels, attend(): pl.pallas_call(functools.partial(attend_kernel, local, heads), out_shape=...  15.2 us
    unnamed x24, local copies, waits for them, and re-layouts  8.43 us
    ppermute x22, waiting for transfers between devices, beside(): return lax.ppermute(value, 'fan', [(0, 1), (1, 0)])  4.24 us
    ppermute x22, starting transfers between devices, beside(): return lax.ppermute(value, 'fan', [(0, 1), (1, 0)])  3.33 us
  transfers between devices with their start and end apart: 45, of which 20 were waited for; matrix products, arithmetic and copies ran while one was open for 1% of the time, Pallas kernels for 30%

profile of v3, /device:TPU:0, one launch (start us, length us, event | category | flops | bytes accessed | tf_op | source)
XLA Modules:
  0.0 131.4 jit_solution(2805430702825582524)
XLA Ops:
  0.6 2.1 %norm_message.1.refs_0_ = bf16[32,4224]{1,0:T(8,128)(2,1)} custom-call(bf16[32,4096]{1,0:T(8,128)(2,1)} %hidden_ref.1, bf16[4096]{0:T(1024)(128)(2,1)} %gain_ref.1, s32[8,32]{1,0:T(8,128)} %bitcast.21, f32[8,32]{1,0:T(8,128)} %bitcast.22), custom_call_target="tpu_custom_call" | custom-call | flops 1048576 | bytes 16384 | tf_op jit(solution)/shard_map/norm_message/pallas_call | solution.py:63
  2.7 1.2 copy-done.4
  3.9 0.9 copy-done.5
  4.9 0.7 copy-done.7
  5.8 0.5 collective-permute-start
  6.2 2.5 %collective-permute-start.4 = (bf16[32,4224]{1,0:T(8,128)(2,1)}, bf16[32,4224]{1,0:T(8,128)(2,1)S(1)}, u32[]{:S(2)}, u32[]{:S(2)}) collective-permute-start(bf16[32,4224]{1,0:T(8,128)(2,1)} %norm_message.1.refs_0_), channel_id=1, source_target_pairs={{0,2},{1,5},{2,0},{3,7},{4,6},{5,1},{6,4},{7,3},{8,10},{9,13},{10,... | collective-permute-start | bytes 811016 | tf_op jit(solution)/shard_map/ppermute | solution.py:373
  9.0 1.3 collective-permute-start.9
  10.3 2.6 %collective-permute-start.2 = (bf16[32,4224]{1,0:T(8,128)(2,1)}, bf16[32,4224]{1,0:T(8,128)(2,1)S(1)}, u32[]{:S(2)}, u32[]{:S(2)}) collective-permute-start(bf16[32,4224]{1,0:T(8,128)(2,1)} %norm_message.1.refs_0_), channel_id=1, source_target_pairs={{0,16},{1,17},{2,18},{3,19},{4,20},{5,21},{6,22},{7,23},{8,24},{9,... | collective-permute-start | bytes 811016 | tf_op jit(solution)/shard_map/ppermute | solution.py:373
  12.8 1.6 %collective-permute-start.3 = (bf16[32,4224]{1,0:T(8,128)(2,1)}, bf16[32,4224]{1,0:T(8,128)(2,1)S(1)}, u32[]{:S(2)}, u32[]{:S(2)}) collective-permute-start(bf16[32,4224]{1,0:T(8,128)(2,1)} %norm_message.1.refs_0_), channel_id=1, source_target_pairs={{0,8},{1,9},{2,10},{3,11},{4,12},{5,13},{6,14},{7,15},{8,0},{9,1},... | collective-permute-start | bytes 811016 | tf_op jit(solution)/shard_map/ppermute | solution.py:373
  14.4 0.8 collective-permute-done.4.refs_1_
  15.2 2.2 %collective-permute-start.5 = (bf16[32,4224]{1,0:T(8,128)(2,1)S(1)}, bf16[32,4224]{1,0:T(8,128)(2,1)S(1)}, u32[]{:S(2)}, u32[]{:S(2)}) collective-permute-start(bf16[32,4224]{1,0:T(8,128)(2,1)S(1)} %collective-permute-done.4.refs_1_), channel_id=1, source_target_pairs={{0,4},{1,3},{2,6},{3,1},{4,0},{5,7},{6,2},{7,5},{8,12},{9,11},{10,... | collective-permute-start | bytes 811016 | tf_op jit(solution)/shard_map/ppermute | solution.py:373
  17.4 2.2 %copy-done.2 = bf16[2,1024,1024]{2,1,0:T(8,128)(2,1)S(1)} copy-done((bf16[2,1024,1024]{2,1,0:T(8,128)(2,1)S(1)}, bf16[2,1024,1024]{2,1,0:T(8,128)(2,1)}, u32[]{:S(2)}) %copy-start.2) | copy-done | bytes 4194328
  19.6 0.7 copy-done.6
  20.2 3.8 %attend.4.refs_0_ = bf16[32,4096]{1,0:T(8,128)(2,1)S(1)} custom-call(s32[4]{0:T(128)S(1)} %copy-done.6, bf16[64,8192]{1,0:T(8,128)(2,1)S(1)} %get-tuple-element.76.q_mine, bf16[64,8192]{1,0:T(8,128)(2,1)S(1)} %collective-permute-done.q_other, bf16[64,1152]{1,0:T(8,128)(2,1)S(1)} %get-tuple-element.136.o_mine, ...), custom_call_target="tpu_custom_call" | custom-call | flops 1048576 | bytes 16384 | tf_op jit(solution)/shard_map/attend/pallas_call | solution.py:223
  24.0 1.5 %collective-permute-done.2.top = bf16[32,4224]{1,0:T(8,128)(2,1)S(1)} collective-permute-done((bf16[32,4224]{1,0:T(8,128)(2,1)}, bf16[32,4224]{1,0:T(8,128)(2,1)S(1)}, u32[]{:S(2)}, u32[]{:S(2)}) %collective-permute-start.2) | collective-permute-done | bytes 270368 | tf_op jit(solution)/shard_map/ppermute | solution.py:373
  25.8 1.3 collective-permute-start.6
  27.1 1.1 collective-permute-start.7
  28.2 0.5 collective-permute-start.13
  28.7 1.4 %collective-permute-start.8 = (bf16[32,4224]{1,0:T(8,128)(2,1)S(1)}, bf16[32,4224]{1,0:T(8,128)(2,1)S(1)}, u32[]{:S(2)}, u32[]{:S(2)}) collective-permute-start(bf16[32,4224]{1,0:T(8,128)(2,1)S(1)} %collective-permute-done.2.top), channel_id=1, source_target_pairs={{0,8},{1,9},{2,10},{3,11},{4,12},{5,13},{6,14},{7,15},{8,0},{9,1},... | collective-permute-start | bytes 811016 | tf_op jit(solution)/shard_map/ppermute | solution.py:373
  30.2 3.8 %attend.5.refs_11_.refs_4_ = bf16[32,4096]{1,0:T(8,128)(2,1)S(1)} custom-call(s32[4]{0:T(128)S(1)} %copy-done.6, bf16[64,8192]{1,0:T(8,128)(2,1)S(1)} %get-tuple-element.76.q_mine, bf16[64,8192]{1,0:T(8,128)(2,1)S(1)} %collective-permute-done.q_other, bf16[64,1152]{1,0:T(8,128)(2,1)S(1)} %get-tuple-element.136.o_mine, ...), custom_call_target="tpu_custom_call" | custom-call | flops 1048576 | bytes 16384 | tf_op jit(solution)/shard_map/attend/pallas_call | solution.py:223
  34.1 3.1 %collective-permute-done.8.refs_0_ = bf16[32,4224]{1,0:T(8,128)(2,1)S(1)} collective-permute-done((bf16[32,4224]{1,0:T(8,128)(2,1)S(1)}, bf16[32,4224]{1,0:T(8,128)(2,1)S(1)}, u32[]{:S(2)}, u32[]{:S(2)}) %collective-permute-start.8) | collective-permute-done | bytes 270368 | tf_op jit(solution)/shard_map/ppermute | solution.py:373
  37.2 2.8 %copy-done.1 = bf16[1,768,4096]{2,1,0:T(8,128)(2,1)S(1)} copy-done((bf16[1,768,4096]{2,1,0:T(8,128)(2,1)S(1)}, bf16[1,768,4096]{2,1,0:T(8,128)(2,1)}, u32[]{:S(2)}) %copy-start.1) | copy-done | bytes 6291480
  40.0 6.3 %expert_chunk.4 = (bf16[64,4096]{1,0:T(8,128)(2,1)S(1)}, bf16[64,4096]{1,0:T(8,128)(2,1)S(1)}, bf16[128,4096]{1,0:T(8,128)(2,1)S(1)}) custom-call(bf16[32,4224]{1,0:T(8,128)(2,1)} %norm_message.1.refs_0_, bf16[32,4224]{1,0:T(8,128)(2,1)S(1)} %collective-permute-done.4.refs_1_, bf16[32,4224]{1,0:T(8,128)(2,1)S(1)} %collective-permute-done.9.refs_2_, ...), custom_call_target="tpu_custom_call" | custom-call | flops 1048576 | bytes 16384 | tf_op jit(solution)/shard_map/expert_chunk/pallas_call | solution.py:327
  46.3 1.0 collective-permute-start.17
  47.3 0.5 collective-permute-start.20
  47.8 3.8 %attend.6.refs_11_.refs_1_ = bf16[32,4096]{1,0:T(8,128)(2,1)S(1)} custom-call(s32[4]{0:T(128)S(1)} %copy-done.6, bf16[64,8192]{1,0:T(8,128)(2,1)S(1)} %get-tuple-element.76.q_mine, bf16[64,8192]{1,0:T(8,128)(2,1)S(1)} %collective-permute-done.q_other, bf16[64,1152]{1,0:T(8,128)(2,1)S(1)} %get-tuple-element.136.o_mine, ...), custom_call_target="tpu_custom_call" | custom-call | flops 1048576 | bytes 16384 | tf_op jit(solution)/shard_map/attend/pallas_call | solution.py:223
  51.6 4.1 %collective-permute-done.17.refs_3_ = bf16[64,4224]{1,0:T(8,128)(2,1)S(1)} collective-permute-done((bf16[64,4224]{1,0:T(8,128)(2,1)S(1)}, bf16[64,4224]{1,0:T(8,128)(2,1)S(1)}, u32[]{:S(2)}, u32[]{:S(2)}) %collective-permute-start.17) | collective-permute-done | bytes 540704 | tf_op jit(solution)/shard_map/ppermute | solution.py:373
  55.7 0.6 collective-permute-start.14
  56.3 1.2 collective-permute-start.15
  57.7 0.4 collective-permute-start.23
  58.0 5.6 %expert_chunk.5 = (bf16[64,4096]{1,0:T(8,128)(2,1)S(1)}, bf16[64,4096]{1,0:T(8,128)(2,1)S(1)}, bf16[128,4096]{1,0:T(8,128)(2,1)S(1)}) custom-call(bf16[64,4224]{1,0:T(8,128)(2,1)S(1)} %stack.1.refs_1_.refs_0_, bf16[64,4224]{1,0:T(8,128)(2,1)S(1)} %collective-permute-done.6.refs_0_.refs_1_, bf16[64,4224]{1,0:T(8,128)(2,1)S(1)} %collective-permute-done.7.refs_2_, ...), custom_call_target="tpu_custom_call" | custom-call | flops 1048576 | bytes 16384 | tf_op jit(solution)/shard_map/expert_chunk/pallas_call | solution.py:327
  63.6 1.4 %collective-permute-done.14.refs_0_.refs_1_ = bf16[32,4224]{1,0:T(8,128)(2,1)S(1)} collective-permute-done((bf16[32,4224]{1,0:T(8,128)(2,1)S(1)}, bf16[32,4224]{1,0:T(8,128)(2,1)S(1)}, u32[]{:S(2)}, u32[]{:S(2)}) %collective-permute-start.14) | collective-permute-done | bytes 270368 | tf_op jit(solution)/shard_map/ppermute | solution.py:373
  65.1 0.4 collective-permute-start.26
  65.5 0.8 collective-permute-start.24
  66.3 0.5 collective-permute-start.28
  66.8 3.8 %attend.7.refs_5_ = bf16[32,4096]{1,0:T(8,128)(2,1)S(1)} custom-call(s32[4]{0:T(128)S(1)} %copy-done.6, bf16[64,8192]{1,0:T(8,128)(2,1)S(1)} %get-tuple-element.76.q_mine, bf16[64,8192]{1,0:T(8,128)(2,1)S(1)} %collective-permute-done.q_other, bf16[64,1152]{1,0:T(8,128)(2,1)S(1)} %get-tuple-element.136.o_mine, ...), custom_call_target="tpu_custom_call" | custom-call | flops 1048576 | bytes 16384 | tf_op jit(solution)/shard_map/attend/pallas_call | solution.py:223
  70.7 1.3 collective-permute-done.24.refs_3_
  72.2 0.8 collective-permute-start.30
  73.2 0.6 collective-permute-done.31.refs_7_
  73.8 5.3 %expert_chunk.6 = (bf16[64,4096]{1,0:T(8,128)(2,1)S(1)}, bf16[64,4096]{1,0:T(8,128)(2,1)S(1)}, bf16[128,4096]{1,0:T(8,128)(2,1)S(1)}) custom-call(bf16[32,4224]{1,0:T(8,128)(2,1)S(1)} %collective-permute-done.8.refs_0_, bf16[32,4224]{1,0:T(8,128)(2,1)S(1)} %collective-permute-done.14.refs_0_.refs_1_, ...), custom_call_target="tpu_custom_call" | custom-call | flops 1048576 | bytes 16384 | tf_op jit(solution)/shard_map/expert_chunk/pallas_call | solution.py:327
  79.1 2.3 %collective-permute-done.30 = bf16[64,4096]{1,0:T(8,128)(2,1)S(1)} collective-permute-done((bf16[64,4096]{1,0:T(8,128)(2,1)S(1)}, bf16[64,4096]{1,0:T(8,128)(2,1)S(1)}, u32[]{:S(2)}, u32[]{:S(2)}) %collective-permute-start.30) | collective-permute-done | bytes 524320 | tf_op jit(solution)/shard_map/ppermute | solution.py:373
  81.5 0.8 collective-permute-start.29
  82.3 1.9 %collective-permute-done.33 = bf16[128,4096]{1,0:T(8,128)(2,1)S(1)} collective-permute-done((bf16[128,4096]{1,0:T(8,128)(2,1)S(1)}, bf16[128,4096]{1,0:T(8,128)(2,1)S(1)}, u32[]{:S(2)}, u32[]{:S(2)}) %collective-permute-start.33) | collective-permute-done | bytes 1048608 | tf_op jit(solution)/shard_map/ppermute | solution.py:385
  84.3 0.8 collective-permute-start.34
  85.2 1.1 collective-permute-start.35
  86.3 5.6 %expert_chunk.7 = (bf16[64,4096]{1,0:T(8,128)(2,1)S(1)}, bf16[64,4096]{1,0:T(8,128)(2,1)S(1)}, bf16[128,4096]{1,0:T(8,128)(2,1)S(1)}) custom-call(bf16[64,4224]{1,0:T(8,128)(2,1)S(1)} %stack.1.refs_1_.refs_0_, bf16[64,4224]{1,0:T(8,128)(2,1)S(1)} %collective-permute-done.6.refs_0_.refs_1_, bf16[64,4224]{1,0:T(8,128)(2,1)S(1)} %collective-permute-done.7.refs_2_, ...), custom_call_target="tpu_custom_call" | custom-call | flops 1048576 | bytes 16384 | tf_op jit(solution)/shard_map/expert_chunk/pallas_call | solution.py:327
  91.9 1.5 %collective-permute-done.29 = bf16[64,4096]{1,0:T(8,128)(2,1)S(1)} collective-permute-done((bf16[64,4096]{1,0:T(8,128)(2,1)S(1)}, bf16[64,4096]{1,0:T(8,128)(2,1)S(1)}, u32[]{:S(2)}, u32[]{:S(2)}) %collective-permute-start.29) | collective-permute-done | bytes 524320 | tf_op jit(solution)/shard_map/ppermute | solution.py:373
  93.5 1.0 collective-permute-done.35
  94.5 4.6 %collective-permute-done.34 = bf16[64,4096]{1,0:T(8,128)(2,1)S(1)} collective-permute-done((bf16[64,4096]{1,0:T(8,128)(2,1)S(1)}, bf16[64,4096]{1,0:T(8,128)(2,1)S(1)}, u32[]{:S(2)}, u32[]{:S(2)}) %collective-permute-start.34) | collective-permute-done | bytes 524320 | tf_op jit(solution)/shard_map/ppermute | solution.py:373
  99.2 1.8 %collective-permute-start.40 = (bf16[32,4096]{1,0:T(8,128)(2,1)S(1)}, bf16[32,4096]{1,0:T(8,128)(2,1)S(1)}, u32[]{:S(2)}, u32[]{:S(2)}) collective-permute-start(bf16[32,4096]{1,0:T(8,128)(2,1)S(1)} %add_convert_fusion.8), channel_id=1, source_target_pairs={{0,16},{1,17},{2,18},{3,19},{4,20},{5,21},{6,22},{7,23},{8,24},{9,... | collective-permute-start | bytes 786440 | tf_op jit(solution)/shard_map/ppermute | solution.py:373
  101.1 0.8 collective-permute-start.39
  102.1 1.6 %collective-permute-done.37 = bf16[128,4096]{1,0:T(8,128)(2,1)S(1)} collective-permute-done((bf16[128,4096]{1,0:T(8,128)(2,1)S(1)}, bf16[128,4096]{1,0:T(8,128)(2,1)S(1)}, u32[]{:S(2)}, u32[]{:S(2)}) %collective-permute-start.37) | collective-permute-done | bytes 1048608 | tf_op jit(solution)/shard_map/ppermute | solution.py:385
  103.8 1.7 %collective-permute-start.38 = (bf16[64,4096]{1,0:T(8,128)(2,1)S(1)}, bf16[64,4096]{1,0:T(8,128)(2,1)S(1)}, u32[]{:S(2)}, u32[]{:S(2)}) collective-permute-start(bf16[64,4096]{1,0:T(8,128)(2,1)S(1)} %add_convert_fusion), channel_id=1, source_target_pairs={{0,4},{1,3},{2,6},{3,1},{4,0},{5,7},{6,2},{7,5},{8,12},{9,11},{10,... | collective-permute-start | bytes 1572872 | tf_op jit(solution)/shard_map/ppermute | solution.py:373
  105.5 3.0 %collective-permute-done.39 = bf16[32,4096]{1,0:T(8,128)(2,1)S(1)} collective-permute-done((bf16[32,4096]{1,0:T(8,128)(2,1)S(1)}, bf16[32,4096]{1,0:T(8,128)(2,1)S(1)}, u32[]{:S(2)}, u32[]{:S(2)}) %collective-permute-start.39) | collective-permute-done | bytes 262176 | tf_op jit(solution)/shard_map/ppermute | solution.py:373
  108.6 1.6 %place_context.1 = bf16[32,2,8192]{2,1,0:T(2,128)(2,1)} custom-call(bf16[64,1152]{1,0:T(8,128)(2,1)S(1)} %get-tuple-element.136.o_mine, bf16[32,4096]{1,0:T(8,128)(2,1)S(1)} %attend.4.refs_0_, bf16[32,4096]{1,0:T(8,128)(2,1)S(1)} %attend.6.refs_11_.refs_1_, bf16[32,4096]{1,0:T(8,128)(2,1)S(1)} %collective-permute-done.22.refs_2_, ...), custom_call_target="tpu_custom_call" | custom-call | flops 1048576 | bytes 16384 | tf_op jit(solution)/shard_map/place_context/pallas_call | solution.py:273
  110.2 3.5 %collective-permute-done.40 = bf16[32,4096]{1,0:T(8,128)(2,1)S(1)} collective-permute-done((bf16[32,4096]{1,0:T(8,128)(2,1)S(1)}, bf16[32,4096]{1,0:T(8,128)(2,1)S(1)}, u32[]{:S(2)}, u32[]{:S(2)}) %collective-permute-start.40) | collective-permute-done | bytes 262176 | tf_op jit(solution)/shard_map/ppermute | solution.py:373
  113.8 0.4 collective-permute-start.42
  114.2 3.0 %collective-permute-start.44 = (bf16[32,4096]{1,0:T(8,128)(2,1)S(1)}, bf16[32,4096]{1,0:T(8,128)(2,1)S(1)}, u32[]{:S(2)}, u32[]{:S(2)}) collective-permute-start(bf16[32,4096]{1,0:T(8,128)(2,1)S(1)} %add_convert_fusion.9), channel_id=1, source_target_pairs={{0,24},{1,25},{2,26},{3,27},{4,28},{5,29},{6,30},{7,31},{8,16},{9,... | collective-permute-start | bytes 786440 | tf_op jit(solution)/shard_map/ppermute | solution.py:373
  117.3 1.2 collective-permute-start.41
  118.5 1.7 %collective-permute-done.42 = bf16[32,4096]{1,0:T(8,128)(2,1)S(1)} collective-permute-done((bf16[32,4096]{1,0:T(8,128)(2,1)S(1)}, bf16[32,4096]{1,0:T(8,128)(2,1)S(1)}, u32[]{:S(2)}, u32[]{:S(2)}) %collective-permute-start.42) | collective-permute-done | bytes 262176 | tf_op jit(solution)/shard_map/ppermute | solution.py:373
  120.3 1.2 collective-permute-start.43
  121.6 3.6 %collective-permute-done.44 = bf16[32,4096]{1,0:T(8,128)(2,1)S(1)} collective-permute-done((bf16[32,4096]{1,0:T(8,128)(2,1)S(1)}, bf16[32,4096]{1,0:T(8,128)(2,1)S(1)}, u32[]{:S(2)}, u32[]{:S(2)}) %collective-permute-start.44) | collective-permute-done | bytes 262176 | tf_op jit(solution)/shard_map/ppermute | solution.py:373
  125.2 5.2 %collective-permute-done.43 = bf16[32,4096]{1,0:T(8,128)(2,1)S(1)} collective-permute-done((bf16[32,4096]{1,0:T(8,128)(2,1)S(1)}, bf16[32,4096]{1,0:T(8,128)(2,1)S(1)}, u32[]{:S(2)}, u32[]{:S(2)}) %collective-permute-start.43) | collective-permute-done | bytes 262176 | tf_op jit(solution)/shard_map/ppermute | solution.py:373
  130.4 0.9 add_convert_fusion.4
  (76 shorter events, 2.6 us)
Async XLA Ops:
  0.6 57.4 %slice-start.2 = ((s8[6291456]{0:T(1024)(128)(4,1)}), s8[2097152]{0:T(1024)(128)(4,1)S(1)}, s32[]{:S(2)}) async-start(s8[6291456]{0:T(1024)(128)(4,1)} %bitcast.16), calls=%async_computation.2 | async-start | bytes 4194304
  2.7 1.2 copy-start.4
  3.9 0.9 copy-start.5
  4.8 0.7 copy-start.7
  5.8 11.6 %collective-permute-start = (bf16[64,8192]{1,0:T(8,128)(2,1)S(1)}, bf16[64,8192]{1,0:T(8,128)(2,1)S(1)}, u32[]{:S(2)}, u32[]{:S(2)}) collective-permute-start(bf16[64,8192]{1,0:T(8,128)(2,1)S(1)} %get-tuple-element.76.q_mine), channel_id=1, source_target_pairs={{0,1},{1,0},{2,3},{3,2},{4,5},{5,4},{6,7},{7,6},{8,9},{9,8},{10,11... | collective-permute-start | bytes 3145736 | tf_op jit(solution)/shard_map/ppermute | solution.py:385
  6.2 9.0 %collective-permute-start.4 = (bf16[32,4224]{1,0:T(8,128)(2,1)}, bf16[32,4224]{1,0:T(8,128)(2,1)S(1)}, u32[]{:S(2)}, u32[]{:S(2)}) collective-permute-start(bf16[32,4224]{1,0:T(8,128)(2,1)} %norm_message.1.refs_0_), channel_id=1, source_target_pairs={{0,2},{1,5},{2,0},{3,7},{4,6},{5,1},{6,4},{7,3},{8,10},{9,13},{10,... | collective-permute-start | bytes 811016 | tf_op jit(solution)/shard_map/ppermute | solution.py:373
  8.7 28.5 %slice-start = ((s8[6291456]{0:T(1024)(128)(4,1)}), s8[4194304]{0:T(1024)(128)(4,1)S(1)}, s32[]{:S(2)}) async-start(s8[6291456]{0:T(1024)(128)(4,1)} %bitcast.5), calls=%async_computation | async-start | bytes 8388608
  8.7 28.5 %copy-start = (bf16[1,4096,768]{2,1,0:T(8,128)(2,1)S(1)}, bf16[1,4096,768]{2,1,0:T(8,128)(2,1)}, u32[]{:S(2)}) copy-start(bf16[1,4096,768]{2,1,0:T(8,128)(2,1)} %param.22) | copy-start | bytes 18874372
  8.7 4.1 %collective-permute-start.1 = (bf16[64,1152]{1,0:T(8,128)(2,1)S(1)}, bf16[64,1152]{1,0:T(8,128)(2,1)S(1)}, u32[]{:S(2)}, u32[]{:S(2)}) collective-permute-start(bf16[64,1152]{1,0:T(8,128)(2,1)S(1)} %get-tuple-element.136.o_mine), channel_id=1, source_target_pairs={{0,1},{1,0},{2,3},{3,2},{4,5},{5,4},{6,7},{7,6},{8,9},{9,8},{10,11... | collective-permute-start | bytes 442376 | tf_op jit(solution)/shard_map/ppermute | solution.py:385
  9.0 8.4 %collective-permute-start.9 = (bf16[32,4224]{1,0:T(8,128)(2,1)}, bf16[32,4224]{1,0:T(8,128)(2,1)S(1)}, u32[]{:S(2)}, u32[]{:S(2)}) collective-permute-start(bf16[32,4224]{1,0:T(8,128)(2,1)} %norm_message.1.refs_0_), channel_id=1, source_target_pairs={{0,4},{1,3},{2,6},{3,1},{4,0},{5,7},{6,2},{7,5},{8,12},{9,11},{10,... | collective-permute-start | bytes 811016 | tf_op jit(solution)/shard_map/ppermute | solution.py:373
  10.3 15.3 %collective-permute-start.2 = (bf16[32,4224]{1,0:T(8,128)(2,1)}, bf16[32,4224]{1,0:T(8,128)(2,1)S(1)}, u32[]{:S(2)}, u32[]{:S(2)}) collective-permute-start(bf16[32,4224]{1,0:T(8,128)(2,1)} %norm_message.1.refs_0_), channel_id=1, source_target_pairs={{0,16},{1,17},{2,18},{3,19},{4,20},{5,21},{6,22},{7,23},{8,24},{9,... | collective-permute-start | bytes 811016 | tf_op jit(solution)/shard_map/ppermute | solution.py:373
  12.8 12.9 %collective-permute-start.3 = (bf16[32,4224]{1,0:T(8,128)(2,1)}, bf16[32,4224]{1,0:T(8,128)(2,1)S(1)}, u32[]{:S(2)}, u32[]{:S(2)}) collective-permute-start(bf16[32,4224]{1,0:T(8,128)(2,1)} %norm_message.1.refs_0_), channel_id=1, source_target_pairs={{0,8},{1,9},{2,10},{3,11},{4,12},{5,13},{6,14},{7,15},{8,0},{9,1},... | collective-permute-start | bytes 811016 | tf_op jit(solution)/shard_map/ppermute | solution.py:373
  15.2 10.6 %collective-permute-start.5 = (bf16[32,4224]{1,0:T(8,128)(2,1)S(1)}, bf16[32,4224]{1,0:T(8,128)(2,1)S(1)}, u32[]{:S(2)}, u32[]{:S(2)}) collective-permute-start(bf16[32,4224]{1,0:T(8,128)(2,1)S(1)} %collective-permute-done.4.refs_1_), channel_id=1, source_target_pairs={{0,4},{1,3},{2,6},{3,1},{4,0},{5,7},{6,2},{7,5},{8,12},{9,11},{10,... | collective-permute-start | bytes 811016 | tf_op jit(solution)/shard_map/ppermute | solution.py:373
  17.4 10.9 %collective-permute-start.12 = (bf16[32,4224]{1,0:T(8,128)(2,1)S(1)}, bf16[32,4224]{1,0:T(8,128)(2,1)S(1)}, u32[]{:S(2)}, u32[]{:S(2)}) collective-permute-start(bf16[32,4224]{1,0:T(8,128)(2,1)S(1)} %collective-permute-done.9.refs_2_), channel_id=1, source_target_pairs={{0,1},{1,0},{2,3},{3,2},{4,5},{5,4},{6,7},{7,6},{8,9},{9,8},{10,11... | collective-permute-start | bytes 811016 | tf_op jit(solution)/shard_map/ppermute | solution.py:385
  17.4 2.2 %copy-start.2 = (bf16[2,1024,1024]{2,1,0:T(8,128)(2,1)S(1)}, bf16[2,1024,1024]{2,1,0:T(8,128)(2,1)}, u32[]{:S(2)}) copy-start(bf16[2,1024,1024]{2,1,0:T(8,128)(2,1)} %cache.7) | copy-start | bytes 12582916
  19.6 0.7 copy-start.6
  24.0 13.2 %slice-start.1 = ((s8[6291456]{0:T(1024)(128)(4,1)}), s8[2097152]{0:T(1024)(128)(4,1)S(1)}, s32[]{:S(2)}) async-start(s8[6291456]{0:T(1024)(128)(4,1)} %bitcast.5), calls=%async_computation.1 | async-start | bytes 4194304
  25.8 3.0 %collective-permute-start.10 = (bf16[32,4224]{1,0:T(8,128)(2,1)}, bf16[32,4224]{1,0:T(8,128)(2,1)S(1)}, u32[]{:S(2)}, u32[]{:S(2)}) collective-permute-start(bf16[32,4224]{1,0:T(8,128)(2,1)} %norm_message.1.refs_0_), channel_id=1, source_target_pairs={{0,1},{1,0},{2,3},{3,2},{4,5},{5,4},{6,7},{7,6},{8,9},{9,8},{10,11... | collective-permute-start | bytes 811016 | tf_op jit(solution)/shard_map/ppermute | solution.py:385
  25.8 20.5 %collective-permute-start.6 = (bf16[64,4224]{1,0:T(8,128)(2,1)S(1)}, bf16[64,4224]{1,0:T(8,128)(2,1)S(1)}, u32[]{:S(2)}, u32[]{:S(2)}) collective-permute-start(bf16[64,4224]{1,0:T(8,128)(2,1)S(1)} %stack.1.refs_1_.refs_0_), channel_id=1, source_target_pairs={{0,2},{1,5},{2,0},{3,7},{4,6},{5,1},{6,4},{7,3},{8,10},{9,13},{10,... | collective-permute-start | bytes 1622024 | tf_op jit(solution)/shard_map/ppermute | solution.py:373
  27.1 19.2 %collective-permute-start.7 = (bf16[64,4224]{1,0:T(8,128)(2,1)S(1)}, bf16[64,4224]{1,0:T(8,128)(2,1)S(1)}, u32[]{:S(2)}, u32[]{:S(2)}) collective-permute-start(bf16[64,4224]{1,0:T(8,128)(2,1)S(1)} %stack.1.refs_1_.refs_0_), channel_id=1, source_target_pairs={{0,4},{1,3},{2,6},{3,1},{4,0},{5,7},{6,2},{7,5},{8,12},{9,11},{10,... | collective-permute-start | bytes 1622024 | tf_op jit(solution)/shard_map/ppermute | solution.py:373
  28.2 5.8 %collective-permute-start.11 = (bf16[32,4224]{1,0:T(8,128)(2,1)S(1)}, bf16[32,4224]{1,0:T(8,128)(2,1)S(1)}, u32[]{:S(2)}, u32[]{:S(2)}) collective-permute-start(bf16[32,4224]{1,0:T(8,128)(2,1)S(1)} %collective-permute-done.4.refs_1_), channel_id=1, source_target_pairs={{0,1},{1,0},{2,3},{3,2},{4,5},{5,4},{6,7},{7,6},{8,9},{9,8},{10,11... | collective-permute-start | bytes 811016 | tf_op jit(solution)/shard_map/ppermute | solution.py:385
  28.2 5.9 %collective-permute-start.13 = (bf16[32,4224]{1,0:T(8,128)(2,1)S(1)}, bf16[32,4224]{1,0:T(8,128)(2,1)S(1)}, u32[]{:S(2)}, u32[]{:S(2)}) collective-permute-start(bf16[32,4224]{1,0:T(8,128)(2,1)S(1)} %collective-permute-done.5.refs_3_), channel_id=1, source_target_pairs={{0,1},{1,0},{2,3},{3,2},{4,5},{5,4},{6,7},{7,6},{8,9},{9,8},{10,11... | collective-permute-start | bytes 811016 | tf_op jit(solution)/shard_map/ppermute | solution.py:385
  28.7 8.5 %collective-permute-start.8 = (bf16[32,4224]{1,0:T(8,128)(2,1)S(1)}, bf16[32,4224]{1,0:T(8,128)(2,1)S(1)}, u32[]{:S(2)}, u32[]{:S(2)}) collective-permute-start(bf16[32,4224]{1,0:T(8,128)(2,1)S(1)} %collective-permute-done.2.top), channel_id=1, source_target_pairs={{0,8},{1,9},{2,10},{3,11},{4,12},{5,13},{6,14},{7,15},{8,0},{9,1},... | collective-permute-start | bytes 811016 | tf_op jit(solution)/shard_map/ppermute | solution.py:373
  34.0 17.6 %collective-permute-start.18 = (bf16[64,4224]{1,0:T(8,128)(2,1)S(1)}, bf16[64,4224]{1,0:T(8,128)(2,1)S(1)}, u32[]{:S(2)}, u32[]{:S(2)}) collective-permute-start(bf16[64,4224]{1,0:T(8,128)(2,1)S(1)} %stack.1.refs_1_.refs_0_), channel_id=1, source_target_pairs={{0,1},{1,0},{2,3},{3,2},{4,5},{5,4},{6,7},{7,6},{8,9},{9,8},{10,11... | collective-permute-start | bytes 1622024 | tf_op jit(solution)/shard_map/ppermute | solution.py:385
  37.2 2.8 %copy-start.1 = (bf16[1,768,4096]{2,1,0:T(8,128)(2,1)S(1)}, bf16[1,768,4096]{2,1,0:T(8,128)(2,1)}, u32[]{:S(2)}) copy-start(bf16[1,768,4096]{2,1,0:T(8,128)(2,1)} %param.23) | copy-start | bytes 18874372
  40.0 7.8 %copy-start.3 = (bf16[2,1024,1024]{2,1,0:T(8,128)(2,1)S(1)}, bf16[2,1024,1024]{2,1,0:T(8,128)(2,1)}, u32[]{:S(2)}) copy-start(bf16[2,1024,1024]{2,1,0:T(8,128)(2,1)} %cache.7) | copy-start | bytes 12582916
  40.0 18.0 %slice-start.3 = ((s8[6291456]{0:T(1024)(128)(4,1)}), s8[4194304]{0:T(1024)(128)(4,1)S(1)}, s32[]{:S(2)}) async-start(s8[6291456]{0:T(1024)(128)(4,1)} %bitcast.16), calls=%async_computation.3 | async-start | bytes 8388608
  46.3 9.4 %collective-permute-start.17 = (bf16[64,4224]{1,0:T(8,128)(2,1)S(1)}, bf16[64,4224]{1,0:T(8,128)(2,1)S(1)}, u32[]{:S(2)}, u32[]{:S(2)}) collective-permute-start(bf16[64,4224]{1,0:T(8,128)(2,1)S(1)} %collective-permute-done.6.refs_0_.refs_1_), channel_id=1, source_target_pairs={{0,4},{1,3},{2,6},{3,1},{4,0},{5,7},{6,2},{7,5},{8,12},{9,11},{10,... | collective-permute-start | bytes 1622024 | tf_op jit(solution)/shard_map/ppermute | solution.py:373
  47.3 8.4 %collective-permute-start.19 = (bf16[64,4224]{1,0:T(8,128)(2,1)S(1)}, bf16[64,4224]{1,0:T(8,128)(2,1)S(1)}, u32[]{:S(2)}, u32[]{:S(2)}) collective-permute-start(bf16[64,4224]{1,0:T(8,128)(2,1)S(1)} %collective-permute-done.6.refs_0_.refs_1_), channel_id=1, source_target_pairs={{0,1},{1,0},{2,3},{3,2},{4,5},{5,4},{6,7},{7,6},{8,9},{9,8},{10,11... | collective-permute-start | bytes 1622024 | tf_op jit(solution)/shard_map/ppermute | solution.py:385
  47.3 8.4 %collective-permute-start.20 = (bf16[64,4224]{1,0:T(8,128)(2,1)S(1)}, bf16[64,4224]{1,0:T(8,128)(2,1)S(1)}, u32[]{:S(2)}, u32[]{:S(2)}) collective-permute-start(bf16[64,4224]{1,0:T(8,128)(2,1)S(1)} %collective-permute-done.7.refs_2_), channel_id=1, source_target_pairs={{0,1},{1,0},{2,3},{3,2},{4,5},{5,4},{6,7},{7,6},{8,9},{9,8},{10,11... | collective-permute-start | bytes 1622024 | tf_op jit(solution)/shard_map/ppermute | solution.py:385
  47.8 17.2 %collective-permute-start.16 = (bf16[128,4096]{1,0:T(8,128)(2,1)S(1)}, bf16[128,4096]{1,0:T(8,128)(2,1)S(1)}, u32[]{:S(2)}, u32[]{:S(2)}) collective-permute-start(bf16[128,4096]{1,0:T(8,128)(2,1)S(1)} %get-tuple-element.98), channel_id=1, source_target_pairs={{0,1},{1,0},{2,3},{3,2},{4,5},{5,4},{6,7},{7,6},{8,9},{9,8},{10,11... | collective-permute-start | bytes 3145736 | tf_op jit(solution)/shard_map/ppermute | solution.py:385
  55.7 1.9 %collective-permute-start.21 = (bf16[64,4224]{1,0:T(8,128)(2,1)S(1)}, bf16[64,4224]{1,0:T(8,128)(2,1)S(1)}, u32[]{:S(2)}, u32[]{:S(2)}) collective-permute-start(bf16[64,4224]{1,0:T(8,128)(2,1)S(1)} %collective-permute-done.17.refs_3_), channel_id=1, source_target_pairs={{0,1},{1,0},{2,3},{3,2},{4,5},{5,4},{6,7},{7,6},{8,9},{9,8},{10,11... | collective-permute-start | bytes 1622024 | tf_op jit(solution)/shard_map/ppermute | solution.py:385
  55.7 9.3 %collective-permute-start.14 = (bf16[32,4224]{1,0:T(8,128)(2,1)S(1)}, bf16[32,4224]{1,0:T(8,128)(2,1)S(1)}, u32[]{:S(2)}, u32[]{:S(2)}) collective-permute-start(bf16[32,4224]{1,0:T(8,128)(2,1)S(1)} %collective-permute-done.8.refs_0_), channel_id=1, source_target_pairs={{0,2},{1,5},{2,0},{3,7},{4,6},{5,1},{6,4},{7,3},{8,10},{9,13},{10,... | collective-permute-start | bytes 811016 | tf_op jit(solution)/shard_map/ppermute | solution.py:373
  56.3 8.7 %collective-permute-start.15 = (bf16[32,4224]{1,0:T(8,128)(2,1)S(1)}, bf16[32,4224]{1,0:T(8,128)(2,1)S(1)}, u32[]{:S(2)}, u32[]{:S(2)}) collective-permute-start(bf16[32,4224]{1,0:T(8,128)(2,1)S(1)} %collective-permute-done.8.refs_0_), channel_id=1, source_target_pairs={{0,4},{1,3},{2,6},{3,1},{4,0},{5,7},{6,2},{7,5},{8,12},{9,11},{10,... | collective-permute-start | bytes 811016 | tf_op jit(solution)/shard_map/ppermute | solution.py:373
  57.5 6.1 %collective-permute-start.22 = (bf16[32,4096]{1,0:T(8,128)(2,1)S(1)}, bf16[32,4096]{1,0:T(8,128)(2,1)S(1)}, u32[]{:S(2)}, u32[]{:S(2)}) collective-permute-start(bf16[32,4096]{1,0:T(8,128)(2,1)S(1)} %attend.4.refs_0_), channel_id=1, source_target_pairs={{0,1},{1,0},{2,3},{3,2},{4,5},{5,4},{6,7},{7,6},{8,9},{9,8},{10,11... | collective-permute-start | bytes 786440 | tf_op jit(solution)/shard_map/ppermute | solution.py:385
  57.7 6.0 %collective-permute-start.23 = (bf16[32,4096]{1,0:T(8,128)(2,1)S(1)}, bf16[32,4096]{1,0:T(8,128)(2,1)S(1)}, u32[]{:S(2)}, u32[]{:S(2)}) collective-permute-start(bf16[32,4096]{1,0:T(8,128)(2,1)S(1)} %attend.5.refs_11_.refs_4_), channel_id=1, source_target_pairs={{0,1},{1,0},{2,3},{3,2},{4,5},{5,4},{6,7},{7,6},{8,9},{9,8},{10,11... | collective-permute-start | bytes 786440 | tf_op jit(solution)/shard_map/ppermute | solution.py:385
  65.0 7.0 %collective-permute-start.25 = (bf16[128,4096]{1,0:T(8,128)(2,1)S(1)}, bf16[128,4096]{1,0:T(8,128)(2,1)S(1)}, u32[]{:S(2)}, u32[]{:S(2)}) collective-permute-start(bf16[128,4096]{1,0:T(8,128)(2,1)S(1)} %get-tuple-element.113), channel_id=1, source_target_pairs={{0,1},{1,0},{2,3},{3,2},{4,5},{5,4},{6,7},{7,6},{8,9},{9,8},{10,11... | collective-permute-start | bytes 3145736 | tf_op jit(solution)/shard_map/ppermute | solution.py:385
  65.1 5.5 %collective-permute-start.26 = (bf16[32,4224]{1,0:T(8,128)(2,1)S(1)}, bf16[32,4224]{1,0:T(8,128)(2,1)S(1)}, u32[]{:S(2)}, u32[]{:S(2)}) collective-permute-start(bf16[32,4224]{1,0:T(8,128)(2,1)S(1)} %collective-permute-done.8.refs_0_), channel_id=1, source_target_pairs={{0,1},{1,0},{2,3},{3,2},{4,5},{5,4},{6,7},{7,6},{8,9},{9,8},{10,11... | collective-permute-start | bytes 811016 | tf_op jit(solution)/shard_map/ppermute | solution.py:385
  65.5 6.5 %collective-permute-start.24 = (bf16[32,4224]{1,0:T(8,128)(2,1)S(1)}, bf16[32,4224]{1,0:T(8,128)(2,1)S(1)}, u32[]{:S(2)}, u32[]{:S(2)}) collective-permute-start(bf16[32,4224]{1,0:T(8,128)(2,1)S(1)} %collective-permute-done.14.refs_0_.refs_1_), channel_id=1, source_target_pairs={{0,4},{1,3},{2,6},{3,1},{4,0},{5,7},{6,2},{7,5},{8,12},{9,11},{10,... | collective-permute-start | bytes 811016 | tf_op jit(solution)/shard_map/ppermute | solution.py:373
  66.3 5.7 %collective-permute-start.27 = (bf16[32,4224]{1,0:T(8,128)(2,1)S(1)}, bf16[32,4224]{1,0:T(8,128)(2,1)S(1)}, u32[]{:S(2)}, u32[]{:S(2)}) collective-permute-start(bf16[32,4224]{1,0:T(8,128)(2,1)S(1)} %collective-permute-done.14.refs_0_.refs_1_), channel_id=1, source_target_pairs={{0,1},{1,0},{2,3},{3,2},{4,5},{5,4},{6,7},{7,6},{8,9},{9,8},{10,11... | collective-permute-start | bytes 811016 | tf_op jit(solution)/shard_map/ppermute | solution.py:385
  66.3 5.7 %collective-permute-start.28 = (bf16[32,4224]{1,0:T(8,128)(2,1)S(1)}, bf16[32,4224]{1,0:T(8,128)(2,1)S(1)}, u32[]{:S(2)}, u32[]{:S(2)}) collective-permute-start(bf16[32,4224]{1,0:T(8,128)(2,1)S(1)} %collective-permute-done.15.refs_1_.refs_2_), channel_id=1, source_target_pairs={{0,1},{1,0},{2,3},{3,2},{4,5},{5,4},{6,7},{7,6},{8,9},{9,8},{10,11... | collective-permute-start | bytes 811016 | tf_op jit(solution)/shard_map/ppermute | solution.py:385
  70.7 8.5 %collective-permute-start.32 = (bf16[32,4096]{1,0:T(8,128)(2,1)S(1)}, bf16[32,4096]{1,0:T(8,128)(2,1)S(1)}, u32[]{:S(2)}, u32[]{:S(2)}) collective-permute-start(bf16[32,4096]{1,0:T(8,128)(2,1)S(1)} %attend.6.refs_11_.refs_1_), channel_id=1, source_target_pairs={{0,1},{1,0},{2,3},{3,2},{4,5},{5,4},{6,7},{7,6},{8,9},{9,8},{10,11... | collective-permute-start | bytes 786440 | tf_op jit(solution)/shard_map/ppermute | solution.py:385
  72.2 1.6 %collective-permute-start.31 = (bf16[32,4224]{1,0:T(8,128)(2,1)S(1)}, bf16[32,4224]{1,0:T(8,128)(2,1)S(1)}, u32[]{:S(2)}, u32[]{:S(2)}) collective-permute-start(bf16[32,4224]{1,0:T(8,128)(2,1)S(1)} %collective-permute-done.24.refs_3_), channel_id=1, source_target_pairs={{0,1},{1,0},{2,3},{3,2},{4,5},{5,4},{6,7},{7,6},{8,9},{9,8},{10,11... | collective-permute-start | bytes 811016 | tf_op jit(solution)/shard_map/ppermute | solution.py:385
  72.2 9.2 %collective-permute-start.30 = (bf16[64,4096]{1,0:T(8,128)(2,1)S(1)}, bf16[64,4096]{1,0:T(8,128)(2,1)S(1)}, u32[]{:S(2)}, u32[]{:S(2)}) collective-permute-start(bf16[64,4096]{1,0:T(8,128)(2,1)S(1)} %add_convert_fusion.3.refs_11_), channel_id=1, source_target_pairs={{0,4},{1,3},{2,6},{3,1},{4,0},{5,7},{6,2},{7,5},{8,12},{9,11},{10,... | collective-permute-start | bytes 1572872 | tf_op jit(solution)/shard_map/ppermute | solution.py:373
  81.5 2.7 %collective-permute-start.33 = (bf16[128,4096]{1,0:T(8,128)(2,1)S(1)}, bf16[128,4096]{1,0:T(8,128)(2,1)S(1)}, u32[]{:S(2)}, u32[]{:S(2)}) collective-permute-start(bf16[128,4096]{1,0:T(8,128)(2,1)S(1)} %get-tuple-element.125), channel_id=1, source_target_pairs={{0,1},{1,0},{2,3},{3,2},{4,5},{5,4},{6,7},{7,6},{8,9},{9,8},{10,11... | collective-permute-start | bytes 3145736 | tf_op jit(solution)/shard_map/ppermute | solution.py:385
  81.5 12.0 %collective-permute-start.29 = (bf16[64,4096]{1,0:T(8,128)(2,1)S(1)}, bf16[64,4096]{1,0:T(8,128)(2,1)S(1)}, u32[]{:S(2)}, u32[]{:S(2)}) collective-permute-start(bf16[64,4096]{1,0:T(8,128)(2,1)S(1)} %add_convert_fusion.2.refs_12_), channel_id=1, source_target_pairs={{0,4},{1,3},{2,6},{3,1},{4,0},{5,7},{6,2},{7,5},{8,12},{9,11},{10,... | collective-permute-start | bytes 1572872 | tf_op jit(solution)/shard_map/ppermute | solution.py:373
  82.3 9.7 %collective-permute-start.36 = (bf16[32,4096]{1,0:T(8,128)(2,1)S(1)}, bf16[32,4096]{1,0:T(8,128)(2,1)S(1)}, u32[]{:S(2)}, u32[]{:S(2)}) collective-permute-start(bf16[32,4096]{1,0:T(8,128)(2,1)S(1)} %attend.7.refs_5_), channel_id=1, source_target_pairs={{0,1},{1,0},{2,3},{3,2},{4,5},{5,4},{6,7},{7,6},{8,9},{9,8},{10,11... | collective-permute-start | bytes 786440 | tf_op jit(solution)/shard_map/ppermute | solution.py:385
  84.3 14.8 %collective-permute-start.34 = (bf16[64,4096]{1,0:T(8,128)(2,1)S(1)}, bf16[64,4096]{1,0:T(8,128)(2,1)S(1)}, u32[]{:S(2)}, u32[]{:S(2)}) collective-permute-start(bf16[64,4096]{1,0:T(8,128)(2,1)S(1)} %add_convert_fusion.1.refs_11_), channel_id=1, source_target_pairs={{0,4},{1,3},{2,6},{3,1},{4,0},{5,7},{6,2},{7,5},{8,12},{9,11},{10,... | collective-permute-start | bytes 1572872 | tf_op jit(solution)/shard_map/ppermute | solution.py:373
  85.2 9.3 %collective-permute-start.35 = (bf16[32,4096]{1,0:T(8,128)(2,1)S(1)}, bf16[32,4096]{1,0:T(8,128)(2,1)S(1)}, u32[]{:S(2)}, u32[]{:S(2)}) collective-permute-start(bf16[32,4096]{1,0:T(8,128)(2,1)S(1)} %add_convert_fusion.11.refs_12_), channel_id=1, source_target_pairs={{0,2},{1,5},{2,0},{3,7},{4,6},{5,1},{6,4},{7,3},{8,10},{9,13},{10,... | collective-permute-start | bytes 786440 | tf_op jit(solution)/shard_map/ppermute | solution.py:373
  99.2 14.4 %collective-permute-start.40 = (bf16[32,4096]{1,0:T(8,128)(2,1)S(1)}, bf16[32,4096]{1,0:T(8,128)(2,1)S(1)}, u32[]{:S(2)}, u32[]{:S(2)}) collective-permute-start(bf16[32,4096]{1,0:T(8,128)(2,1)S(1)} %add_convert_fusion.8), channel_id=1, source_target_pairs={{0,16},{1,17},{2,18},{3,19},{4,20},{5,21},{6,22},{7,23},{8,24},{9,... | collective-permute-start | bytes 786440 | tf_op jit(solution)/shard_map/ppermute | solution.py:373
  101.0 2.7 %collective-permute-start.37 = (bf16[128,4096]{1,0:T(8,128)(2,1)S(1)}, bf16[128,4096]{1,0:T(8,128)(2,1)S(1)}, u32[]{:S(2)}, u32[]{:S(2)}) collective-permute-start(bf16[128,4096]{1,0:T(8,128)(2,1)S(1)} %get-tuple-element.133), channel_id=1, source_target_pairs={{0,1},{1,0},{2,3},{3,2},{4,5},{5,4},{6,7},{7,6},{8,9},{9,8},{10,11... | collective-permute-start | bytes 3145736 | tf_op jit(solution)/shard_map/ppermute | solution.py:385
  101.1 7.3 %collective-permute-start.39 = (bf16[32,4096]{1,0:T(8,128)(2,1)S(1)}, bf16[32,4096]{1,0:T(8,128)(2,1)S(1)}, u32[]{:S(2)}, u32[]{:S(2)}) collective-permute-start(bf16[32,4096]{1,0:T(8,128)(2,1)S(1)} %add_convert_fusion.10), channel_id=1, source_target_pairs={{0,2},{1,5},{2,0},{3,7},{4,6},{5,1},{6,4},{7,3},{8,10},{9,13},{10,... | collective-permute-start | bytes 786440 | tf_op jit(solution)/shard_map/ppermute | solution.py:373
  103.8 9.8 %collective-permute-start.38 = (bf16[64,4096]{1,0:T(8,128)(2,1)S(1)}, bf16[64,4096]{1,0:T(8,128)(2,1)S(1)}, u32[]{:S(2)}, u32[]{:S(2)}) collective-permute-start(bf16[64,4096]{1,0:T(8,128)(2,1)S(1)} %add_convert_fusion), channel_id=1, source_target_pairs={{0,4},{1,3},{2,6},{3,1},{4,0},{5,7},{6,2},{7,5},{8,12},{9,11},{10,... | collective-permute-start | bytes 1572872 | tf_op jit(solution)/shard_map/ppermute | solution.py:373
  113.8 6.4 %collective-permute-start.42 = (bf16[32,4096]{1,0:T(8,128)(2,1)S(1)}, bf16[32,4096]{1,0:T(8,128)(2,1)S(1)}, u32[]{:S(2)}, u32[]{:S(2)}) collective-permute-start(bf16[32,4096]{1,0:T(8,128)(2,1)S(1)} %add_convert_fusion.7), channel_id=1, source_target_pairs={{0,2},{1,5},{2,0},{3,7},{4,6},{5,1},{6,4},{7,3},{8,10},{9,13},{10,... | collective-permute-start | bytes 786440 | tf_op jit(solution)/shard_map/ppermute | solution.py:373
  114.2 11.0 %collective-permute-start.44 = (bf16[32,4096]{1,0:T(8,128)(2,1)S(1)}, bf16[32,4096]{1,0:T(8,128)(2,1)S(1)}, u32[]{:S(2)}, u32[]{:S(2)}) collective-permute-start(bf16[32,4096]{1,0:T(8,128)(2,1)S(1)} %add_convert_fusion.9), channel_id=1, source_target_pairs={{0,24},{1,25},{2,26},{3,27},{4,28},{5,29},{6,30},{7,31},{8,16},{9,... | collective-permute-start | bytes 786440 | tf_op jit(solution)/shard_map/ppermute | solution.py:373
  117.3 7.9 %collective-permute-start.41 = (bf16[32,4096]{1,0:T(8,128)(2,1)S(1)}, bf16[32,4096]{1,0:T(8,128)(2,1)S(1)}, u32[]{:S(2)}, u32[]{:S(2)}) collective-permute-start(bf16[32,4096]{1,0:T(8,128)(2,1)S(1)} %add_convert_fusion.6), channel_id=1, source_target_pairs={{0,2},{1,5},{2,0},{3,7},{4,6},{5,1},{6,4},{7,3},{8,10},{9,13},{10,... | collective-permute-start | bytes 786440 | tf_op jit(solution)/shard_map/ppermute | solution.py:373
  120.3 10.1 %collective-permute-start.43 = (bf16[32,4096]{1,0:T(8,128)(2,1)S(1)}, bf16[32,4096]{1,0:T(8,128)(2,1)S(1)}, u32[]{:S(2)}, u32[]{:S(2)}) collective-permute-start(bf16[32,4096]{1,0:T(8,128)(2,1)S(1)} %add_convert_fusion.5), channel_id=1, source_target_pairs={{0,8},{1,9},{2,10},{3,11},{4,12},{5,13},{6,14},{7,15},{8,0},{9,1},... | collective-permute-start | bytes 786440 | tf_op jit(solution)/shard_map/ppermute | solution.py:373

commit v4 on v3

--- a/solution.py
+++ b/solution.py
@@ -434,59 +434,59 @@
     level_3 = far(level_2, 1)
     pieces_0 = with_fan([own_0, first_0, cross_0, third_0])
     context_0b = attend_half(0, 1, context_0a, pair)
-    context_0b, level_3, *pieces_0 = sync((context_0b, level_3, *pieces_0))
-    result_0 = expert(pieces_0, 0, context_0b)
-
-    first_p, cross_p, result_0 = sync((near(pair), cross(pair), result_0))
-    back_0 = beside(result_0[2])
+    context_0b, level_3, first_p, cross_p, *pieces_0 = sync(
+        (context_0b, level_3, near(pair), cross(pair), *pieces_0)
+    )
     third_p = cross(first_p)
     first_3, cross_3 = near(level_3), cross(level_3)
     fans_p = [beside(value) for value in (pair, first_p, cross_p)]
-    context_1a = attend_half(1, 0, first_p)
-    context_1a, third_p, *fans_p = sync((context_1a, third_p, *fans_p))
+    result_0 = expert(pieces_0, 0, context_0b, first_p)
+
+    third_p, result_0, *fans_p = sync((third_p, result_0, *fans_p))
+    back_0 = beside(result_0[2])
     pieces_p = [pair, first_p, cross_p, third_p, *fans_p, beside(third_p)]
-    result_2 = expert(pieces_p, 0, context_1a)
-
-    sent = [beside(value) for value in (context_0a, context_0b)]
-    first_3, cross_3, back_0, result_2, *sent = sync(
-        (first_3, cross_3, back_0, result_2, *sent)
+    result_2 = expert(pieces_p, 0, result_0[0])
+
+    first_3, cross_3, back_0, result_2, fan_3 = sync(
+        (first_3, cross_3, back_0, result_2, beside(level_3))
     )
     back_2 = beside(result_2[2])
     third_3 = cross(first_3)
-    fans_3 = [beside(value) for value in (level_3, first_3, cross_3)]
-    context_1b = attend_half(1, 1, first_3, cross_3)
-    context_1b, third_3, back_2, *fans_3 = sync((context_1b, third_3, back_2, *fans_3))
-    pieces_3 = [level_3, first_3, cross_3, third_3, *fans_3, beside(third_3)]
+    fans_3 = [beside(value) for value in (first_3, cross_3)]
+    there_0 = sum_cores(result_0, back_0)
+    context_1a = attend_half(1, 0, first_3, cross_3, there_0)
+    context_1a, third_3, back_2, *fans_3 = sync((context_1a, third_3, back_2, *fans_3))
+    pieces_3 = [level_3, first_3, cross_3, third_3, fan_3, *fans_3, beside(third_3)]
     there_2 = sum_cores(result_2, back_2)
-    back_0, there_2 = sync((back_0, there_2))
-    there_0 = sum_cores(result_0, back_0)
-    result_3 = expert(pieces_3, 0, there_2, there_0)
-
-    turned_2, result_3, sent_1a = sync((cross(there_2), result_3, beside(context_1a)))
+    result_3 = expert(pieces_3, 0, there_2)
+
+    turned_0, turned_2, result_3 = sync((cross(there_0), cross(there_2), result_3))
     back_3 = beside(result_3[2])
     held_2, passed_2 = sum_cross(result_2, back_2, turned_2)
     there_3 = sum_cores(result_3, back_3)
+    sent = [beside(value) for value in (context_0a, context_0b, context_1a)]
+    held_0, passed_0 = sum_cross(result_0, back_0, turned_0)
     result_1 = expert(pieces_p, tokens, there_3, passed_2)
 
-    contexts = [context_0a, context_0b, context_1a, context_1b]
-    turned_0, turned_3, ended_2, result_1, sent_1b = sync(
-        (cross(there_0), cross(there_3), near(passed_2), result_1, beside(context_1b))
-    )
-    sent = [*sent, sent_1a, sent_1b]
+    turned_3, ended_2, result_1, *sent = sync((cross(there_3), near(passed_2), result_1, *sent))
     far_2 = far(narrow(held_2 + widen(ended_2)), 2)
     back_1 = beside(result_1[2])
     held_3, passed_3 = sum_cross(result_3, back_3, turned_3)
-    held_0, passed_0 = sum_cross(result_0, back_0, turned_0)
+    passed_3, back_1 = sync((passed_3, back_1))
     there_1 = sum_cores(result_1, back_1)
     total_3 = narrow(held_3 + widen(near(passed_3)))
     far_3 = far(total_3, 3)
+    turned_1, far_2 = sync((cross(there_1), far_2))
+    held_1, passed_1 = sum_cross(result_1, back_1, turned_1)
+    context_1b = attend_half(1, 1, total_3, passed_1)
+    contexts = [context_0a, context_0b, context_1a, context_1b]
+    sent = [*sent, beside(context_1b)]
     ordered = [contexts[0], contexts[2], sent[0], sent[2], contexts[1], contexts[3], sent[1], sent[3]]
-    own_late, _ = sync((own_mine, total_3))
+    own_late, far_3 = sync((own_mine, far_3))
     context = place_context(own_late, ordered, jax.ShapeDtypeStruct(queries.shape, jnp.bfloat16))
-    turned_1, context, far_2 = sync((cross(there_1), context, far_2))
-    held_1, passed_1 = sum_cross(result_1, back_1, turned_1)
-    passed_1, passed_0 = sync((passed_1, passed_0))
-    far_1 = far(narrow(held_1 + widen(near(passed_1))), 1)
+    total_1, passed_0 = sync((narrow(held_1 + widen(near(passed_1))), passed_0))
+    far_1 = far(total_1, 1)
+    context, far_1 = sync((context, far_1))
     total = held_0 + widen(near(passed_0)) + widen(far_1)
     expert_out = narrow(total + widen(far_2) + widen(far_3))
     return (context, expert_out)

time: 132 us -> 127 us (0.962)
  waiting for transfers between devices: 43.1 us -> 37 us
  starting transfers between devices: 34.7 us -> 37 us
    ppermute x23, waiting for transfers between devices: 38.9 us -> 32.3 us  [swap(): return lax.ppermute(value, ('ep', 'fan'), pairs)]
    ppermute x23, starting transfers between devices: 31.4 us -> 32.9 us  [swap(): return lax.ppermute(value, ('ep', 'fan'), pairs)]
    unnamed x24 -> x26, local copies, waits for them, and re-layouts: 8.43 us -> 8.44 us
  transfers between devices with their start and end apart: 45 -> 45, of which waited for: 20 -> 16; matrix products, arithmetic and copies ran while one was open for 1% -> 1% of each run, Pallas kernels for 30% -> 31%
where the time goes in v4:
time: 127 us
  Pallas kernels  41.4 us (33%)
  starting transfers between devices  37 us (29%)
  waiting for transfers between devices  37 us (29%)
  local copies, waits for them, and re-layouts  8.44 us (7%)
  other arithmetic  2.24 us (2%)
    ppermute x23, starting transfers between devices, swap(): return lax.ppermute(value, ('ep', 'fan'), pairs)  32.9 us
    ppermute x23, waiting for transfers between devices, swap(): return lax.ppermute(value, ('ep', 'fan'), pairs)  32.3 us
    pallas_call x4, Pallas kernels, expert_chunk(): pl.pallas_call(functools.partial(expert_kernel, count, at_row, tokens), o...  22.3 us
    pallas_call x4, Pallas kernels, attend(): pl.pallas_call(functools.partial(attend_kernel, local, heads), out_shape=...  15.2 us
    unnamed x26, local copies, waits for them, and re-layouts  8.44 us
    ppermute x22, waiting for transfers between devices, beside(): return lax.ppermute(value, 'fan', [(0, 1), (1, 0)])  4.75 us
    ppermute x22, starting transfers between devices, beside(): return lax.ppermute(value, 'fan', [(0, 1), (1, 0)])  4.07 us
  transfers between devices with their start and end apart: 45, of which 16 were waited for; matrix products, arithmetic and copies ran while one was open for 1% of the time, Pallas kernels for 31%

profile of v4, /device:TPU:0, one launch (start us, length us, event | category | flops | bytes accessed | tf_op | source)
XLA Modules:
  0.0 127.1 jit_solution(17872092811653400431)
XLA Ops:
  0.6 1.9 %norm_message.1.refs_0_ = bf16[32,4224]{1,0:T(8,128)(2,1)} custom-call(bf16[32,4096]{1,0:T(8,128)(2,1)} %hidden_ref.1, bf16[4096]{0:T(1024)(128)(2,1)} %gain_ref.1, s32[8,32]{1,0:T(8,128)} %bitcast.21, f32[8,32]{1,0:T(8,128)} %bitcast.22), custom_call_target="tpu_custom_call" | custom-call | flops 1048576 | bytes 16384 | tf_op jit(solution)/shard_map/norm_message/pallas_call | solution.py:63
  2.6 1.2 copy-done.4
  3.8 0.9 copy-done.5
  4.7 0.7 copy-done.8
  5.4 0.2 pack.1
  5.6 0.5 collective-permute-start
  6.1 2.5 %collective-permute-start.4 = (bf16[32,4224]{1,0:T(8,128)(2,1)}, bf16[32,4224]{1,0:T(8,128)(2,1)S(1)}, u32[]{:S(2)}, u32[]{:S(2)}) collective-permute-start(bf16[32,4224]{1,0:T(8,128)(2,1)} %norm_message.1.refs_0_), channel_id=1, source_target_pairs={{0,2},{1,5},{2,0},{3,7},{4,6},{5,1},{6,4},{7,3},{8,10},{9,13},{10,... | collective-permute-start | bytes 811016 | tf_op jit(solution)/shard_map/ppermute | solution.py:373
  8.6 0.2 collective-permute-start.1
  8.8 1.3 %collective-permute-start.9 = (bf16[32,4224]{1,0:T(8,128)(2,1)}, bf16[32,4224]{1,0:T(8,128)(2,1)S(1)}, u32[]{:S(2)}, u32[]{:S(2)}) collective-permute-start(bf16[32,4224]{1,0:T(8,128)(2,1)} %norm_message.1.refs_0_), channel_id=1, source_target_pairs={{0,4},{1,3},{2,6},{3,1},{4,0},{5,7},{6,2},{7,5},{8,12},{9,11},{10,... | collective-permute-start | bytes 811016 | tf_op jit(solution)/shard_map/ppermute | solution.py:373
  10.1 2.6 %collective-permute-start.2 = (bf16[32,4224]{1,0:T(8,128)(2,1)}, bf16[32,4224]{1,0:T(8,128)(2,1)S(1)}, u32[]{:S(2)}, u32[]{:S(2)}) collective-permute-start(bf16[32,4224]{1,0:T(8,128)(2,1)} %norm_message.1.refs_0_), channel_id=1, source_target_pairs={{0,16},{1,17},{2,18},{3,19},{4,20},{5,21},{6,22},{7,23},{8,24},{9,... | collective-permute-start | bytes 811016 | tf_op jit(solution)/shard_map/ppermute | solution.py:373
  12.7 1.6 %collective-permute-start.3 = (bf16[32,4224]{1,0:T(8,128)(2,1)}, bf16[32,4224]{1,0:T(8,128)(2,1)S(1)}, u32[]{:S(2)}, u32[]{:S(2)}) collective-permute-start(bf16[32,4224]{1,0:T(8,128)(2,1)} %norm_message.1.refs_0_), channel_id=1, source_target_pairs={{0,8},{1,9},{2,10},{3,11},{4,12},{5,13},{6,14},{7,15},{8,0},{9,1},... | collective-permute-start | bytes 811016 | tf_op jit(solution)/shard_map/ppermute | solution.py:373
  14.3 0.8 collective-permute-done.4.refs_1_
  15.1 2.2 %collective-permute-start.5 = (bf16[32,4224]{1,0:T(8,128)(2,1)S(1)}, bf16[32,4224]{1,0:T(8,128)(2,1)S(1)}, u32[]{:S(2)}, u32[]{:S(2)}) collective-permute-start(bf16[32,4224]{1,0:T(8,128)(2,1)S(1)} %collective-permute-done.4.refs_1_), channel_id=1, source_target_pairs={{0,4},{1,3},{2,6},{3,1},{4,0},{5,7},{6,2},{7,5},{8,12},{9,11},{10,... | collective-permute-start | bytes 811016 | tf_op jit(solution)/shard_map/ppermute | solution.py:373
  17.2 2.2 %copy-done.2 = bf16[2,1024,1024]{2,1,0:T(8,128)(2,1)S(1)} copy-done((bf16[2,1024,1024]{2,1,0:T(8,128)(2,1)S(1)}, bf16[2,1024,1024]{2,1,0:T(8,128)(2,1)}, u32[]{:S(2)}) %copy-start.2) | copy-done | bytes 4194328
  19.4 0.7 copy-done.6
  20.1 3.8 %attend.4.refs_0_ = bf16[32,4096]{1,0:T(8,128)(2,1)S(1)} custom-call(s32[4]{0:T(128)S(1)} %copy-done.6, bf16[64,8192]{1,0:T(8,128)(2,1)S(1)} %get-tuple-element.77.q_mine, bf16[64,8192]{1,0:T(8,128)(2,1)S(1)} %collective-permute-done.q_other, bf16[64,1152]{1,0:T(8,128)(2,1)S(1)} %get-tuple-element.134.o_mine, ...), custom_call_target="tpu_custom_call" | custom-call | flops 1048576 | bytes 16384 | tf_op jit(solution)/shard_map/attend/pallas_call | solution.py:223
  23.9 1.5 %collective-permute-done.2.top = bf16[32,4224]{1,0:T(8,128)(2,1)S(1)} collective-permute-done((bf16[32,4224]{1,0:T(8,128)(2,1)}, bf16[32,4224]{1,0:T(8,128)(2,1)S(1)}, u32[]{:S(2)}, u32[]{:S(2)}) %collective-permute-start.2) | collective-permute-done | bytes 270368 | tf_op jit(solution)/shard_map/ppermute | solution.py:373
  25.7 1.3 %collective-permute-start.7 = (bf16[64,4224]{1,0:T(8,128)(2,1)S(1)}, bf16[64,4224]{1,0:T(8,128)(2,1)S(1)}, u32[]{:S(2)}, u32[]{:S(2)}) collective-permute-start(bf16[64,4224]{1,0:T(8,128)(2,1)S(1)} %stack.1.refs_1_.refs_0_), channel_id=1, source_target_pairs={{0,2},{1,5},{2,0},{3,7},{4,6},{5,1},{6,4},{7,3},{8,10},{9,13},{10,... | collective-permute-start | bytes 1622024 | tf_op jit(solution)/shard_map/ppermute | solution.py:373
  27.0 1.1 collective-permute-start.8
  28.1 0.5 collective-permute-start.13
  28.6 1.4 %collective-permute-start.6 = (bf16[32,4224]{1,0:T(8,128)(2,1)S(1)}, bf16[32,4224]{1,0:T(8,128)(2,1)S(1)}, u32[]{:S(2)}, u32[]{:S(2)}) collective-permute-start(bf16[32,4224]{1,0:T(8,128)(2,1)S(1)} %collective-permute-done.2.top), channel_id=1, source_target_pairs={{0,8},{1,9},{2,10},{3,11},{4,12},{5,13},{6,14},{7,15},{8,0},{9,1},... | collective-permute-start | bytes 811016 | tf_op jit(solution)/shard_map/ppermute | solution.py:373
  30.0 3.8 %attend.5.refs_11_.refs_4_ = bf16[32,4096]{1,0:T(8,128)(2,1)S(1)} custom-call(s32[4]{0:T(128)S(1)} %copy-done.7, bf16[64,8192]{1,0:T(8,128)(2,1)S(1)} %get-tuple-element.77.q_mine, bf16[64,8192]{1,0:T(8,128)(2,1)S(1)} %collective-permute-done.q_other, bf16[64,1152]{1,0:T(8,128)(2,1)S(1)} %get-tuple-element.134.o_mine, ...), custom_call_target="tpu_custom_call" | custom-call | flops 1048576 | bytes 16384 | tf_op jit(solution)/shard_map/attend/pallas_call | solution.py:223
  33.9 3.1 %collective-permute-done.6.refs_0_ = bf16[32,4224]{1,0:T(8,128)(2,1)S(1)} collective-permute-done((bf16[32,4224]{1,0:T(8,128)(2,1)S(1)}, bf16[32,4224]{1,0:T(8,128)(2,1)S(1)}, u32[]{:S(2)}, u32[]{:S(2)}) %collective-permute-start.6) | collective-permute-done | bytes 270368 | tf_op jit(solution)/shard_map/ppermute | solution.py:373
  37.0 3.7 %collective-permute-done.7.refs_12_.refs_1_ = bf16[64,4224]{1,0:T(8,128)(2,1)S(1)} collective-permute-done((bf16[64,4224]{1,0:T(8,128)(2,1)S(1)}, bf16[64,4224]{1,0:T(8,128)(2,1)S(1)}, u32[]{:S(2)}, u32[]{:S(2)}) %collective-permute-start.7) | collective-permute-done | bytes 540704 | tf_op jit(solution)/shard_map/ppermute | solution.py:373
  40.8 0.6 collective-permute-start.14
  41.4 0.3 collective-permute-start.16
  41.7 0.2 collective-permute-start.17
  41.9 2.8 %copy-done.1 = bf16[1,768,4096]{2,1,0:T(8,128)(2,1)S(1)} copy-done((bf16[1,768,4096]{2,1,0:T(8,128)(2,1)S(1)}, bf16[1,768,4096]{2,1,0:T(8,128)(2,1)}, u32[]{:S(2)}) %copy-start.1) | copy-done | bytes 6291480
  44.7 6.1 %expert_chunk.4 = (bf16[64,4096]{1,0:T(8,128)(2,1)S(1)}, bf16[64,4096]{1,0:T(8,128)(2,1)S(1)}, bf16[128,4096]{1,0:T(8,128)(2,1)S(1)}) custom-call(bf16[32,4224]{1,0:T(8,128)(2,1)} %norm_message.1.refs_0_, bf16[32,4224]{1,0:T(8,128)(2,1)S(1)} %collective-permute-done.4.refs_1_, bf16[32,4224]{1,0:T(8,128)(2,1)S(1)} %collective-permute-done.9.refs_2_, ...), custom_call_target="tpu_custom_call" | custom-call | flops 1048576 | bytes 16384 | tf_op jit(solution)/shard_map/expert_chunk/pallas_call | solution.py:327
  50.8 0.4 collective-permute-start.20
  51.4 1.6 %collective-permute-start.18 = (bf16[32,4224]{1,0:T(8,128)(2,1)S(1)}, bf16[32,4224]{1,0:T(8,128)(2,1)S(1)}, u32[]{:S(2)}, u32[]{:S(2)}) collective-permute-start(bf16[32,4224]{1,0:T(8,128)(2,1)S(1)} %collective-permute-done.6.refs_0_), channel_id=1, source_target_pairs={{0,2},{1,5},{2,0},{3,7},{4,6},{5,1},{6,4},{7,3},{8,10},{9,13},{10,... | collective-permute-start | bytes 811016 | tf_op jit(solution)/shard_map/ppermute | solution.py:373
  53.0 0.9 collective-permute-start.19
  53.9 0.4 collective-permute-done.21.refs_7_
  54.3 5.3 %expert_chunk.5 = (bf16[64,4096]{1,0:T(8,128)(2,1)S(1)}, bf16[64,4096]{1,0:T(8,128)(2,1)S(1)}, bf16[128,4096]{1,0:T(8,128)(2,1)S(1)}) custom-call(bf16[64,4224]{1,0:T(8,128)(2,1)S(1)} %stack.1.refs_1_.refs_0_, bf16[64,4224]{1,0:T(8,128)(2,1)S(1)} %collective-permute-done.7.refs_12_.refs_1_, bf16[64,4224]{1,0:T(8,128)(2,1)S(1)} %collective-permute-done.8.refs_2_, ...), custom_call_target="tpu_custom_call" | custom-call | flops 1048576 | bytes 16384 | tf_op jit(solution)/shard_map/expert_chunk/pallas_call | solution.py:327
  59.7 0.8 collective-permute-done.18.refs_0_.refs_1_
  60.6 1.4 %collective-permute-start.24 = (bf16[32,4224]{1,0:T(8,128)(2,1)S(1)}, bf16[32,4224]{1,0:T(8,128)(2,1)S(1)}, u32[]{:S(2)}, u32[]{:S(2)}) collective-permute-start(bf16[32,4224]{1,0:T(8,128)(2,1)S(1)} %collective-permute-done.18.refs_0_.refs_1_), channel_id=1, source_target_pairs={{0,4},{1,3},{2,6},{3,1},{4,0},{5,7},{6,2},{7,5},{8,12},{9,11},{10,... | collective-permute-start | bytes 811016 | tf_op jit(solution)/shard_map/ppermute | solution.py:373
  62.0 0.4 collective-permute-start.26
  62.7 1.1 collective-permute-start.23
  63.8 3.8 %attend.6.refs_1_ = bf16[32,4096]{1,0:T(8,128)(2,1)S(1)} custom-call(s32[4]{0:T(128)S(1)} %copy-done.7, bf16[64,8192]{1,0:T(8,128)(2,1)S(1)} %get-tuple-element.77.q_mine, bf16[64,8192]{1,0:T(8,128)(2,1)S(1)} %collective-permute-done.q_other, bf16[64,1152]{1,0:T(8,128)(2,1)S(1)} %get-tuple-element.134.o_mine, ...), custom_call_target="tpu_custom_call" | custom-call | flops 1048576 | bytes 16384 | tf_op jit(solution)/shard_map/attend/pallas_call | solution.py:223
  67.7 1.1 collective-permute-start.28
  68.8 1.5 %collective-permute-done.29.refs_7_ = bf16[32,4224]{1,0:T(8,128)(2,1)S(1)} collective-permute-done((bf16[32,4224]{1,0:T(8,128)(2,1)S(1)}, bf16[32,4224]{1,0:T(8,128)(2,1)S(1)}, u32[]{:S(2)}, u32[]{:S(2)}) %collective-permute-start.29) | collective-permute-done | bytes 270368 | tf_op jit(solution)/shard_map/ppermute | solution.py:385
  70.4 5.6 %expert_chunk.6 = (bf16[64,4096]{1,0:T(8,128)(2,1)S(1)}, bf16[64,4096]{1,0:T(8,128)(2,1)S(1)}, bf16[128,4096]{1,0:T(8,128)(2,1)S(1)}) custom-call(bf16[32,4224]{1,0:T(8,128)(2,1)S(1)} %collective-permute-done.6.refs_0_, bf16[32,4224]{1,0:T(8,128)(2,1)S(1)} %collective-permute-done.18.refs_0_.refs_1_, ...), custom_call_target="tpu_custom_call" | custom-call | flops 1048576 | bytes 16384 | tf_op jit(solution)/shard_map/expert_chunk/pallas_call | solution.py:327
  76.0 2.4 %collective-permute-done.28 = bf16[64,4096]{1,0:T(8,128)(2,1)S(1)} collective-permute-done((bf16[64,4096]{1,0:T(8,128)(2,1)S(1)}, bf16[64,4096]{1,0:T(8,128)(2,1)S(1)}, u32[]{:S(2)}, u32[]{:S(2)}) %collective-permute-start.28) | collective-permute-done | bytes 524320 | tf_op jit(solution)/shard_map/ppermute | solution.py:373
  78.4 0.5 collective-permute-start.33
  78.9 0.5 collective-permute-start.35
  79.4 1.6 %collective-permute-done.30 = bf16[128,4096]{1,0:T(8,128)(2,1)S(1)} collective-permute-done((bf16[128,4096]{1,0:T(8,128)(2,1)S(1)}, bf16[128,4096]{1,0:T(8,128)(2,1)S(1)}, u32[]{:S(2)}, u32[]{:S(2)}) %collective-permute-start.30) | collective-permute-done | bytes 1048608 | tf_op jit(solution)/shard_map/ppermute | solution.py:385
  81.2 1.4 %collective-permute-start.31 = (bf16[64,4096]{1,0:T(8,128)(2,1)S(1)}, bf16[64,4096]{1,0:T(8,128)(2,1)S(1)}, u32[]{:S(2)}, u32[]{:S(2)}) collective-permute-start(bf16[64,4096]{1,0:T(8,128)(2,1)S(1)} %add_convert_fusion.1.refs_11_), channel_id=1, source_target_pairs={{0,4},{1,3},{2,6},{3,1},{4,0},{5,7},{6,2},{7,5},{8,12},{9,11},{10,... | collective-permute-start | bytes 1572872 | tf_op jit(solution)/shard_map/ppermute | solution.py:373
  82.7 1.4 %collective-permute-start.32 = (bf16[32,4096]{1,0:T(8,128)(2,1)S(1)}, bf16[32,4096]{1,0:T(8,128)(2,1)S(1)}, u32[]{:S(2)}, u32[]{:S(2)}) collective-permute-start(bf16[32,4096]{1,0:T(8,128)(2,1)S(1)} %add_convert_fusion.11.refs_12_), channel_id=1, source_target_pairs={{0,2},{1,5},{2,0},{3,7},{4,6},{5,1},{6,4},{7,3},{8,10},{9,13},{10,... | collective-permute-start | bytes 786440 | tf_op jit(solution)/shard_map/ppermute | solution.py:373
  84.1 5.3 %expert_chunk.7 = (bf16[64,4096]{1,0:T(8,128)(2,1)S(1)}, bf16[64,4096]{1,0:T(8,128)(2,1)S(1)}, bf16[128,4096]{1,0:T(8,128)(2,1)S(1)}) custom-call(bf16[64,4224]{1,0:T(8,128)(2,1)S(1)} %stack.1.refs_1_.refs_0_, bf16[64,4224]{1,0:T(8,128)(2,1)S(1)} %collective-permute-done.7.refs_12_.refs_1_, bf16[64,4224]{1,0:T(8,128)(2,1)S(1)} %collective-permute-done.8.refs_2_, ...), custom_call_target="tpu_custom_call" | custom-call | flops 1048576 | bytes 16384 | tf_op jit(solution)/shard_map/expert_chunk/pallas_call | solution.py:327
  89.5 2.5 %collective-permute-done.32 = bf16[32,4096]{1,0:T(8,128)(2,1)S(1)} collective-permute-done((bf16[32,4096]{1,0:T(8,128)(2,1)S(1)}, bf16[32,4096]{1,0:T(8,128)(2,1)S(1)}, u32[]{:S(2)}, u32[]{:S(2)}) %collective-permute-start.32) | collective-permute-done | bytes 262176 | tf_op jit(solution)/shard_map/ppermute | solution.py:373
  92.0 1.2 collective-permute-done.31
  93.3 1.3 %collective-permute-start.40 = (bf16[32,4096]{1,0:T(8,128)(2,1)S(1)}, bf16[32,4096]{1,0:T(8,128)(2,1)S(1)}, u32[]{:S(2)}, u32[]{:S(2)}) collective-permute-start(bf16[32,4096]{1,0:T(8,128)(2,1)S(1)} %add_convert_fusion.8), channel_id=1, source_target_pairs={{0,16},{1,17},{2,18},{3,19},{4,20},{5,21},{6,22},{7,23},{8,24},{9,... | collective-permute-start | bytes 786440 | tf_op jit(solution)/shard_map/ppermute | solution.py:373
  94.7 1.1 collective-permute-done.36
  96.0 1.4 %collective-permute-start.39 = (bf16[64,4096]{1,0:T(8,128)(2,1)S(1)}, bf16[64,4096]{1,0:T(8,128)(2,1)S(1)}, u32[]{:S(2)}, u32[]{:S(2)}) collective-permute-start(bf16[64,4096]{1,0:T(8,128)(2,1)S(1)} %add_convert_fusion), channel_id=1, source_target_pairs={{0,4},{1,3},{2,6},{3,1},{4,0},{5,7},{6,2},{7,5},{8,12},{9,11},{10,... | collective-permute-start | bytes 1572872 | tf_op jit(solution)/shard_map/ppermute | solution.py:373
  97.5 1.1 collective-permute-start.37
  98.7 10.0 %collective-permute-done.40 = bf16[32,4096]{1,0:T(8,128)(2,1)S(1)} collective-permute-done((bf16[32,4096]{1,0:T(8,128)(2,1)S(1)}, bf16[32,4096]{1,0:T(8,128)(2,1)S(1)}, u32[]{:S(2)}, u32[]{:S(2)}) %collective-permute-start.40) | collective-permute-done | bytes 262176 | tf_op jit(solution)/shard_map/ppermute | solution.py:373
  108.8 1.2 collective-permute-start.42
  110.0 3.3 %collective-permute-start.38 = (bf16[32,4096]{1,0:T(8,128)(2,1)S(1)}, bf16[32,4096]{1,0:T(8,128)(2,1)S(1)}, u32[]{:S(2)}, u32[]{:S(2)}) collective-permute-start(bf16[32,4096]{1,0:T(8,128)(2,1)S(1)} %add_convert_fusion.9.refs_0_), channel_id=1, source_target_pairs={{0,24},{1,25},{2,26},{3,27},{4,28},{5,29},{6,30},{7,31},{8,16},{9,... | collective-permute-start | bytes 786440 | tf_op jit(solution)/shard_map/ppermute | solution.py:373
  113.3 3.8 %attend.7.refs_5_ = bf16[32,4096]{1,0:T(8,128)(2,1)S(1)} custom-call(s32[4]{0:T(128)S(1)} %copy-done.7, bf16[64,8192]{1,0:T(8,128)(2,1)S(1)} %get-tuple-element.77.q_mine, bf16[64,8192]{1,0:T(8,128)(2,1)S(1)} %collective-permute-done.q_other, bf16[64,1152]{1,0:T(8,128)(2,1)S(1)} %get-tuple-element.134.o_mine, ...), custom_call_target="tpu_custom_call" | custom-call | flops 1048576 | bytes 16384 | tf_op jit(solution)/shard_map/attend/pallas_call | solution.py:223
  117.4 1.0 collective-permute-start.44
  118.4 1.7 %collective-permute-done.38 = bf16[32,4096]{1,0:T(8,128)(2,1)S(1)} collective-permute-done((bf16[32,4096]{1,0:T(8,128)(2,1)S(1)}, bf16[32,4096]{1,0:T(8,128)(2,1)S(1)}, u32[]{:S(2)}, u32[]{:S(2)}) %collective-permute-start.38) | collective-permute-done | bytes 262176 | tf_op jit(solution)/shard_map/ppermute | solution.py:373
  120.1 1.6 %place_context.1 = bf16[32,2,8192]{2,1,0:T(2,128)(2,1)} custom-call(bf16[64,1152]{1,0:T(8,128)(2,1)S(1)} %get-tuple-element.134.o_mine, bf16[32,4096]{1,0:T(8,128)(2,1)S(1)} %attend.4.refs_0_, bf16[32,4096]{1,0:T(8,128)(2,1)S(1)} %attend.6.refs_1_, bf16[32,4096]{1,0:T(8,128)(2,1)S(1)} %collective-permute-done.33.refs_2_, ...), custom_call_target="tpu_custom_call" | custom-call | flops 1048576 | bytes 16384 | tf_op jit(solution)/shard_map/place_context/pallas_call | solution.py:273
  121.7 4.4 %collective-permute-done.43 = bf16[32,4096]{1,0:T(8,128)(2,1)S(1)} collective-permute-done((bf16[32,4096]{1,0:T(8,128)(2,1)S(1)}, bf16[32,4096]{1,0:T(8,128)(2,1)S(1)}, u32[]{:S(2)}, u32[]{:S(2)}) %collective-permute-start.43) | collective-permute-done | bytes 262176 | tf_op jit(solution)/shard_map/ppermute | solution.py:373
  126.1 0.9 add_convert_fusion.4
  (78 shorter events, 2.3 us)
Async XLA Ops:
  0.6 29.4 %copy-start.7 = (s32[4]{0:T(128)S(1)}, s32[4]{0:T(128)}, u32[]{:S(2)}) copy-start(s32[4]{0:T(128)} %lens_ref.7) | copy-start | bytes 52
  2.6 1.2 copy-start.4
  3.8 0.9 copy-start.5
  4.7 0.7 copy-start.8
  5.6 11.6 %collective-permute-start = (bf16[64,8192]{1,0:T(8,128)(2,1)S(1)}, bf16[64,8192]{1,0:T(8,128)(2,1)S(1)}, u32[]{:S(2)}, u32[]{:S(2)}) collective-permute-start(bf16[64,8192]{1,0:T(8,128)(2,1)S(1)} %get-tuple-element.77.q_mine), channel_id=1, source_target_pairs={{0,1},{1,0},{2,3},{3,2},{4,5},{5,4},{6,7},{7,6},{8,9},{9,8},{10,11... | collective-permute-start | bytes 3145736 | tf_op jit(solution)/shard_map/ppermute | solution.py:385
  6.1 9.0 %collective-permute-start.4 = (bf16[32,4224]{1,0:T(8,128)(2,1)}, bf16[32,4224]{1,0:T(8,128)(2,1)S(1)}, u32[]{:S(2)}, u32[]{:S(2)}) collective-permute-start(bf16[32,4224]{1,0:T(8,128)(2,1)} %norm_message.1.refs_0_), channel_id=1, source_target_pairs={{0,2},{1,5},{2,0},{3,7},{4,6},{5,1},{6,4},{7,3},{8,10},{9,13},{10,... | collective-permute-start | bytes 811016 | tf_op jit(solution)/shard_map/ppermute | solution.py:373
  8.6 33.3 %slice-start = ((s8[6291456]{0:T(1024)(128)(4,1)}), s8[4194304]{0:T(1024)(128)(4,1)S(1)}, s32[]{:S(2)}) async-start(s8[6291456]{0:T(1024)(128)(4,1)} %bitcast.5), calls=%async_computation | async-start | bytes 8388608
  8.6 33.3 %copy-start = (bf16[1,4096,768]{2,1,0:T(8,128)(2,1)S(1)}, bf16[1,4096,768]{2,1,0:T(8,128)(2,1)}, u32[]{:S(2)}) copy-start(bf16[1,4096,768]{2,1,0:T(8,128)(2,1)} %param.22) | copy-start | bytes 18874372
  8.6 4.1 %collective-permute-start.1 = (bf16[64,1152]{1,0:T(8,128)(2,1)S(1)}, bf16[64,1152]{1,0:T(8,128)(2,1)S(1)}, u32[]{:S(2)}, u32[]{:S(2)}) collective-permute-start(bf16[64,1152]{1,0:T(8,128)(2,1)S(1)} %get-tuple-element.134.o_mine), channel_id=1, source_target_pairs={{0,1},{1,0},{2,3},{3,2},{4,5},{5,4},{6,7},{7,6},{8,9},{9,8},{10,11... | collective-permute-start | bytes 442376 | tf_op jit(solution)/shard_map/ppermute | solution.py:385
  8.8 8.4 %collective-permute-start.9 = (bf16[32,4224]{1,0:T(8,128)(2,1)}, bf16[32,4224]{1,0:T(8,128)(2,1)S(1)}, u32[]{:S(2)}, u32[]{:S(2)}) collective-permute-start(bf16[32,4224]{1,0:T(8,128)(2,1)} %norm_message.1.refs_0_), channel_id=1, source_target_pairs={{0,4},{1,3},{2,6},{3,1},{4,0},{5,7},{6,2},{7,5},{8,12},{9,11},{10,... | collective-permute-start | bytes 811016 | tf_op jit(solution)/shard_map/ppermute | solution.py:373
  10.1 15.3 %collective-permute-start.2 = (bf16[32,4224]{1,0:T(8,128)(2,1)}, bf16[32,4224]{1,0:T(8,128)(2,1)S(1)}, u32[]{:S(2)}, u32[]{:S(2)}) collective-permute-start(bf16[32,4224]{1,0:T(8,128)(2,1)} %norm_message.1.refs_0_), channel_id=1, source_target_pairs={{0,16},{1,17},{2,18},{3,19},{4,20},{5,21},{6,22},{7,23},{8,24},{9,... | collective-permute-start | bytes 811016 | tf_op jit(solution)/shard_map/ppermute | solution.py:373
  12.7 12.9 %collective-permute-start.3 = (bf16[32,4224]{1,0:T(8,128)(2,1)}, bf16[32,4224]{1,0:T(8,128)(2,1)S(1)}, u32[]{:S(2)}, u32[]{:S(2)}) collective-permute-start(bf16[32,4224]{1,0:T(8,128)(2,1)} %norm_message.1.refs_0_), channel_id=1, source_target_pairs={{0,8},{1,9},{2,10},{3,11},{4,12},{5,13},{6,14},{7,15},{8,0},{9,1},... | collective-permute-start | bytes 811016 | tf_op jit(solution)/shard_map/ppermute | solution.py:373
  15.1 10.6 %collective-permute-start.5 = (bf16[32,4224]{1,0:T(8,128)(2,1)S(1)}, bf16[32,4224]{1,0:T(8,128)(2,1)S(1)}, u32[]{:S(2)}, u32[]{:S(2)}) collective-permute-start(bf16[32,4224]{1,0:T(8,128)(2,1)S(1)} %collective-permute-done.4.refs_1_), channel_id=1, source_target_pairs={{0,4},{1,3},{2,6},{3,1},{4,0},{5,7},{6,2},{7,5},{8,12},{9,11},{10,... | collective-permute-start | bytes 811016 | tf_op jit(solution)/shard_map/ppermute | solution.py:373
  17.2 10.9 %collective-permute-start.12 = (bf16[32,4224]{1,0:T(8,128)(2,1)S(1)}, bf16[32,4224]{1,0:T(8,128)(2,1)S(1)}, u32[]{:S(2)}, u32[]{:S(2)}) collective-permute-start(bf16[32,4224]{1,0:T(8,128)(2,1)S(1)} %collective-permute-done.9.refs_2_), channel_id=1, source_target_pairs={{0,1},{1,0},{2,3},{3,2},{4,5},{5,4},{6,7},{7,6},{8,9},{9,8},{10,11... | collective-permute-start | bytes 811016 | tf_op jit(solution)/shard_map/ppermute | solution.py:385
  17.2 2.2 %copy-start.2 = (bf16[2,1024,1024]{2,1,0:T(8,128)(2,1)S(1)}, bf16[2,1024,1024]{2,1,0:T(8,128)(2,1)}, u32[]{:S(2)}) copy-start(bf16[2,1024,1024]{2,1,0:T(8,128)(2,1)} %cache.7) | copy-start | bytes 12582916
  19.4 0.7 copy-start.6
  23.9 18.0 %slice-start.1 = ((s8[6291456]{0:T(1024)(128)(4,1)}), s8[2097152]{0:T(1024)(128)(4,1)S(1)}, s32[]{:S(2)}) async-start(s8[6291456]{0:T(1024)(128)(4,1)} %bitcast.5), calls=%async_computation.1 | async-start | bytes 4194304
  25.6 3.0 %collective-permute-start.10 = (bf16[32,4224]{1,0:T(8,128)(2,1)}, bf16[32,4224]{1,0:T(8,128)(2,1)S(1)}, u32[]{:S(2)}, u32[]{:S(2)}) collective-permute-start(bf16[32,4224]{1,0:T(8,128)(2,1)} %norm_message.1.refs_0_), channel_id=1, source_target_pairs={{0,1},{1,0},{2,3},{3,2},{4,5},{5,4},{6,7},{7,6},{8,9},{9,8},{10,11... | collective-permute-start | bytes 811016 | tf_op jit(solution)/shard_map/ppermute | solution.py:385
  25.7 15.1 %collective-permute-start.7 = (bf16[64,4224]{1,0:T(8,128)(2,1)S(1)}, bf16[64,4224]{1,0:T(8,128)(2,1)S(1)}, u32[]{:S(2)}, u32[]{:S(2)}) collective-permute-start(bf16[64,4224]{1,0:T(8,128)(2,1)S(1)} %stack.1.refs_1_.refs_0_), channel_id=1, source_target_pairs={{0,2},{1,5},{2,0},{3,7},{4,6},{5,1},{6,4},{7,3},{8,10},{9,13},{10,... | collective-permute-start | bytes 1622024 | tf_op jit(solution)/shard_map/ppermute | solution.py:373
  27.0 13.8 %collective-permute-start.8 = (bf16[64,4224]{1,0:T(8,128)(2,1)S(1)}, bf16[64,4224]{1,0:T(8,128)(2,1)S(1)}, u32[]{:S(2)}, u32[]{:S(2)}) collective-permute-start(bf16[64,4224]{1,0:T(8,128)(2,1)S(1)} %stack.1.refs_1_.refs_0_), channel_id=1, source_target_pairs={{0,4},{1,3},{2,6},{3,1},{4,0},{5,7},{6,2},{7,5},{8,12},{9,11},{10,... | collective-permute-start | bytes 1622024 | tf_op jit(solution)/shard_map/ppermute | solution.py:373
  28.1 5.8 %collective-permute-start.11 = (bf16[32,4224]{1,0:T(8,128)(2,1)S(1)}, bf16[32,4224]{1,0:T(8,128)(2,1)S(1)}, u32[]{:S(2)}, u32[]{:S(2)}) collective-permute-start(bf16[32,4224]{1,0:T(8,128)(2,1)S(1)} %collective-permute-done.4.refs_1_), channel_id=1, source_target_pairs={{0,1},{1,0},{2,3},{3,2},{4,5},{5,4},{6,7},{7,6},{8,9},{9,8},{10,11... | collective-permute-start | bytes 811016 | tf_op jit(solution)/shard_map/ppermute | solution.py:385
  28.1 5.9 %collective-permute-start.13 = (bf16[32,4224]{1,0:T(8,128)(2,1)S(1)}, bf16[32,4224]{1,0:T(8,128)(2,1)S(1)}, u32[]{:S(2)}, u32[]{:S(2)}) collective-permute-start(bf16[32,4224]{1,0:T(8,128)(2,1)S(1)} %collective-permute-done.5.refs_3_), channel_id=1, source_target_pairs={{0,1},{1,0},{2,3},{3,2},{4,5},{5,4},{6,7},{7,6},{8,9},{9,8},{10,11... | collective-permute-start | bytes 811016 | tf_op jit(solution)/shard_map/ppermute | solution.py:385
  28.6 8.5 %collective-permute-start.6 = (bf16[32,4224]{1,0:T(8,128)(2,1)S(1)}, bf16[32,4224]{1,0:T(8,128)(2,1)S(1)}, u32[]{:S(2)}, u32[]{:S(2)}) collective-permute-start(bf16[32,4224]{1,0:T(8,128)(2,1)S(1)} %collective-permute-done.2.top), channel_id=1, source_target_pairs={{0,8},{1,9},{2,10},{3,11},{4,12},{5,13},{6,14},{7,15},{8,0},{9,1},... | collective-permute-start | bytes 811016 | tf_op jit(solution)/shard_map/ppermute | solution.py:373
  33.9 16.9 %collective-permute-start.15 = (bf16[64,4224]{1,0:T(8,128)(2,1)S(1)}, bf16[64,4224]{1,0:T(8,128)(2,1)S(1)}, u32[]{:S(2)}, u32[]{:S(2)}) collective-permute-start(bf16[64,4224]{1,0:T(8,128)(2,1)S(1)} %stack.1.refs_1_.refs_0_), channel_id=1, source_target_pairs={{0,1},{1,0},{2,3},{3,2},{4,5},{5,4},{6,7},{7,6},{8,9},{9,8},{10,11... | collective-permute-start | bytes 1622024 | tf_op jit(solution)/shard_map/ppermute | solution.py:385
  40.8 10.0 %collective-permute-start.14 = (bf16[64,4224]{1,0:T(8,128)(2,1)S(1)}, bf16[64,4224]{1,0:T(8,128)(2,1)S(1)}, u32[]{:S(2)}, u32[]{:S(2)}) collective-permute-start(bf16[64,4224]{1,0:T(8,128)(2,1)S(1)} %collective-permute-done.7.refs_12_.refs_1_), channel_id=1, source_target_pairs={{0,4},{1,3},{2,6},{3,1},{4,0},{5,7},{6,2},{7,5},{8,12},{9,11},{10,... | collective-permute-start | bytes 1622024 | tf_op jit(solution)/shard_map/ppermute | solution.py:373
  41.4 9.4 %collective-permute-start.16 = (bf16[64,4224]{1,0:T(8,128)(2,1)S(1)}, bf16[64,4224]{1,0:T(8,128)(2,1)S(1)}, u32[]{:S(2)}, u32[]{:S(2)}) collective-permute-start(bf16[64,4224]{1,0:T(8,128)(2,1)S(1)} %collective-permute-done.7.refs_12_.refs_1_), channel_id=1, source_target_pairs={{0,1},{1,0},{2,3},{3,2},{4,5},{5,4},{6,7},{7,6},{8,9},{9,8},{10,11... | collective-permute-start | bytes 1622024 | tf_op jit(solution)/shard_map/ppermute | solution.py:385
  41.7 9.1 %collective-permute-start.17 = (bf16[64,4224]{1,0:T(8,128)(2,1)S(1)}, bf16[64,4224]{1,0:T(8,128)(2,1)S(1)}, u32[]{:S(2)}, u32[]{:S(2)}) collective-permute-start(bf16[64,4224]{1,0:T(8,128)(2,1)S(1)} %collective-permute-done.8.refs_2_), channel_id=1, source_target_pairs={{0,1},{1,0},{2,3},{3,2},{4,5},{5,4},{6,7},{7,6},{8,9},{9,8},{10,11... | collective-permute-start | bytes 1622024 | tf_op jit(solution)/shard_map/ppermute | solution.py:385
  41.9 2.8 %copy-start.1 = (bf16[1,768,4096]{2,1,0:T(8,128)(2,1)S(1)}, bf16[1,768,4096]{2,1,0:T(8,128)(2,1)}, u32[]{:S(2)}) copy-start(bf16[1,768,4096]{2,1,0:T(8,128)(2,1)} %param.23) | copy-start | bytes 18874372
  50.8 19.6 %slice-start.2 = ((s8[6291456]{0:T(1024)(128)(4,1)}), s8[4194304]{0:T(1024)(128)(4,1)S(1)}, s32[]{:S(2)}) async-start(s8[6291456]{0:T(1024)(128)(4,1)} %bitcast.17), calls=%async_computation.2 | async-start | bytes 8388608
  50.8 12.9 %copy-start.3 = (bf16[2,1024,1024]{2,1,0:T(8,128)(2,1)S(1)}, bf16[2,1024,1024]{2,1,0:T(8,128)(2,1)}, u32[]{:S(2)}) copy-start(bf16[2,1024,1024]{2,1,0:T(8,128)(2,1)} %cache.7) | copy-start | bytes 12582916
  50.8 19.6 %slice-start.3 = ((s8[6291456]{0:T(1024)(128)(4,1)}), s8[2097152]{0:T(1024)(128)(4,1)S(1)}, s32[]{:S(2)}) async-start(s8[6291456]{0:T(1024)(128)(4,1)} %bitcast.17), calls=%async_computation.3 | async-start | bytes 4194304
  50.8 9.7 %collective-permute-start.20 = (bf16[128,4096]{1,0:T(8,128)(2,1)S(1)}, bf16[128,4096]{1,0:T(8,128)(2,1)S(1)}, u32[]{:S(2)}, u32[]{:S(2)}) collective-permute-start(bf16[128,4096]{1,0:T(8,128)(2,1)S(1)} %get-tuple-element.100), channel_id=1, source_target_pairs={{0,1},{1,0},{2,3},{3,2},{4,5},{5,4},{6,7},{7,6},{8,9},{9,8},{10,11... | collective-permute-start | bytes 3145736 | tf_op jit(solution)/shard_map/ppermute | solution.py:385
  51.2 3.1 %collective-permute-start.21 = (bf16[64,4224]{1,0:T(8,128)(2,1)S(1)}, bf16[64,4224]{1,0:T(8,128)(2,1)S(1)}, u32[]{:S(2)}, u32[]{:S(2)}) collective-permute-start(bf16[64,4224]{1,0:T(8,128)(2,1)S(1)} %collective-permute-done.14.refs_3_), channel_id=1, source_target_pairs={{0,1},{1,0},{2,3},{3,2},{4,5},{5,4},{6,7},{7,6},{8,9},{9,8},{10,11... | collective-permute-start | bytes 1622024 | tf_op jit(solution)/shard_map/ppermute | solution.py:385
  51.4 9.1 %collective-permute-start.18 = (bf16[32,4224]{1,0:T(8,128)(2,1)S(1)}, bf16[32,4224]{1,0:T(8,128)(2,1)S(1)}, u32[]{:S(2)}, u32[]{:S(2)}) collective-permute-start(bf16[32,4224]{1,0:T(8,128)(2,1)S(1)} %collective-permute-done.6.refs_0_), channel_id=1, source_target_pairs={{0,2},{1,5},{2,0},{3,7},{4,6},{5,1},{6,4},{7,3},{8,10},{9,13},{10,... | collective-permute-start | bytes 811016 | tf_op jit(solution)/shard_map/ppermute | solution.py:373
  53.0 7.5 %collective-permute-start.19 = (bf16[32,4224]{1,0:T(8,128)(2,1)S(1)}, bf16[32,4224]{1,0:T(8,128)(2,1)S(1)}, u32[]{:S(2)}, u32[]{:S(2)}) collective-permute-start(bf16[32,4224]{1,0:T(8,128)(2,1)S(1)} %collective-permute-done.6.refs_0_), channel_id=1, source_target_pairs={{0,4},{1,3},{2,6},{3,1},{4,0},{5,7},{6,2},{7,5},{8,12},{9,11},{10,... | collective-permute-start | bytes 811016 | tf_op jit(solution)/shard_map/ppermute | solution.py:373
  53.9 6.6 %collective-permute-start.22 = (bf16[32,4224]{1,0:T(8,128)(2,1)S(1)}, bf16[32,4224]{1,0:T(8,128)(2,1)S(1)}, u32[]{:S(2)}, u32[]{:S(2)}) collective-permute-start(bf16[32,4224]{1,0:T(8,128)(2,1)S(1)} %collective-permute-done.6.refs_0_), channel_id=1, source_target_pairs={{0,1},{1,0},{2,3},{3,2},{4,5},{5,4},{6,7},{7,6},{8,9},{9,8},{10,11... | collective-permute-start | bytes 811016 | tf_op jit(solution)/shard_map/ppermute | solution.py:385
  60.5 7.1 %collective-permute-start.25 = (bf16[128,4096]{1,0:T(8,128)(2,1)S(1)}, bf16[128,4096]{1,0:T(8,128)(2,1)S(1)}, u32[]{:S(2)}, u32[]{:S(2)}) collective-permute-start(bf16[128,4096]{1,0:T(8,128)(2,1)S(1)} %get-tuple-element.113), channel_id=1, source_target_pairs={{0,1},{1,0},{2,3},{3,2},{4,5},{5,4},{6,7},{7,6},{8,9},{9,8},{10,11... | collective-permute-start | bytes 3145736 | tf_op jit(solution)/shard_map/ppermute | solution.py:385
  60.6 6.9 %collective-permute-start.24 = (bf16[32,4224]{1,0:T(8,128)(2,1)S(1)}, bf16[32,4224]{1,0:T(8,128)(2,1)S(1)}, u32[]{:S(2)}, u32[]{:S(2)}) collective-permute-start(bf16[32,4224]{1,0:T(8,128)(2,1)S(1)} %collective-permute-done.18.refs_0_.refs_1_), channel_id=1, source_target_pairs={{0,4},{1,3},{2,6},{3,1},{4,0},{5,7},{6,2},{7,5},{8,12},{9,11},{10,... | collective-permute-start | bytes 811016 | tf_op jit(solution)/shard_map/ppermute | solution.py:373
  62.0 5.5 %collective-permute-start.26 = (bf16[32,4224]{1,0:T(8,128)(2,1)S(1)}, bf16[32,4224]{1,0:T(8,128)(2,1)S(1)}, u32[]{:S(2)}, u32[]{:S(2)}) collective-permute-start(bf16[32,4224]{1,0:T(8,128)(2,1)S(1)} %collective-permute-done.18.refs_0_.refs_1_), channel_id=1, source_target_pairs={{0,1},{1,0},{2,3},{3,2},{4,5},{5,4},{6,7},{7,6},{8,9},{9,8},{10,11... | collective-permute-start | bytes 811016 | tf_op jit(solution)/shard_map/ppermute | solution.py:385
  62.4 5.2 %collective-permute-start.27 = (bf16[32,4224]{1,0:T(8,128)(2,1)S(1)}, bf16[32,4224]{1,0:T(8,128)(2,1)S(1)}, u32[]{:S(2)}, u32[]{:S(2)}) collective-permute-start(bf16[32,4224]{1,0:T(8,128)(2,1)S(1)} %collective-permute-done.19.refs_1_.refs_2_), channel_id=1, source_target_pairs={{0,1},{1,0},{2,3},{3,2},{4,5},{5,4},{6,7},{7,6},{8,9},{9,8},{10,11... | collective-permute-start | bytes 811016 | tf_op jit(solution)/shard_map/ppermute | solution.py:385
  62.7 13.3 %collective-permute-start.23 = (bf16[64,4096]{1,0:T(8,128)(2,1)S(1)}, bf16[64,4096]{1,0:T(8,128)(2,1)S(1)}, u32[]{:S(2)}, u32[]{:S(2)}) collective-permute-start(bf16[64,4096]{1,0:T(8,128)(2,1)S(1)} %add_convert_fusion.3.refs_2_), channel_id=1, source_target_pairs={{0,4},{1,3},{2,6},{3,1},{4,0},{5,7},{6,2},{7,5},{8,12},{9,11},{10,... | collective-permute-start | bytes 1572872 | tf_op jit(solution)/shard_map/ppermute | solution.py:373
  67.7 10.6 %collective-permute-start.28 = (bf16[64,4096]{1,0:T(8,128)(2,1)S(1)}, bf16[64,4096]{1,0:T(8,128)(2,1)S(1)}, u32[]{:S(2)}, u32[]{:S(2)}) collective-permute-start(bf16[64,4096]{1,0:T(8,128)(2,1)S(1)} %add_convert_fusion.2.refs_11_), channel_id=1, source_target_pairs={{0,4},{1,3},{2,6},{3,1},{4,0},{5,7},{6,2},{7,5},{8,12},{9,11},{10,... | collective-permute-start | bytes 1572872 | tf_op jit(solution)/shard_map/ppermute | solution.py:373
  68.8 1.5 %collective-permute-start.29 = (bf16[32,4224]{1,0:T(8,128)(2,1)S(1)}, bf16[32,4224]{1,0:T(8,128)(2,1)S(1)}, u32[]{:S(2)}, u32[]{:S(2)}) collective-permute-start(bf16[32,4224]{1,0:T(8,128)(2,1)S(1)} %collective-permute-done.24.refs_3_), channel_id=1, source_target_pairs={{0,1},{1,0},{2,3},{3,2},{4,5},{5,4},{6,7},{7,6},{8,9},{9,8},{10,11... | collective-permute-start | bytes 811016 | tf_op jit(solution)/shard_map/ppermute | solution.py:385
  78.4 2.7 %collective-permute-start.30 = (bf16[128,4096]{1,0:T(8,128)(2,1)S(1)}, bf16[128,4096]{1,0:T(8,128)(2,1)S(1)}, u32[]{:S(2)}, u32[]{:S(2)}) collective-permute-start(bf16[128,4096]{1,0:T(8,128)(2,1)S(1)} %get-tuple-element.123), channel_id=1, source_target_pairs={{0,1},{1,0},{2,3},{3,2},{4,5},{5,4},{6,7},{7,6},{8,9},{9,8},{10,11... | collective-permute-start | bytes 3145736 | tf_op jit(solution)/shard_map/ppermute | solution.py:385
  78.4 11.1 %collective-permute-start.33 = (bf16[32,4096]{1,0:T(8,128)(2,1)S(1)}, bf16[32,4096]{1,0:T(8,128)(2,1)S(1)}, u32[]{:S(2)}, u32[]{:S(2)}) collective-permute-start(bf16[32,4096]{1,0:T(8,128)(2,1)S(1)} %attend.4.refs_0_), channel_id=1, source_target_pairs={{0,1},{1,0},{2,3},{3,2},{4,5},{5,4},{6,7},{7,6},{8,9},{9,8},{10,11... | collective-permute-start | bytes 786440 | tf_op jit(solution)/shard_map/ppermute | solution.py:385
  78.9 10.6 %collective-permute-start.34 = (bf16[32,4096]{1,0:T(8,128)(2,1)S(1)}, bf16[32,4096]{1,0:T(8,128)(2,1)S(1)}, u32[]{:S(2)}, u32[]{:S(2)}) collective-permute-start(bf16[32,4096]{1,0:T(8,128)(2,1)S(1)} %attend.5.refs_11_.refs_4_), channel_id=1, source_target_pairs={{0,1},{1,0},{2,3},{3,2},{4,5},{5,4},{6,7},{7,6},{8,9},{9,8},{10,11... | collective-permute-start | bytes 786440 | tf_op jit(solution)/shard_map/ppermute | solution.py:385
  78.9 10.6 %collective-permute-start.35 = (bf16[32,4096]{1,0:T(8,128)(2,1)S(1)}, bf16[32,4096]{1,0:T(8,128)(2,1)S(1)}, u32[]{:S(2)}, u32[]{:S(2)}) collective-permute-start(bf16[32,4096]{1,0:T(8,128)(2,1)S(1)} %attend.6.refs_1_), channel_id=1, source_target_pairs={{0,1},{1,0},{2,3},{3,2},{4,5},{5,4},{6,7},{7,6},{8,9},{9,8},{10,11... | collective-permute-start | bytes 786440 | tf_op jit(solution)/shard_map/ppermute | solution.py:385
  81.2 12.1 %collective-permute-start.31 = (bf16[64,4096]{1,0:T(8,128)(2,1)S(1)}, bf16[64,4096]{1,0:T(8,128)(2,1)S(1)}, u32[]{:S(2)}, u32[]{:S(2)}) collective-permute-start(bf16[64,4096]{1,0:T(8,128)(2,1)S(1)} %add_convert_fusion.1.refs_11_), channel_id=1, source_target_pairs={{0,4},{1,3},{2,6},{3,1},{4,0},{5,7},{6,2},{7,5},{8,12},{9,11},{10,... | collective-permute-start | bytes 1572872 | tf_op jit(solution)/shard_map/ppermute | solution.py:373
  82.7 9.3 %collective-permute-start.32 = (bf16[32,4096]{1,0:T(8,128)(2,1)S(1)}, bf16[32,4096]{1,0:T(8,128)(2,1)S(1)}, u32[]{:S(2)}, u32[]{:S(2)}) collective-permute-start(bf16[32,4096]{1,0:T(8,128)(2,1)S(1)} %add_convert_fusion.11.refs_12_), channel_id=1, source_target_pairs={{0,2},{1,5},{2,0},{3,7},{4,6},{5,1},{6,4},{7,3},{8,10},{9,13},{10,... | collective-permute-start | bytes 786440 | tf_op jit(solution)/shard_map/ppermute | solution.py:373
  93.2 2.7 %collective-permute-start.36 = (bf16[128,4096]{1,0:T(8,128)(2,1)S(1)}, bf16[128,4096]{1,0:T(8,128)(2,1)S(1)}, u32[]{:S(2)}, u32[]{:S(2)}) collective-permute-start(bf16[128,4096]{1,0:T(8,128)(2,1)S(1)} %get-tuple-element.132), channel_id=1, source_target_pairs={{0,1},{1,0},{2,3},{3,2},{4,5},{5,4},{6,7},{7,6},{8,9},{9,8},{10,11... | collective-permute-start | bytes 3145736 | tf_op jit(solution)/shard_map/ppermute | solution.py:385
  93.3 15.3 %collective-permute-start.40 = (bf16[32,4096]{1,0:T(8,128)(2,1)S(1)}, bf16[32,4096]{1,0:T(8,128)(2,1)S(1)}, u32[]{:S(2)}, u32[]{:S(2)}) collective-permute-start(bf16[32,4096]{1,0:T(8,128)(2,1)S(1)} %add_convert_fusion.8), channel_id=1, source_target_pairs={{0,16},{1,17},{2,18},{3,19},{4,20},{5,21},{6,22},{7,23},{8,24},{9,... | collective-permute-start | bytes 786440 | tf_op jit(solution)/shard_map/ppermute | solution.py:373
  96.0 12.7 %collective-permute-start.39 = (bf16[64,4096]{1,0:T(8,128)(2,1)S(1)}, bf16[64,4096]{1,0:T(8,128)(2,1)S(1)}, u32[]{:S(2)}, u32[]{:S(2)}) collective-permute-start(bf16[64,4096]{1,0:T(8,128)(2,1)S(1)} %add_convert_fusion), channel_id=1, source_target_pairs={{0,4},{1,3},{2,6},{3,1},{4,0},{5,7},{6,2},{7,5},{8,12},{9,11},{10,... | collective-permute-start | bytes 1572872 | tf_op jit(solution)/shard_map/ppermute | solution.py:373
  97.5 12.4 %collective-permute-start.37 = (bf16[32,4096]{1,0:T(8,128)(2,1)S(1)}, bf16[32,4096]{1,0:T(8,128)(2,1)S(1)}, u32[]{:S(2)}, u32[]{:S(2)}) collective-permute-start(bf16[32,4096]{1,0:T(8,128)(2,1)S(1)} %add_convert_fusion.10), channel_id=1, source_target_pairs={{0,2},{1,5},{2,0},{3,7},{4,6},{5,1},{6,4},{7,3},{8,10},{9,13},{10,... | collective-permute-start | bytes 786440 | tf_op jit(solution)/shard_map/ppermute | solution.py:373
  108.8 8.4 %collective-permute-start.42 = (bf16[32,4096]{1,0:T(8,128)(2,1)S(1)}, bf16[32,4096]{1,0:T(8,128)(2,1)S(1)}, u32[]{:S(2)}, u32[]{:S(2)}) collective-permute-start(bf16[32,4096]{1,0:T(8,128)(2,1)S(1)} %add_convert_fusion.7.refs_1_), channel_id=1, source_target_pairs={{0,2},{1,5},{2,0},{3,7},{4,6},{5,1},{6,4},{7,3},{8,10},{9,13},{10,... | collective-permute-start | bytes 786440 | tf_op jit(solution)/shard_map/ppermute | solution.py:373
  110.0 10.1 %collective-permute-start.38 = (bf16[32,4096]{1,0:T(8,128)(2,1)S(1)}, bf16[32,4096]{1,0:T(8,128)(2,1)S(1)}, u32[]{:S(2)}, u32[]{:S(2)}) collective-permute-start(bf16[32,4096]{1,0:T(8,128)(2,1)S(1)} %add_convert_fusion.9.refs_0_), channel_id=1, source_target_pairs={{0,24},{1,25},{2,26},{3,27},{4,28},{5,29},{6,30},{7,31},{8,16},{9,... | collective-permute-start | bytes 786440 | tf_op jit(solution)/shard_map/ppermute | solution.py:373
  117.1 3.0 %collective-permute-start.41 = (bf16[32,4096]{1,0:T(8,128)(2,1)S(1)}, bf16[32,4096]{1,0:T(8,128)(2,1)S(1)}, u32[]{:S(2)}, u32[]{:S(2)}) collective-permute-start(bf16[32,4096]{1,0:T(8,128)(2,1)S(1)} %attend.7.refs_5_), channel_id=1, source_target_pairs={{0,1},{1,0},{2,3},{3,2},{4,5},{5,4},{6,7},{7,6},{8,9},{9,8},{10,11... | collective-permute-start | bytes 786440 | tf_op jit(solution)/shard_map/ppermute | solution.py:385
  117.3 8.8 %collective-permute-start.43 = (bf16[32,4096]{1,0:T(8,128)(2,1)S(1)}, bf16[32,4096]{1,0:T(8,128)(2,1)S(1)}, u32[]{:S(2)}, u32[]{:S(2)}) collective-permute-start(bf16[32,4096]{1,0:T(8,128)(2,1)S(1)} %add_convert_fusion.6), channel_id=1, source_target_pairs={{0,8},{1,9},{2,10},{3,11},{4,12},{5,13},{6,14},{7,15},{8,0},{9,1},... | collective-permute-start | bytes 786440 | tf_op jit(solution)/shard_map/ppermute | solution.py:373
  117.4 8.7 %collective-permute-start.44 = (bf16[32,4096]{1,0:T(8,128)(2,1)S(1)}, bf16[32,4096]{1,0:T(8,128)(2,1)S(1)}, u32[]{:S(2)}, u32[]{:S(2)}) collective-permute-start(bf16[32,4096]{1,0:T(8,128)(2,1)S(1)} %add_convert_fusion.5), channel_id=1, source_target_pairs={{0,2},{1,5},{2,0},{3,7},{4,6},{5,1},{6,4},{7,3},{8,10},{9,13},{10,... | collective-permute-start | bytes 786440 | tf_op jit(solution)/shard_map/ppermute | solution.py:373

commit v5 on v4

--- a/solution.py
+++ b/solution.py
@@ -474,15 +474,14 @@
     held_3, passed_3 = sum_cross(result_3, back_3, turned_3)
     passed_3, back_1 = sync((passed_3, back_1))
     there_1 = sum_cores(result_1, back_1)
-    total_3 = narrow(held_3 + widen(near(passed_3)))
-    far_3 = far(total_3, 3)
-    turned_1, far_2 = sync((cross(there_1), far_2))
+    context_1b = attend_half(1, 1, there_1)
+    ended_3, turned_1, context_1b = sync((near(passed_3), cross(there_1), context_1b))
+    far_3 = far(narrow(held_3 + widen(ended_3)), 3)
     held_1, passed_1 = sum_cross(result_1, back_1, turned_1)
-    context_1b = attend_half(1, 1, total_3, passed_1)
     contexts = [context_0a, context_0b, context_1a, context_1b]
     sent = [*sent, beside(context_1b)]
     ordered = [contexts[0], contexts[2], sent[0], sent[2], contexts[1], contexts[3], sent[1], sent[3]]
-    own_late, far_3 = sync((own_mine, far_3))
+    own_late, far_2, far_3 = sync((own_mine, far_2, far_3))
     context = place_context(own_late, ordered, jax.ShapeDtypeStruct(queries.shape, jnp.bfloat16))
     total_1, passed_0 = sync((narrow(held_1 + widen(near(passed_1))), passed_0))
     far_1 = far(total_1, 1)

time: 127 us -> 126 us (level)
  waiting for transfers between devices: 37 us -> 33.8 us
  starting transfers between devices: 37 us -> 38.7 us
    ppermute x23, waiting for transfers between devices: 32.3 us -> 27.8 us  [swap(): return lax.ppermute(value, ('ep', 'fan'), pairs)]
    ppermute x23, starting transfers between devices: 32.9 us -> 34.7 us  [swap(): return lax.ppermute(value, ('ep', 'fan'), pairs)]
    ppermute x22, waiting for transfers between devices: 4.75 us -> 6.07 us  [beside(): return lax.ppermute(value, 'fan', [(0, 1), (1, 0)])]
  transfers between devices with their start and end apart: 45 -> 45, of which waited for: 16 -> 19; matrix products, arithmetic and copies ran while one was open for 1% -> 1% of each run, Pallas kernels for 31% -> 31%
where the time goes in v5:
time: 126 us
  Pallas kernels  41.4 us (33%)
  starting transfers between devices  38.7 us (31%)
  waiting for transfers between devices  33.8 us (27%)
  local copies, waits for them, and re-layouts  8.44 us (7%)
  other arithmetic  2.23 us (2%)
    ppermute x23, starting transfers between devices, swap(): return lax.ppermute(value, ('ep', 'fan'), pairs)  34.7 us
    ppermute x23, waiting for transfers between devices, swap(): return lax.ppermute(value, ('ep', 'fan'), pairs)  27.8 us
    pallas_call x4, Pallas kernels, expert_chunk(): pl.pallas_call(functools.partial(expert_kernel, count, at_row, tokens), o...  22.3 us
    pallas_call x4, Pallas kernels, attend(): pl.pallas_call(functools.partial(attend_kernel, local, heads), out_shape=...  15.2 us
    unnamed x26, local copies, waits for them, and re-layouts  8.44 us
    ppermute x22, waiting for transfers between devices, beside(): return lax.ppermute(value, 'fan', [(0, 1), (1, 0)])  6.07 us
    ppermute x22, starting transfers between devices, beside(): return lax.ppermute(value, 'fan', [(0, 1), (1, 0)])  4 us
  transfers between devices with their start and end apart: 45, of which 19 were waited for; matrix products, arithmetic and copies ran while one was open for 1% of the time, Pallas kernels for 31%

profile of v5, /device:TPU:0, one launch (start us, length us, event | category | flops | bytes accessed | tf_op | source)
XLA Modules:
  0.0 125.6 jit_solution(14910952003276873772)
XLA Ops:
  0.6 1.9 %norm_message.1.refs_0_ = bf16[32,4224]{1,0:T(8,128)(2,1)} custom-call(bf16[32,4096]{1,0:T(8,128)(2,1)} %hidden_ref.1, bf16[4096]{0:T(1024)(128)(2,1)} %gain_ref.1, s32[8,32]{1,0:T(8,128)} %bitcast.21, f32[8,32]{1,0:T(8,128)} %bitcast.22), custom_call_target="tpu_custom_call" | custom-call | flops 1048576 | bytes 16384 | tf_op jit(solution)/shard_map/norm_message/pallas_call | solution.py:63
  2.6 1.2 copy-done.4
  3.8 0.9 copy-done.5
  4.7 0.7 copy-done.8
  5.6 0.5 collective-permute-start
  6.1 2.5 %collective-permute-start.4 = (bf16[32,4224]{1,0:T(8,128)(2,1)}, bf16[32,4224]{1,0:T(8,128)(2,1)S(1)}, u32[]{:S(2)}, u32[]{:S(2)}) collective-permute-start(bf16[32,4224]{1,0:T(8,128)(2,1)} %norm_message.1.refs_0_), channel_id=1, source_target_pairs={{0,2},{1,5},{2,0},{3,7},{4,6},{5,1},{6,4},{7,3},{8,10},{9,13},{10,... | collective-permute-start | bytes 811016 | tf_op jit(solution)/shard_map/ppermute | solution.py:373
  8.8 1.3 %collective-permute-start.9 = (bf16[32,4224]{1,0:T(8,128)(2,1)}, bf16[32,4224]{1,0:T(8,128)(2,1)S(1)}, u32[]{:S(2)}, u32[]{:S(2)}) collective-permute-start(bf16[32,4224]{1,0:T(8,128)(2,1)} %norm_message.1.refs_0_), channel_id=1, source_target_pairs={{0,4},{1,3},{2,6},{3,1},{4,0},{5,7},{6,2},{7,5},{8,12},{9,11},{10,... | collective-permute-start | bytes 811016 | tf_op jit(solution)/shard_map/ppermute | solution.py:373
  10.1 2.6 %collective-permute-start.2 = (bf16[32,4224]{1,0:T(8,128)(2,1)}, bf16[32,4224]{1,0:T(8,128)(2,1)S(1)}, u32[]{:S(2)}, u32[]{:S(2)}) collective-permute-start(bf16[32,4224]{1,0:T(8,128)(2,1)} %norm_message.1.refs_0_), channel_id=1, source_target_pairs={{0,16},{1,17},{2,18},{3,19},{4,20},{5,21},{6,22},{7,23},{8,24},{9,... | collective-permute-start | bytes 811016 | tf_op jit(solution)/shard_map/ppermute | solution.py:373
  12.7 1.6 %collective-permute-start.3 = (bf16[32,4224]{1,0:T(8,128)(2,1)}, bf16[32,4224]{1,0:T(8,128)(2,1)S(1)}, u32[]{:S(2)}, u32[]{:S(2)}) collective-permute-start(bf16[32,4224]{1,0:T(8,128)(2,1)} %norm_message.1.refs_0_), channel_id=1, source_target_pairs={{0,8},{1,9},{2,10},{3,11},{4,12},{5,13},{6,14},{7,15},{8,0},{9,1},... | collective-permute-start | bytes 811016 | tf_op jit(solution)/shard_map/ppermute | solution.py:373
  14.3 0.8 collective-permute-done.4.refs_1_
  15.1 2.2 %collective-permute-start.5 = (bf16[32,4224]{1,0:T(8,128)(2,1)S(1)}, bf16[32,4224]{1,0:T(8,128)(2,1)S(1)}, u32[]{:S(2)}, u32[]{:S(2)}) collective-permute-start(bf16[32,4224]{1,0:T(8,128)(2,1)S(1)} %collective-permute-done.4.refs_1_), channel_id=1, source_target_pairs={{0,4},{1,3},{2,6},{3,1},{4,0},{5,7},{6,2},{7,5},{8,12},{9,11},{10,... | collective-permute-start | bytes 811016 | tf_op jit(solution)/shard_map/ppermute | solution.py:373
  17.2 2.2 %copy-done.2 = bf16[2,1024,1024]{2,1,0:T(8,128)(2,1)S(1)} copy-done((bf16[2,1024,1024]{2,1,0:T(8,128)(2,1)S(1)}, bf16[2,1024,1024]{2,1,0:T(8,128)(2,1)}, u32[]{:S(2)}) %copy-start.2) | copy-done | bytes 4194328
  19.4 0.7 copy-done.6
  20.1 3.8 %attend.4.refs_0_ = bf16[32,4096]{1,0:T(8,128)(2,1)S(1)} custom-call(s32[4]{0:T(128)S(1)} %copy-done.6, bf16[64,8192]{1,0:T(8,128)(2,1)S(1)} %get-tuple-element.79.q_mine, bf16[64,8192]{1,0:T(8,128)(2,1)S(1)} %collective-permute-done.q_other, bf16[64,1152]{1,0:T(8,128)(2,1)S(1)} %get-tuple-element.140.o_mine, ...), custom_call_target="tpu_custom_call" | custom-call | flops 1048576 | bytes 16384 | tf_op jit(solution)/shard_map/attend/pallas_call | solution.py:223
  23.9 1.5 %collective-permute-done.2.top = bf16[32,4224]{1,0:T(8,128)(2,1)S(1)} collective-permute-done((bf16[32,4224]{1,0:T(8,128)(2,1)}, bf16[32,4224]{1,0:T(8,128)(2,1)S(1)}, u32[]{:S(2)}, u32[]{:S(2)}) %collective-permute-start.2) | collective-permute-done | bytes 270368 | tf_op jit(solution)/shard_map/ppermute | solution.py:373
  25.7 1.3 %collective-permute-start.7 = (bf16[64,4224]{1,0:T(8,128)(2,1)S(1)}, bf16[64,4224]{1,0:T(8,128)(2,1)S(1)}, u32[]{:S(2)}, u32[]{:S(2)}) collective-permute-start(bf16[64,4224]{1,0:T(8,128)(2,1)S(1)} %stack.1.refs_1_.refs_0_), channel_id=1, source_target_pairs={{0,2},{1,5},{2,0},{3,7},{4,6},{5,1},{6,4},{7,3},{8,10},{9,13},{10,... | collective-permute-start | bytes 1622024 | tf_op jit(solution)/shard_map/ppermute | solution.py:373
  27.0 1.1 collective-permute-start.8
  28.1 0.5 collective-permute-start.13
  28.6 1.4 %collective-permute-start.6 = (bf16[32,4224]{1,0:T(8,128)(2,1)S(1)}, bf16[32,4224]{1,0:T(8,128)(2,1)S(1)}, u32[]{:S(2)}, u32[]{:S(2)}) collective-permute-start(bf16[32,4224]{1,0:T(8,128)(2,1)S(1)} %collective-permute-done.2.top), channel_id=1, source_target_pairs={{0,8},{1,9},{2,10},{3,11},{4,12},{5,13},{6,14},{7,15},{8,0},{9,1},... | collective-permute-start | bytes 811016 | tf_op jit(solution)/shard_map/ppermute | solution.py:373
  30.0 3.8 %attend.5.refs_11_.refs_4_ = bf16[32,4096]{1,0:T(8,128)(2,1)S(1)} custom-call(s32[4]{0:T(128)S(1)} %copy-done.7, bf16[64,8192]{1,0:T(8,128)(2,1)S(1)} %get-tuple-element.79.q_mine, bf16[64,8192]{1,0:T(8,128)(2,1)S(1)} %collective-permute-done.q_other, bf16[64,1152]{1,0:T(8,128)(2,1)S(1)} %get-tuple-element.140.o_mine, ...), custom_call_target="tpu_custom_call" | custom-call | flops 1048576 | bytes 16384 | tf_op jit(solution)/shard_map/attend/pallas_call | solution.py:223
  33.9 3.1 %collective-permute-done.6.refs_0_ = bf16[32,4224]{1,0:T(8,128)(2,1)S(1)} collective-permute-done((bf16[32,4224]{1,0:T(8,128)(2,1)S(1)}, bf16[32,4224]{1,0:T(8,128)(2,1)S(1)}, u32[]{:S(2)}, u32[]{:S(2)}) %collective-permute-start.6) | collective-permute-done | bytes 270368 | tf_op jit(solution)/shard_map/ppermute | solution.py:373
  37.0 3.7 %collective-permute-done.7.refs_12_.refs_1_ = bf16[64,4224]{1,0:T(8,128)(2,1)S(1)} collective-permute-done((bf16[64,4224]{1,0:T(8,128)(2,1)S(1)}, bf16[64,4224]{1,0:T(8,128)(2,1)S(1)}, u32[]{:S(2)}, u32[]{:S(2)}) %collective-permute-start.7) | collective-permute-done | bytes 540704 | tf_op jit(solution)/shard_map/ppermute | solution.py:373
  40.8 0.6 collective-permute-start.16
  41.9 2.8 %copy-done.1 = bf16[1,768,4096]{2,1,0:T(8,128)(2,1)S(1)} copy-done((bf16[1,768,4096]{2,1,0:T(8,128)(2,1)S(1)}, bf16[1,768,4096]{2,1,0:T(8,128)(2,1)}, u32[]{:S(2)}) %copy-start.1) | copy-done | bytes 6291480
  44.7 6.1 %expert_chunk.4 = (bf16[64,4096]{1,0:T(8,128)(2,1)S(1)}, bf16[64,4096]{1,0:T(8,128)(2,1)S(1)}, bf16[128,4096]{1,0:T(8,128)(2,1)S(1)}) custom-call(bf16[32,4224]{1,0:T(8,128)(2,1)} %norm_message.1.refs_0_, bf16[32,4224]{1,0:T(8,128)(2,1)S(1)} %collective-permute-done.4.refs_1_, bf16[32,4224]{1,0:T(8,128)(2,1)S(1)} %collective-permute-done.9.refs_2_, ...), custom_call_target="tpu_custom_call" | custom-call | flops 1048576 | bytes 16384 | tf_op jit(solution)/shard_map/expert_chunk/pallas_call | solution.py:327
  50.8 0.4 collective-permute-start.20
  51.4 1.6 %collective-permute-start.14 = (bf16[32,4224]{1,0:T(8,128)(2,1)S(1)}, bf16[32,4224]{1,0:T(8,128)(2,1)S(1)}, u32[]{:S(2)}, u32[]{:S(2)}) collective-permute-start(bf16[32,4224]{1,0:T(8,128)(2,1)S(1)} %collective-permute-done.6.refs_0_), channel_id=1, source_target_pairs={{0,2},{1,5},{2,0},{3,7},{4,6},{5,1},{6,4},{7,3},{8,10},{9,13},{10,... | collective-permute-start | bytes 811016 | tf_op jit(solution)/shard_map/ppermute | solution.py:373
  53.0 0.9 collective-permute-start.15
  53.9 0.4 collective-permute-done.21.refs_7_
  54.3 5.3 %expert_chunk.5 = (bf16[64,4096]{1,0:T(8,128)(2,1)S(1)}, bf16[64,4096]{1,0:T(8,128)(2,1)S(1)}, bf16[128,4096]{1,0:T(8,128)(2,1)S(1)}) custom-call(bf16[64,4224]{1,0:T(8,128)(2,1)S(1)} %stack.1.refs_1_.refs_0_, bf16[64,4224]{1,0:T(8,128)(2,1)S(1)} %collective-permute-done.7.refs_12_.refs_1_, bf16[64,4224]{1,0:T(8,128)(2,1)S(1)} %collective-permute-done.8.refs_2_, ...), custom_call_target="tpu_custom_call" | custom-call | flops 1048576 | bytes 16384 | tf_op jit(solution)/shard_map/expert_chunk/pallas_call | solution.py:327
  59.7 0.8 collective-permute-done.14.refs_0_.refs_1_
  60.6 1.4 %collective-permute-start.23 = (bf16[32,4224]{1,0:T(8,128)(2,1)S(1)}, bf16[32,4224]{1,0:T(8,128)(2,1)S(1)}, u32[]{:S(2)}, u32[]{:S(2)}) collective-permute-start(bf16[32,4224]{1,0:T(8,128)(2,1)S(1)} %collective-permute-done.14.refs_0_.refs_1_), channel_id=1, source_target_pairs={{0,4},{1,3},{2,6},{3,1},{4,0},{5,7},{6,2},{7,5},{8,12},{9,11},{10,... | collective-permute-start | bytes 811016 | tf_op jit(solution)/shard_map/ppermute | solution.py:373
  62.0 0.4 collective-permute-start.25
  62.7 1.1 collective-permute-start.27
  63.8 3.8 %attend.6.refs_1_ = bf16[32,4096]{1,0:T(8,128)(2,1)S(1)} custom-call(s32[4]{0:T(128)S(1)} %copy-done.7, bf16[64,8192]{1,0:T(8,128)(2,1)S(1)} %get-tuple-element.79.q_mine, bf16[64,8192]{1,0:T(8,128)(2,1)S(1)} %collective-permute-done.q_other, bf16[64,1152]{1,0:T(8,128)(2,1)S(1)} %get-tuple-element.140.o_mine, ...), custom_call_target="tpu_custom_call" | custom-call | flops 1048576 | bytes 16384 | tf_op jit(solution)/shard_map/attend/pallas_call | solution.py:223
  67.7 1.1 collective-permute-start.28
  68.8 1.5 %collective-permute-done.29.refs_7_ = bf16[32,4224]{1,0:T(8,128)(2,1)S(1)} collective-permute-done((bf16[32,4224]{1,0:T(8,128)(2,1)S(1)}, bf16[32,4224]{1,0:T(8,128)(2,1)S(1)}, u32[]{:S(2)}, u32[]{:S(2)}) %collective-permute-start.29) | collective-permute-done | bytes 270368 | tf_op jit(solution)/shard_map/ppermute | solution.py:385
  70.4 5.6 %expert_chunk.6 = (bf16[64,4096]{1,0:T(8,128)(2,1)S(1)}, bf16[64,4096]{1,0:T(8,128)(2,1)S(1)}, bf16[128,4096]{1,0:T(8,128)(2,1)S(1)}) custom-call(bf16[32,4224]{1,0:T(8,128)(2,1)S(1)} %collective-permute-done.6.refs_0_, bf16[32,4224]{1,0:T(8,128)(2,1)S(1)} %collective-permute-done.14.refs_0_.refs_1_, ...), custom_call_target="tpu_custom_call" | custom-call | flops 1048576 | bytes 16384 | tf_op jit(solution)/shard_map/expert_chunk/pallas_call | solution.py:327
  76.0 2.4 %collective-permute-done.28 = bf16[64,4096]{1,0:T(8,128)(2,1)S(1)} collective-permute-done((bf16[64,4096]{1,0:T(8,128)(2,1)S(1)}, bf16[64,4096]{1,0:T(8,128)(2,1)S(1)}, u32[]{:S(2)}, u32[]{:S(2)}) %collective-permute-start.28) | collective-permute-done | bytes 524320 | tf_op jit(solution)/shard_map/ppermute | solution.py:373
  78.4 0.5 collective-permute-start.33
  78.9 0.5 collective-permute-start.35
  79.4 1.6 %collective-permute-done.30 = bf16[128,4096]{1,0:T(8,128)(2,1)S(1)} collective-permute-done((bf16[128,4096]{1,0:T(8,128)(2,1)S(1)}, bf16[128,4096]{1,0:T(8,128)(2,1)S(1)}, u32[]{:S(2)}, u32[]{:S(2)}) %collective-permute-start.30) | collective-permute-done | bytes 1048608 | tf_op jit(solution)/shard_map/ppermute | solution.py:385
  81.2 1.4 %collective-permute-start.31 = (bf16[64,4096]{1,0:T(8,128)(2,1)S(1)}, bf16[64,4096]{1,0:T(8,128)(2,1)S(1)}, u32[]{:S(2)}, u32[]{:S(2)}) collective-permute-start(bf16[64,4096]{1,0:T(8,128)(2,1)S(1)} %add_convert_fusion.1.refs_11_), channel_id=1, source_target_pairs={{0,4},{1,3},{2,6},{3,1},{4,0},{5,7},{6,2},{7,5},{8,12},{9,11},{10,... | collective-permute-start | bytes 1572872 | tf_op jit(solution)/shard_map/ppermute | solution.py:373
  82.7 1.4 %collective-permute-start.32 = (bf16[32,4096]{1,0:T(8,128)(2,1)S(1)}, bf16[32,4096]{1,0:T(8,128)(2,1)S(1)}, u32[]{:S(2)}, u32[]{:S(2)}) collective-permute-start(bf16[32,4096]{1,0:T(8,128)(2,1)S(1)} %add_convert_fusion.11.refs_12_), channel_id=1, source_target_pairs={{0,2},{1,5},{2,0},{3,7},{4,6},{5,1},{6,4},{7,3},{8,10},{9,13},{10,... | collective-permute-start | bytes 786440 | tf_op jit(solution)/shard_map/ppermute | solution.py:373
  84.1 5.3 %expert_chunk.7 = (bf16[64,4096]{1,0:T(8,128)(2,1)S(1)}, bf16[64,4096]{1,0:T(8,128)(2,1)S(1)}, bf16[128,4096]{1,0:T(8,128)(2,1)S(1)}) custom-call(bf16[64,4224]{1,0:T(8,128)(2,1)S(1)} %stack.1.refs_1_.refs_0_, bf16[64,4224]{1,0:T(8,128)(2,1)S(1)} %collective-permute-done.7.refs_12_.refs_1_, bf16[64,4224]{1,0:T(8,128)(2,1)S(1)} %collective-permute-done.8.refs_2_, ...), custom_call_target="tpu_custom_call" | custom-call | flops 1048576 | bytes 16384 | tf_op jit(solution)/shard_map/expert_chunk/pallas_call | solution.py:327
  89.5 2.5 %collective-permute-done.32 = bf16[32,4096]{1,0:T(8,128)(2,1)S(1)} collective-permute-done((bf16[32,4096]{1,0:T(8,128)(2,1)S(1)}, bf16[32,4096]{1,0:T(8,128)(2,1)S(1)}, u32[]{:S(2)}, u32[]{:S(2)}) %collective-permute-start.32) | collective-permute-done | bytes 262176 | tf_op jit(solution)/shard_map/ppermute | solution.py:373
  92.0 1.2 collective-permute-done.31
  93.4 2.4 %collective-permute-done.37 = bf16[128,4096]{1,0:T(8,128)(2,1)S(1)} collective-permute-done((bf16[128,4096]{1,0:T(8,128)(2,1)S(1)}, bf16[128,4096]{1,0:T(8,128)(2,1)S(1)}, u32[]{:S(2)}, u32[]{:S(2)}) %collective-permute-start.37) | collective-permute-done | bytes 1048608 | tf_op jit(solution)/shard_map/ppermute | solution.py:385
  96.0 1.4 %collective-permute-start.39 = (bf16[64,4096]{1,0:T(8,128)(2,1)S(1)}, bf16[64,4096]{1,0:T(8,128)(2,1)S(1)}, u32[]{:S(2)}, u32[]{:S(2)}) collective-permute-start(bf16[64,4096]{1,0:T(8,128)(2,1)S(1)} %add_convert_fusion.refs_0_), channel_id=1, source_target_pairs={{0,4},{1,3},{2,6},{3,1},{4,0},{5,7},{6,2},{7,5},{8,12},{9,11},{10,... | collective-permute-start | bytes 1572872 | tf_op jit(solution)/shard_map/ppermute | solution.py:373
  97.4 1.1 collective-permute-start.38
  98.6 1.2 collective-permute-start.36
  99.8 3.8 %attend.7.refs_5_ = bf16[32,4096]{1,0:T(8,128)(2,1)S(1)} custom-call(s32[4]{0:T(128)S(1)} %copy-done.7, bf16[64,8192]{1,0:T(8,128)(2,1)S(1)} %get-tuple-element.79.q_mine, bf16[64,8192]{1,0:T(8,128)(2,1)S(1)} %collective-permute-done.q_other, bf16[64,1152]{1,0:T(8,128)(2,1)S(1)} %get-tuple-element.140.o_mine, ...), custom_call_target="tpu_custom_call" | custom-call | flops 1048576 | bytes 16384 | tf_op jit(solution)/shard_map/attend/pallas_call | solution.py:223
  103.6 3.0 %collective-permute-done.38 = bf16[32,4096]{1,0:T(8,128)(2,1)S(1)} collective-permute-done((bf16[32,4096]{1,0:T(8,128)(2,1)S(1)}, bf16[32,4096]{1,0:T(8,128)(2,1)S(1)}, u32[]{:S(2)}, u32[]{:S(2)}) %collective-permute-start.38) | collective-permute-done | bytes 262176 | tf_op jit(solution)/shard_map/ppermute | solution.py:373
  106.7 1.4 %collective-permute-done.39 = bf16[64,4096]{1,0:T(8,128)(2,1)S(1)} collective-permute-done((bf16[64,4096]{1,0:T(8,128)(2,1)S(1)}, bf16[64,4096]{1,0:T(8,128)(2,1)S(1)}, u32[]{:S(2)}, u32[]{:S(2)}) %collective-permute-start.39) | collective-permute-done | bytes 524320 | tf_op jit(solution)/shard_map/ppermute | solution.py:373
  108.1 1.0 collective-permute-start.42
  109.3 3.9 %collective-permute-start.40 = (bf16[32,4096]{1,0:T(8,128)(2,1)S(1)}, bf16[32,4096]{1,0:T(8,128)(2,1)S(1)}, u32[]{:S(2)}, u32[]{:S(2)}) collective-permute-start(bf16[32,4096]{1,0:T(8,128)(2,1)S(1)} %add_convert_fusion.8), channel_id=1, source_target_pairs={{0,24},{1,25},{2,26},{3,27},{4,28},{5,29},{6,30},{7,31},{8,16},{9,... | collective-permute-start | bytes 786440 | tf_op jit(solution)/shard_map/ppermute | solution.py:373
  113.1 1.4 %collective-permute-done.42 = bf16[32,4096]{1,0:T(8,128)(2,1)S(1)} collective-permute-done((bf16[32,4096]{1,0:T(8,128)(2,1)S(1)}, bf16[32,4096]{1,0:T(8,128)(2,1)S(1)}, u32[]{:S(2)}, u32[]{:S(2)}) %collective-permute-start.42) | collective-permute-done | bytes 262176 | tf_op jit(solution)/shard_map/ppermute | solution.py:373
  114.7 1.7 %collective-permute-start.43 = (bf16[32,4096]{1,0:T(8,128)(2,1)S(1)}, bf16[32,4096]{1,0:T(8,128)(2,1)S(1)}, u32[]{:S(2)}, u32[]{:S(2)}) collective-permute-start(bf16[32,4096]{1,0:T(8,128)(2,1)S(1)} %add_convert_fusion.6), channel_id=1, source_target_pairs={{0,8},{1,9},{2,10},{3,11},{4,12},{5,13},{6,14},{7,15},{8,0},{9,1},... | collective-permute-start | bytes 786440 | tf_op jit(solution)/shard_map/ppermute | solution.py:373
  116.4 0.9 collective-permute-start.44
  117.3 1.2 collective-permute-done.36
  118.5 1.4 %collective-permute-done.40 = bf16[32,4096]{1,0:T(8,128)(2,1)S(1)} collective-permute-done((bf16[32,4096]{1,0:T(8,128)(2,1)S(1)}, bf16[32,4096]{1,0:T(8,128)(2,1)S(1)}, u32[]{:S(2)}, u32[]{:S(2)}) %collective-permute-start.40) | collective-permute-done | bytes 262176 | tf_op jit(solution)/shard_map/ppermute | solution.py:373
  119.9 1.6 %place_context.1 = bf16[32,2,8192]{2,1,0:T(2,128)(2,1)} custom-call(bf16[64,1152]{1,0:T(8,128)(2,1)S(1)} %get-tuple-element.140.o_mine, bf16[32,4096]{1,0:T(8,128)(2,1)S(1)} %attend.4.refs_0_, bf16[32,4096]{1,0:T(8,128)(2,1)S(1)} %attend.6.refs_1_, bf16[32,4096]{1,0:T(8,128)(2,1)S(1)} %collective-permute-done.33.refs_2_, ...), custom_call_target="tpu_custom_call" | custom-call | flops 1048576 | bytes 16384 | tf_op jit(solution)/shard_map/place_context/pallas_call | solution.py:273
  121.5 3.1 %collective-permute-done.43 = bf16[32,4096]{1,0:T(8,128)(2,1)S(1)} collective-permute-done((bf16[32,4096]{1,0:T(8,128)(2,1)S(1)}, bf16[32,4096]{1,0:T(8,128)(2,1)S(1)}, u32[]{:S(2)}, u32[]{:S(2)}) %collective-permute-start.43) | collective-permute-done | bytes 262176 | tf_op jit(solution)/shard_map/ppermute | solution.py:373
  124.6 0.9 add_convert_fusion.4
  (78 shorter events, 3.1 us)
Async XLA Ops:
  0.6 29.4 %copy-start.7 = (s32[4]{0:T(128)S(1)}, s32[4]{0:T(128)}, u32[]{:S(2)}) copy-start(s32[4]{0:T(128)} %lens_ref.7) | copy-start | bytes 52
  2.6 1.2 copy-start.4
  3.8 0.9 copy-start.5
  4.7 0.7 copy-start.8
  5.6 11.6 %collective-permute-start = (bf16[64,8192]{1,0:T(8,128)(2,1)S(1)}, bf16[64,8192]{1,0:T(8,128)(2,1)S(1)}, u32[]{:S(2)}, u32[]{:S(2)}) collective-permute-start(bf16[64,8192]{1,0:T(8,128)(2,1)S(1)} %get-tuple-element.79.q_mine), channel_id=1, source_target_pairs={{0,1},{1,0},{2,3},{3,2},{4,5},{5,4},{6,7},{7,6},{8,9},{9,8},{10,11... | collective-permute-start | bytes 3145736 | tf_op jit(solution)/shard_map/ppermute | solution.py:385
  6.1 9.0 %collective-permute-start.4 = (bf16[32,4224]{1,0:T(8,128)(2,1)}, bf16[32,4224]{1,0:T(8,128)(2,1)S(1)}, u32[]{:S(2)}, u32[]{:S(2)}) collective-permute-start(bf16[32,4224]{1,0:T(8,128)(2,1)} %norm_message.1.refs_0_), channel_id=1, source_target_pairs={{0,2},{1,5},{2,0},{3,7},{4,6},{5,1},{6,4},{7,3},{8,10},{9,13},{10,... | collective-permute-start | bytes 811016 | tf_op jit(solution)/shard_map/ppermute | solution.py:373
  8.6 33.3 %slice-start = ((s8[6291456]{0:T(1024)(128)(4,1)}), s8[4194304]{0:T(1024)(128)(4,1)S(1)}, s32[]{:S(2)}) async-start(s8[6291456]{0:T(1024)(128)(4,1)} %bitcast.5), calls=%async_computation | async-start | bytes 8388608
  8.6 33.3 %copy-start = (bf16[1,4096,768]{2,1,0:T(8,128)(2,1)S(1)}, bf16[1,4096,768]{2,1,0:T(8,128)(2,1)}, u32[]{:S(2)}) copy-start(bf16[1,4096,768]{2,1,0:T(8,128)(2,1)} %param.22) | copy-start | bytes 18874372
  8.6 4.1 %collective-permute-start.1 = (bf16[64,1152]{1,0:T(8,128)(2,1)S(1)}, bf16[64,1152]{1,0:T(8,128)(2,1)S(1)}, u32[]{:S(2)}, u32[]{:S(2)}) collective-permute-start(bf16[64,1152]{1,0:T(8,128)(2,1)S(1)} %get-tuple-element.140.o_mine), channel_id=1, source_target_pairs={{0,1},{1,0},{2,3},{3,2},{4,5},{5,4},{6,7},{7,6},{8,9},{9,8},{10,11... | collective-permute-start | bytes 442376 | tf_op jit(solution)/shard_map/ppermute | solution.py:385
  8.8 8.4 %collective-permute-start.9 = (bf16[32,4224]{1,0:T(8,128)(2,1)}, bf16[32,4224]{1,0:T(8,128)(2,1)S(1)}, u32[]{:S(2)}, u32[]{:S(2)}) collective-permute-start(bf16[32,4224]{1,0:T(8,128)(2,1)} %norm_message.1.refs_0_), channel_id=1, source_target_pairs={{0,4},{1,3},{2,6},{3,1},{4,0},{5,7},{6,2},{7,5},{8,12},{9,11},{10,... | collective-permute-start | bytes 811016 | tf_op jit(solution)/shard_map/ppermute | solution.py:373
  10.1 15.3 %collective-permute-start.2 = (bf16[32,4224]{1,0:T(8,128)(2,1)}, bf16[32,4224]{1,0:T(8,128)(2,1)S(1)}, u32[]{:S(2)}, u32[]{:S(2)}) collective-permute-start(bf16[32,4224]{1,0:T(8,128)(2,1)} %norm_message.1.refs_0_), channel_id=1, source_target_pairs={{0,16},{1,17},{2,18},{3,19},{4,20},{5,21},{6,22},{7,23},{8,24},{9,... | collective-permute-start | bytes 811016 | tf_op jit(solution)/shard_map/ppermute | solution.py:373
  12.7 12.9 %collective-permute-start.3 = (bf16[32,4224]{1,0:T(8,128)(2,1)}, bf16[32,4224]{1,0:T(8,128)(2,1)S(1)}, u32[]{:S(2)}, u32[]{:S(2)}) collective-permute-start(bf16[32,4224]{1,0:T(8,128)(2,1)} %norm_message.1.refs_0_), channel_id=1, source_target_pairs={{0,8},{1,9},{2,10},{3,11},{4,12},{5,13},{6,14},{7,15},{8,0},{9,1},... | collective-permute-start | bytes 811016 | tf_op jit(solution)/shard_map/ppermute | solution.py:373
  15.1 10.6 %collective-permute-start.5 = (bf16[32,4224]{1,0:T(8,128)(2,1)S(1)}, bf16[32,4224]{1,0:T(8,128)(2,1)S(1)}, u32[]{:S(2)}, u32[]{:S(2)}) collective-permute-start(bf16[32,4224]{1,0:T(8,128)(2,1)S(1)} %collective-permute-done.4.refs_1_), channel_id=1, source_target_pairs={{0,4},{1,3},{2,6},{3,1},{4,0},{5,7},{6,2},{7,5},{8,12},{9,11},{10,... | collective-permute-start | bytes 811016 | tf_op jit(solution)/shard_map/ppermute | solution.py:373
  17.2 10.9 %collective-permute-start.12 = (bf16[32,4224]{1,0:T(8,128)(2,1)S(1)}, bf16[32,4224]{1,0:T(8,128)(2,1)S(1)}, u32[]{:S(2)}, u32[]{:S(2)}) collective-permute-start(bf16[32,4224]{1,0:T(8,128)(2,1)S(1)} %collective-permute-done.9.refs_2_), channel_id=1, source_target_pairs={{0,1},{1,0},{2,3},{3,2},{4,5},{5,4},{6,7},{7,6},{8,9},{9,8},{10,11... | collective-permute-start | bytes 811016 | tf_op jit(solution)/shard_map/ppermute | solution.py:385
  17.2 2.2 %copy-start.2 = (bf16[2,1024,1024]{2,1,0:T(8,128)(2,1)S(1)}, bf16[2,1024,1024]{2,1,0:T(8,128)(2,1)}, u32[]{:S(2)}) copy-start(bf16[2,1024,1024]{2,1,0:T(8,128)(2,1)} %cache.7) | copy-start | bytes 12582916
  19.4 0.7 copy-start.6
  23.9 18.0 %slice-start.1 = ((s8[6291456]{0:T(1024)(128)(4,1)}), s8[2097152]{0:T(1024)(128)(4,1)S(1)}, s32[]{:S(2)}) async-start(s8[6291456]{0:T(1024)(128)(4,1)} %bitcast.5), calls=%async_computation.1 | async-start | bytes 4194304
  25.6 3.0 %collective-permute-start.10 = (bf16[32,4224]{1,0:T(8,128)(2,1)}, bf16[32,4224]{1,0:T(8,128)(2,1)S(1)}, u32[]{:S(2)}, u32[]{:S(2)}) collective-permute-start(bf16[32,4224]{1,0:T(8,128)(2,1)} %norm_message.1.refs_0_), channel_id=1, source_target_pairs={{0,1},{1,0},{2,3},{3,2},{4,5},{5,4},{6,7},{7,6},{8,9},{9,8},{10,11... | collective-permute-start | bytes 811016 | tf_op jit(solution)/shard_map/ppermute | solution.py:385
  25.7 15.1 %collective-permute-start.7 = (bf16[64,4224]{1,0:T(8,128)(2,1)S(1)}, bf16[64,4224]{1,0:T(8,128)(2,1)S(1)}, u32[]{:S(2)}, u32[]{:S(2)}) collective-permute-start(bf16[64,4224]{1,0:T(8,128)(2,1)S(1)} %stack.1.refs_1_.refs_0_), channel_id=1, source_target_pairs={{0,2},{1,5},{2,0},{3,7},{4,6},{5,1},{6,4},{7,3},{8,10},{9,13},{10,... | collective-permute-start | bytes 1622024 | tf_op jit(solution)/shard_map/ppermute | solution.py:373
  27.0 13.8 %collective-permute-start.8 = (bf16[64,4224]{1,0:T(8,128)(2,1)S(1)}, bf16[64,4224]{1,0:T(8,128)(2,1)S(1)}, u32[]{:S(2)}, u32[]{:S(2)}) collective-permute-start(bf16[64,4224]{1,0:T(8,128)(2,1)S(1)} %stack.1.refs_1_.refs_0_), channel_id=1, source_target_pairs={{0,4},{1,3},{2,6},{3,1},{4,0},{5,7},{6,2},{7,5},{8,12},{9,11},{10,... | collective-permute-start | bytes 1622024 | tf_op jit(solution)/shard_map/ppermute | solution.py:373
  28.1 5.8 %collective-permute-start.11 = (bf16[32,4224]{1,0:T(8,128)(2,1)S(1)}, bf16[32,4224]{1,0:T(8,128)(2,1)S(1)}, u32[]{:S(2)}, u32[]{:S(2)}) collective-permute-start(bf16[32,4224]{1,0:T(8,128)(2,1)S(1)} %collective-permute-done.4.refs_1_), channel_id=1, source_target_pairs={{0,1},{1,0},{2,3},{3,2},{4,5},{5,4},{6,7},{7,6},{8,9},{9,8},{10,11... | collective-permute-start | bytes 811016 | tf_op jit(solution)/shard_map/ppermute | solution.py:385
  28.1 5.9 %collective-permute-start.13 = (bf16[32,4224]{1,0:T(8,128)(2,1)S(1)}, bf16[32,4224]{1,0:T(8,128)(2,1)S(1)}, u32[]{:S(2)}, u32[]{:S(2)}) collective-permute-start(bf16[32,4224]{1,0:T(8,128)(2,1)S(1)} %collective-permute-done.5.refs_3_), channel_id=1, source_target_pairs={{0,1},{1,0},{2,3},{3,2},{4,5},{5,4},{6,7},{7,6},{8,9},{9,8},{10,11... | collective-permute-start | bytes 811016 | tf_op jit(solution)/shard_map/ppermute | solution.py:385
  28.6 8.5 %collective-permute-start.6 = (bf16[32,4224]{1,0:T(8,128)(2,1)S(1)}, bf16[32,4224]{1,0:T(8,128)(2,1)S(1)}, u32[]{:S(2)}, u32[]{:S(2)}) collective-permute-start(bf16[32,4224]{1,0:T(8,128)(2,1)S(1)} %collective-permute-done.2.top), channel_id=1, source_target_pairs={{0,8},{1,9},{2,10},{3,11},{4,12},{5,13},{6,14},{7,15},{8,0},{9,1},... | collective-permute-start | bytes 811016 | tf_op jit(solution)/shard_map/ppermute | solution.py:373
  33.9 16.9 %collective-permute-start.17 = (bf16[64,4224]{1,0:T(8,128)(2,1)S(1)}, bf16[64,4224]{1,0:T(8,128)(2,1)S(1)}, u32[]{:S(2)}, u32[]{:S(2)}) collective-permute-start(bf16[64,4224]{1,0:T(8,128)(2,1)S(1)} %stack.1.refs_1_.refs_0_), channel_id=1, source_target_pairs={{0,1},{1,0},{2,3},{3,2},{4,5},{5,4},{6,7},{7,6},{8,9},{9,8},{10,11... | collective-permute-start | bytes 1622024 | tf_op jit(solution)/shard_map/ppermute | solution.py:385
  40.8 10.0 %collective-permute-start.16 = (bf16[64,4224]{1,0:T(8,128)(2,1)S(1)}, bf16[64,4224]{1,0:T(8,128)(2,1)S(1)}, u32[]{:S(2)}, u32[]{:S(2)}) collective-permute-start(bf16[64,4224]{1,0:T(8,128)(2,1)S(1)} %collective-permute-done.7.refs_12_.refs_1_), channel_id=1, source_target_pairs={{0,4},{1,3},{2,6},{3,1},{4,0},{5,7},{6,2},{7,5},{8,12},{9,11},{10,... | collective-permute-start | bytes 1622024 | tf_op jit(solution)/shard_map/ppermute | solution.py:373
  41.4 9.4 %collective-permute-start.18 = (bf16[64,4224]{1,0:T(8,128)(2,1)S(1)}, bf16[64,4224]{1,0:T(8,128)(2,1)S(1)}, u32[]{:S(2)}, u32[]{:S(2)}) collective-permute-start(bf16[64,4224]{1,0:T(8,128)(2,1)S(1)} %collective-permute-done.7.refs_12_.refs_1_), channel_id=1, source_target_pairs={{0,1},{1,0},{2,3},{3,2},{4,5},{5,4},{6,7},{7,6},{8,9},{9,8},{10,11... | collective-permute-start | bytes 1622024 | tf_op jit(solution)/shard_map/ppermute | solution.py:385
  41.7 9.1 %collective-permute-start.19 = (bf16[64,4224]{1,0:T(8,128)(2,1)S(1)}, bf16[64,4224]{1,0:T(8,128)(2,1)S(1)}, u32[]{:S(2)}, u32[]{:S(2)}) collective-permute-start(bf16[64,4224]{1,0:T(8,128)(2,1)S(1)} %collective-permute-done.8.refs_2_), channel_id=1, source_target_pairs={{0,1},{1,0},{2,3},{3,2},{4,5},{5,4},{6,7},{7,6},{8,9},{9,8},{10,11... | collective-permute-start | bytes 1622024 | tf_op jit(solution)/shard_map/ppermute | solution.py:385
  41.9 2.8 %copy-start.1 = (bf16[1,768,4096]{2,1,0:T(8,128)(2,1)S(1)}, bf16[1,768,4096]{2,1,0:T(8,128)(2,1)}, u32[]{:S(2)}) copy-start(bf16[1,768,4096]{2,1,0:T(8,128)(2,1)} %param.23) | copy-start | bytes 18874372
  50.8 19.6 %slice-start.2 = ((s8[6291456]{0:T(1024)(128)(4,1)}), s8[4194304]{0:T(1024)(128)(4,1)S(1)}, s32[]{:S(2)}) async-start(s8[6291456]{0:T(1024)(128)(4,1)} %bitcast.17), calls=%async_computation.2 | async-start | bytes 8388608
  50.8 12.9 %copy-start.3 = (bf16[2,1024,1024]{2,1,0:T(8,128)(2,1)S(1)}, bf16[2,1024,1024]{2,1,0:T(8,128)(2,1)}, u32[]{:S(2)}) copy-start(bf16[2,1024,1024]{2,1,0:T(8,128)(2,1)} %cache.7) | copy-start | bytes 12582916
  50.8 19.6 %slice-start.3 = ((s8[6291456]{0:T(1024)(128)(4,1)}), s8[2097152]{0:T(1024)(128)(4,1)S(1)}, s32[]{:S(2)}) async-start(s8[6291456]{0:T(1024)(128)(4,1)} %bitcast.17), calls=%async_computation.3 | async-start | bytes 4194304
  50.8 9.7 %collective-permute-start.20 = (bf16[128,4096]{1,0:T(8,128)(2,1)S(1)}, bf16[128,4096]{1,0:T(8,128)(2,1)S(1)}, u32[]{:S(2)}, u32[]{:S(2)}) collective-permute-start(bf16[128,4096]{1,0:T(8,128)(2,1)S(1)} %get-tuple-element.101), channel_id=1, source_target_pairs={{0,1},{1,0},{2,3},{3,2},{4,5},{5,4},{6,7},{7,6},{8,9},{9,8},{10,11... | collective-permute-start | bytes 3145736 | tf_op jit(solution)/shard_map/ppermute | solution.py:385
  51.2 3.1 %collective-permute-start.21 = (bf16[64,4224]{1,0:T(8,128)(2,1)S(1)}, bf16[64,4224]{1,0:T(8,128)(2,1)S(1)}, u32[]{:S(2)}, u32[]{:S(2)}) collective-permute-start(bf16[64,4224]{1,0:T(8,128)(2,1)S(1)} %collective-permute-done.16.refs_3_), channel_id=1, source_target_pairs={{0,1},{1,0},{2,3},{3,2},{4,5},{5,4},{6,7},{7,6},{8,9},{9,8},{10,11... | collective-permute-start | bytes 1622024 | tf_op jit(solution)/shard_map/ppermute | solution.py:385
  51.4 9.1 %collective-permute-start.14 = (bf16[32,4224]{1,0:T(8,128)(2,1)S(1)}, bf16[32,4224]{1,0:T(8,128)(2,1)S(1)}, u32[]{:S(2)}, u32[]{:S(2)}) collective-permute-start(bf16[32,4224]{1,0:T(8,128)(2,1)S(1)} %collective-permute-done.6.refs_0_), channel_id=1, source_target_pairs={{0,2},{1,5},{2,0},{3,7},{4,6},{5,1},{6,4},{7,3},{8,10},{9,13},{10,... | collective-permute-start | bytes 811016 | tf_op jit(solution)/shard_map/ppermute | solution.py:373
  53.0 7.5 %collective-permute-start.15 = (bf16[32,4224]{1,0:T(8,128)(2,1)S(1)}, bf16[32,4224]{1,0:T(8,128)(2,1)S(1)}, u32[]{:S(2)}, u32[]{:S(2)}) collective-permute-start(bf16[32,4224]{1,0:T(8,128)(2,1)S(1)} %collective-permute-done.6.refs_0_), channel_id=1, source_target_pairs={{0,4},{1,3},{2,6},{3,1},{4,0},{5,7},{6,2},{7,5},{8,12},{9,11},{10,... | collective-permute-start | bytes 811016 | tf_op jit(solution)/shard_map/ppermute | solution.py:373
  53.9 6.6 %collective-permute-start.22 = (bf16[32,4224]{1,0:T(8,128)(2,1)S(1)}, bf16[32,4224]{1,0:T(8,128)(2,1)S(1)}, u32[]{:S(2)}, u32[]{:S(2)}) collective-permute-start(bf16[32,4224]{1,0:T(8,128)(2,1)S(1)} %collective-permute-done.6.refs_0_), channel_id=1, source_target_pairs={{0,1},{1,0},{2,3},{3,2},{4,5},{5,4},{6,7},{7,6},{8,9},{9,8},{10,11... | collective-permute-start | bytes 811016 | tf_op jit(solution)/shard_map/ppermute | solution.py:385
  60.5 7.1 %collective-permute-start.24 = (bf16[128,4096]{1,0:T(8,128)(2,1)S(1)}, bf16[128,4096]{1,0:T(8,128)(2,1)S(1)}, u32[]{:S(2)}, u32[]{:S(2)}) collective-permute-start(bf16[128,4096]{1,0:T(8,128)(2,1)S(1)} %get-tuple-element.115), channel_id=1, source_target_pairs={{0,1},{1,0},{2,3},{3,2},{4,5},{5,4},{6,7},{7,6},{8,9},{9,8},{10,11... | collective-permute-start | bytes 3145736 | tf_op jit(solution)/shard_map/ppermute | solution.py:385
  60.6 6.9 %collective-permute-start.23 = (bf16[32,4224]{1,0:T(8,128)(2,1)S(1)}, bf16[32,4224]{1,0:T(8,128)(2,1)S(1)}, u32[]{:S(2)}, u32[]{:S(2)}) collective-permute-start(bf16[32,4224]{1,0:T(8,128)(2,1)S(1)} %collective-permute-done.14.refs_0_.refs_1_), channel_id=1, source_target_pairs={{0,4},{1,3},{2,6},{3,1},{4,0},{5,7},{6,2},{7,5},{8,12},{9,11},{10,... | collective-permute-start | bytes 811016 | tf_op jit(solution)/shard_map/ppermute | solution.py:373
  62.0 5.5 %collective-permute-start.25 = (bf16[32,4224]{1,0:T(8,128)(2,1)S(1)}, bf16[32,4224]{1,0:T(8,128)(2,1)S(1)}, u32[]{:S(2)}, u32[]{:S(2)}) collective-permute-start(bf16[32,4224]{1,0:T(8,128)(2,1)S(1)} %collective-permute-done.14.refs_0_.refs_1_), channel_id=1, source_target_pairs={{0,1},{1,0},{2,3},{3,2},{4,5},{5,4},{6,7},{7,6},{8,9},{9,8},{10,11... | collective-permute-start | bytes 811016 | tf_op jit(solution)/shard_map/ppermute | solution.py:385
  62.4 5.2 %collective-permute-start.26 = (bf16[32,4224]{1,0:T(8,128)(2,1)S(1)}, bf16[32,4224]{1,0:T(8,128)(2,1)S(1)}, u32[]{:S(2)}, u32[]{:S(2)}) collective-permute-start(bf16[32,4224]{1,0:T(8,128)(2,1)S(1)} %collective-permute-done.15.refs_1_.refs_2_), channel_id=1, source_target_pairs={{0,1},{1,0},{2,3},{3,2},{4,5},{5,4},{6,7},{7,6},{8,9},{9,8},{10,11... | collective-permute-start | bytes 811016 | tf_op jit(solution)/shard_map/ppermute | solution.py:385
  62.7 13.3 %collective-permute-start.27 = (bf16[64,4096]{1,0:T(8,128)(2,1)S(1)}, bf16[64,4096]{1,0:T(8,128)(2,1)S(1)}, u32[]{:S(2)}, u32[]{:S(2)}) collective-permute-start(bf16[64,4096]{1,0:T(8,128)(2,1)S(1)} %add_convert_fusion.3.refs_2_), channel_id=1, source_target_pairs={{0,4},{1,3},{2,6},{3,1},{4,0},{5,7},{6,2},{7,5},{8,12},{9,11},{10,... | collective-permute-start | bytes 1572872 | tf_op jit(solution)/shard_map/ppermute | solution.py:373
  67.7 10.6 %collective-permute-start.28 = (bf16[64,4096]{1,0:T(8,128)(2,1)S(1)}, bf16[64,4096]{1,0:T(8,128)(2,1)S(1)}, u32[]{:S(2)}, u32[]{:S(2)}) collective-permute-start(bf16[64,4096]{1,0:T(8,128)(2,1)S(1)} %add_convert_fusion.2.refs_11_), channel_id=1, source_target_pairs={{0,4},{1,3},{2,6},{3,1},{4,0},{5,7},{6,2},{7,5},{8,12},{9,11},{10,... | collective-permute-start | bytes 1572872 | tf_op jit(solution)/shard_map/ppermute | solution.py:373
  68.8 1.5 %collective-permute-start.29 = (bf16[32,4224]{1,0:T(8,128)(2,1)S(1)}, bf16[32,4224]{1,0:T(8,128)(2,1)S(1)}, u32[]{:S(2)}, u32[]{:S(2)}) collective-permute-start(bf16[32,4224]{1,0:T(8,128)(2,1)S(1)} %collective-permute-done.23.refs_3_), channel_id=1, source_target_pairs={{0,1},{1,0},{2,3},{3,2},{4,5},{5,4},{6,7},{7,6},{8,9},{9,8},{10,11... | collective-permute-start | bytes 811016 | tf_op jit(solution)/shard_map/ppermute | solution.py:385
  78.4 2.7 %collective-permute-start.30 = (bf16[128,4096]{1,0:T(8,128)(2,1)S(1)}, bf16[128,4096]{1,0:T(8,128)(2,1)S(1)}, u32[]{:S(2)}, u32[]{:S(2)}) collective-permute-start(bf16[128,4096]{1,0:T(8,128)(2,1)S(1)} %get-tuple-element.127), channel_id=1, source_target_pairs={{0,1},{1,0},{2,3},{3,2},{4,5},{5,4},{6,7},{7,6},{8,9},{9,8},{10,11... | collective-permute-start | bytes 3145736 | tf_op jit(solution)/shard_map/ppermute | solution.py:385
  78.4 11.1 %collective-permute-start.33 = (bf16[32,4096]{1,0:T(8,128)(2,1)S(1)}, bf16[32,4096]{1,0:T(8,128)(2,1)S(1)}, u32[]{:S(2)}, u32[]{:S(2)}) collective-permute-start(bf16[32,4096]{1,0:T(8,128)(2,1)S(1)} %attend.4.refs_0_), channel_id=1, source_target_pairs={{0,1},{1,0},{2,3},{3,2},{4,5},{5,4},{6,7},{7,6},{8,9},{9,8},{10,11... | collective-permute-start | bytes 786440 | tf_op jit(solution)/shard_map/ppermute | solution.py:385
  78.9 10.6 %collective-permute-start.34 = (bf16[32,4096]{1,0:T(8,128)(2,1)S(1)}, bf16[32,4096]{1,0:T(8,128)(2,1)S(1)}, u32[]{:S(2)}, u32[]{:S(2)}) collective-permute-start(bf16[32,4096]{1,0:T(8,128)(2,1)S(1)} %attend.5.refs_11_.refs_4_), channel_id=1, source_target_pairs={{0,1},{1,0},{2,3},{3,2},{4,5},{5,4},{6,7},{7,6},{8,9},{9,8},{10,11... | collective-permute-start | bytes 786440 | tf_op jit(solution)/shard_map/ppermute | solution.py:385
  78.9 10.6 %collective-permute-start.35 = (bf16[32,4096]{1,0:T(8,128)(2,1)S(1)}, bf16[32,4096]{1,0:T(8,128)(2,1)S(1)}, u32[]{:S(2)}, u32[]{:S(2)}) collective-permute-start(bf16[32,4096]{1,0:T(8,128)(2,1)S(1)} %attend.6.refs_1_), channel_id=1, source_target_pairs={{0,1},{1,0},{2,3},{3,2},{4,5},{5,4},{6,7},{7,6},{8,9},{9,8},{10,11... | collective-permute-start | bytes 786440 | tf_op jit(solution)/shard_map/ppermute | solution.py:385
  81.2 12.1 %collective-permute-start.31 = (bf16[64,4096]{1,0:T(8,128)(2,1)S(1)}, bf16[64,4096]{1,0:T(8,128)(2,1)S(1)}, u32[]{:S(2)}, u32[]{:S(2)}) collective-permute-start(bf16[64,4096]{1,0:T(8,128)(2,1)S(1)} %add_convert_fusion.1.refs_11_), channel_id=1, source_target_pairs={{0,4},{1,3},{2,6},{3,1},{4,0},{5,7},{6,2},{7,5},{8,12},{9,11},{10,... | collective-permute-start | bytes 1572872 | tf_op jit(solution)/shard_map/ppermute | solution.py:373
  82.7 9.3 %collective-permute-start.32 = (bf16[32,4096]{1,0:T(8,128)(2,1)S(1)}, bf16[32,4096]{1,0:T(8,128)(2,1)S(1)}, u32[]{:S(2)}, u32[]{:S(2)}) collective-permute-start(bf16[32,4096]{1,0:T(8,128)(2,1)S(1)} %add_convert_fusion.11.refs_12_), channel_id=1, source_target_pairs={{0,2},{1,5},{2,0},{3,7},{4,6},{5,1},{6,4},{7,3},{8,10},{9,13},{10,... | collective-permute-start | bytes 786440 | tf_op jit(solution)/shard_map/ppermute | solution.py:373
  93.2 2.7 %collective-permute-start.37 = (bf16[128,4096]{1,0:T(8,128)(2,1)S(1)}, bf16[128,4096]{1,0:T(8,128)(2,1)S(1)}, u32[]{:S(2)}, u32[]{:S(2)}) collective-permute-start(bf16[128,4096]{1,0:T(8,128)(2,1)S(1)} %get-tuple-element.135), channel_id=1, source_target_pairs={{0,1},{1,0},{2,3},{3,2},{4,5},{5,4},{6,7},{7,6},{8,9},{9,8},{10,11... | collective-permute-start | bytes 3145736 | tf_op jit(solution)/shard_map/ppermute | solution.py:385
  96.0 12.0 %collective-permute-start.39 = (bf16[64,4096]{1,0:T(8,128)(2,1)S(1)}, bf16[64,4096]{1,0:T(8,128)(2,1)S(1)}, u32[]{:S(2)}, u32[]{:S(2)}) collective-permute-start(bf16[64,4096]{1,0:T(8,128)(2,1)S(1)} %add_convert_fusion.refs_0_), channel_id=1, source_target_pairs={{0,4},{1,3},{2,6},{3,1},{4,0},{5,7},{6,2},{7,5},{8,12},{9,11},{10,... | collective-permute-start | bytes 1572872 | tf_op jit(solution)/shard_map/ppermute | solution.py:373
  97.4 9.2 %collective-permute-start.38 = (bf16[32,4096]{1,0:T(8,128)(2,1)S(1)}, bf16[32,4096]{1,0:T(8,128)(2,1)S(1)}, u32[]{:S(2)}, u32[]{:S(2)}) collective-permute-start(bf16[32,4096]{1,0:T(8,128)(2,1)S(1)} %add_convert_fusion.9), channel_id=1, source_target_pairs={{0,2},{1,5},{2,0},{3,7},{4,6},{5,1},{6,4},{7,3},{8,10},{9,13},{10,... | collective-permute-start | bytes 786440 | tf_op jit(solution)/shard_map/ppermute | solution.py:373
  98.6 19.9 %collective-permute-start.36 = (bf16[32,4096]{1,0:T(8,128)(2,1)S(1)}, bf16[32,4096]{1,0:T(8,128)(2,1)S(1)}, u32[]{:S(2)}, u32[]{:S(2)}) collective-permute-start(bf16[32,4096]{1,0:T(8,128)(2,1)S(1)} %add_convert_fusion.10), channel_id=1, source_target_pairs={{0,16},{1,17},{2,18},{3,19},{4,20},{5,21},{6,22},{7,23},{8,24},{9,... | collective-permute-start | bytes 786440 | tf_op jit(solution)/shard_map/ppermute | solution.py:373
  108.1 6.4 %collective-permute-start.42 = (bf16[32,4096]{1,0:T(8,128)(2,1)S(1)}, bf16[32,4096]{1,0:T(8,128)(2,1)S(1)}, u32[]{:S(2)}, u32[]{:S(2)}) collective-permute-start(bf16[32,4096]{1,0:T(8,128)(2,1)S(1)} %add_convert_fusion.7), channel_id=1, source_target_pairs={{0,2},{1,5},{2,0},{3,7},{4,6},{5,1},{6,4},{7,3},{8,10},{9,13},{10,... | collective-permute-start | bytes 786440 | tf_op jit(solution)/shard_map/ppermute | solution.py:373
  109.3 10.6 %collective-permute-start.40 = (bf16[32,4096]{1,0:T(8,128)(2,1)S(1)}, bf16[32,4096]{1,0:T(8,128)(2,1)S(1)}, u32[]{:S(2)}, u32[]{:S(2)}) collective-permute-start(bf16[32,4096]{1,0:T(8,128)(2,1)S(1)} %add_convert_fusion.8), channel_id=1, source_target_pairs={{0,24},{1,25},{2,26},{3,27},{4,28},{5,29},{6,30},{7,31},{8,16},{9,... | collective-permute-start | bytes 786440 | tf_op jit(solution)/shard_map/ppermute | solution.py:373
  113.1 6.8 %collective-permute-start.41 = (bf16[32,4096]{1,0:T(8,128)(2,1)S(1)}, bf16[32,4096]{1,0:T(8,128)(2,1)S(1)}, u32[]{:S(2)}, u32[]{:S(2)}) collective-permute-start(bf16[32,4096]{1,0:T(8,128)(2,1)S(1)} %attend.7.refs_5_), channel_id=1, source_target_pairs={{0,1},{1,0},{2,3},{3,2},{4,5},{5,4},{6,7},{7,6},{8,9},{9,8},{10,11... | collective-permute-start | bytes 786440 | tf_op jit(solution)/shard_map/ppermute | solution.py:385
  114.7 9.9 %collective-permute-start.43 = (bf16[32,4096]{1,0:T(8,128)(2,1)S(1)}, bf16[32,4096]{1,0:T(8,128)(2,1)S(1)}, u32[]{:S(2)}, u32[]{:S(2)}) collective-permute-start(bf16[32,4096]{1,0:T(8,128)(2,1)S(1)} %add_convert_fusion.6), channel_id=1, source_target_pairs={{0,8},{1,9},{2,10},{3,11},{4,12},{5,13},{6,14},{7,15},{8,0},{9,1},... | collective-permute-start | bytes 786440 | tf_op jit(solution)/shard_map/ppermute | solution.py:373
  116.4 8.2 %collective-permute-start.44 = (bf16[32,4096]{1,0:T(8,128)(2,1)S(1)}, bf16[32,4096]{1,0:T(8,128)(2,1)S(1)}, u32[]{:S(2)}, u32[]{:S(2)}) collective-permute-start(bf16[32,4096]{1,0:T(8,128)(2,1)S(1)} %add_convert_fusion.5), channel_id=1, source_target_pairs={{0,2},{1,5},{2,0},{3,7},{4,6},{5,1},{6,4},{7,3},{8,10},{9,13},{10,... | collective-permute-start | bytes 786440 | tf_op jit(solution)/shard_map/ppermute | solution.py:373
